TPU v7x, 32 devices: a whole 2x2x4 slice. The times are simulated.
32 devices in a mesh: seq: 2 (over x), tensor: 16 (over z, y, core).
Axes of the slice: x: 2, y: 2, z: 4, core: 2. Of those that a mesh axis runs over, the one named last changes fastest.
Arguments:
- tokens: bfloat16 [768, 8192], P('tensor', 'seq'), may hold values from -6 to 6
- w_gate: bfloat16 [8192, 28672], P('seq', 'tensor'), may hold values from -0.109375 to 0.109375
- w_up: bfloat16 [8192, 28672], P('seq', 'tensor'), may hold values from -0.109375 to 0.109375
- w_down: bfloat16 [28672, 8192], P('tensor', 'seq'), may hold values from -0.0546875 to 0.0546875
- mask_gate: int32 [64, 224], P('seq', 'tensor'), may hold values 0 or 1
- mask_up: int32 [64, 224], P('seq', 'tensor'), may hold values 0 or 1
- mask_down: int32 [224, 64], P('tensor', 'seq'), may hold values 0 or 1
- cotangent: bfloat16 [768, 8192], P('tensor', 'seq'), may hold values from -6 to 6
Outputs:
- output: bfloat16 [768, 8192], P('tensor', 'seq')
- grad_tokens: bfloat16 [768, 8192], P('tensor', 'seq')
- grad_gate: bfloat16 [8192, 28672], P('seq', 'tensor')
- grad_up: bfloat16 [8192, 28672], P('seq', 'tensor')
- grad_down: bfloat16 [28672, 8192], P('tensor', 'seq')
All inputs are finite; a program needn't handle non-finite values. No bound on the sum of `mask_gate` or of `mask_up` or of `mask_down` on one device may be relied on, other than what follows from the above.
Results may differ from a plain program's by a relative error of at most 0.0049.
Values may be sent and summed in bfloat16 or wider, within the bound.
No kernel may reach another device: no remote copies, remote signals or barrier semaphores. Data moves between devices by JAX's collectives and lax.ppermute only.
A program may use at most 320 MiB of HBM per device.

v0:
```python
import jax
import jax.numpy as jnp
from jax import lax
from jax.sharding import PartitionSpec as P


def widen(mask, rows):
    block = rows // mask.shape[0]
    full = jnp.repeat(jnp.repeat(mask, block, axis=0), block, axis=1)
    return full.astype(jnp.bfloat16)


def gating(summed, width):
    gate = summed[:, :width]
    up = summed[:, width:]
    sig = jax.nn.sigmoid(gate)
    act = gate * sig
    return (gate, up, sig, act)


def gate_up_grads(gate, up, sig, act, grad_hidden):
    dgate = (grad_hidden * up * sig * (1.0 + gate * (1.0 - sig))).astype(jnp.bfloat16)
    dup = (grad_hidden * act).astype(jnp.bfloat16)
    return jnp.concatenate([dgate, dup], axis=1)


def per_device(tokens, w_gate, w_up, w_down, mask_gate, mask_up, mask_down, cotangent):
    width = w_gate.shape[1]
    gate_mask = widen(mask_gate, w_gate.shape[0])
    up_mask = widen(mask_up, w_up.shape[0])
    down_mask = widen(mask_down, w_down.shape[0])
    joined = jnp.concatenate([w_gate * gate_mask, w_up * up_mask], axis=1)
    down_w = w_down * down_mask
    contract_first = (((0,), (0,)), ((), ()))
    contract_last = (((1,), (1,)), ((), ()))
    gathered = lax.all_gather(tokens, "tensor", axis=0, tiled=True)
    partial_value = jnp.dot(gathered, joined, preferred_element_type=jnp.float32)
    summed = lax.psum(partial_value, "seq")
    gate, up, sig, act = gating(summed, width)
    hidden = (act * up).astype(jnp.bfloat16)
    rows_here = hidden
    output = lax.psum_scatter(
        jnp.dot(rows_here, down_w, preferred_element_type=jnp.float32),
        "tensor",
        scatter_dimension=0,
        tiled=True,
    ).astype(jnp.bfloat16)
    cot_rows = lax.all_gather(cotangent, "tensor", axis=0, tiled=True)
    grad_part = lax.dot_general(cot_rows, down_w, contract_last, preferred_element_type=jnp.float32)
    grad_hidden = lax.psum(grad_part, "seq")
    grads = gate_up_grads(gate, up, sig, act, grad_hidden)
    rows_here = grads
    grad_tokens = lax.psum_scatter(
        lax.dot_general(rows_here, joined, contract_last, preferred_element_type=jnp.float32),
        "tensor",
        scatter_dimension=0,
        tiled=True,
    ).astype(jnp.bfloat16)
    weight_grad = lax.dot_general(
        gathered, grads, contract_first, preferred_element_type=jnp.float32
    )
    grad_gate = (weight_grad[:, :width] * gate_mask).astype(jnp.bfloat16)
    grad_up = (weight_grad[:, width:] * up_mask).astype(jnp.bfloat16)
    down_grad = lax.dot_general(
        hidden, cot_rows, contract_first, preferred_element_type=jnp.float32
    )
    grad_down = (down_grad * down_mask).astype(jnp.bfloat16)
    return (output, grad_tokens, grad_gate, grad_up, grad_down)


def solution(mesh):
    return jax.shard_map(
        per_device,
        mesh=mesh,
        in_specs=(
            P("tensor", "seq"),
            P("seq", "tensor"),
            P("seq", "tensor"),
            P("tensor", "seq"),
            P("seq", "tensor"),
            P("seq", "tensor"),
            P("tensor", "seq"),
            P("tensor", "seq"),
        ),
        out_specs=(
            P("tensor", "seq"),
            P("tensor", "seq"),
            P("seq", "tensor"),
            P("seq", "tensor"),
            P("tensor", "seq"),
        ),
        check_vma=False,
    )
```

profile of v0, /device:TPU:0, one launch (start us, length us, event | category | flops | bytes accessed | tf_op | source)
XLA Modules:
  0.0 866.6 jit_solution(164712756107958285)
XLA Ops:
  7.2 0.7 all-gather.5.cloned.1.call-update
  7.9 0.7 all-gather.3.cloned.1.call-update
  8.7 0.7 convert_element_type.66
  9.4 0.7 convert_element_type.69
  10.1 0.7 convert_element_type.73
  10.8 0.1 broadcast_bitcast_fusion
  10.9 0.1 copy.18
  11.0 0.1 broadcast_bitcast_fusion.1
  11.2 0.1 copy.17
  11.2 20.2 %copy.13 = bf16[4096,1792]{0,1:T(8,128)(2,1)} copy(bf16[4096,1792]{1,0:T(8,128)(2,1)} %param.9) | data formatting | bytes 29360128 | tf_op args[1]
  31.4 19.6 %copy.14 = bf16[4096,1792]{0,1:T(8,128)(2,1)} copy(bf16[4096,1792]{1,0:T(8,128)(2,1)} %param.10) | data formatting | bytes 29360128 | tf_op args[2]
  51.0 21.4 %bitcast_multiply_fusion = (bf16[4096,1792]{0,1:T(8,128)(2,1)}, bf16[4096,1792]{0,1:T(8,128)(2,1)}) fusion(bf16[4096,1792]{0,1:T(8,128)(2,1)} %copy.14, bf16[4096,14]{0,1:T(8,128)(2,1)S(1)} %bitcast.43, bf16[4096,1792]{0,1:T(8,128)(2,1)} %copy.13, bf16[4096,14]{0,1:T(8,128)(2,1)S(1)} %bitcast.45), kind=kLoop, calls=%fused_computation.7 | loop fusion | flops 14680064 | bytes 58949632 | tf_op jit(solution)/shard_map/mul | solution.py:32
  72.4 2.4 all-gather.5.cloned.1.call-done
  74.9 0.1 broadcast_in_dim.22
  74.9 9.9 %broadcast_in_dim.23 = bf16[1792,32,128]{2,1,0:T(8,128)(2,1)} broadcast(bf16[1792,32]{1,0:T(8,128)(2,1)S(1)} %bitcast.42), dimensions={0,1} | broadcast | bytes 14794752 | tf_op jit(solution)/shard_map/broadcast_in_dim | solution.py:9
  84.8 24.1 %fusion.8 = f32[768,1792]{0,1:T(8,128)} fusion(bf16[768,4096]{1,0:T(8,128)(2,1)} %all-gather.5.cloned.1.call-done, bf16[1792,4096]{1,0:T(8,128)(2,1)} %param.11, bf16[224,8,32,128]{3,2,1,0:T(8,128)(2,1)} %bitcast.39), kind=kOutput, calls=%fused_computation.21 | convolution fusion | flops 11281629184 | bytes 41156608 | tf_op jit(solution)/shard_map/dot_general | solution.py:49
  108.9 28.7 %all-gather.3.cloned.1.call-done = bf16[768,4096]{1,0:T(8,128)(2,1)} async-done(((bf16[48,4096]{1,0:T(8,128)(2,1)}), bf16[768,4096]{1,0:T(8,128)(2,1)}) %all-gather.3.cloned.1.call-update) | async-done | bytes 6291472 | tf_op jit(solution)/shard_map/all_gather | solution.py:36
  137.6 34.5 %fusion.4 = f32[768,3584]{0,1:T(8,128)} fusion(bf16[768,4096]{1,0:T(8,128)(2,1)} %all-gather.3.cloned.1.call-done, bf16[4096,1792]{0,1:T(8,128)(2,1)} %get-tuple-element.17, bf16[4096,1792]{0,1:T(8,128)(2,1)} %get-tuple-element.18), kind=kOutput, calls=%fused_computation.12 | convolution fusion | flops 22607298560 | bytes 46661632 | tf_op jit(solution)/shard_map/dot_general | solution.py:37
  172.1 0.0 reduce-scatter.5.cloned.1.call-start
  172.2 371.9 %all-reduce.3.cloned.1.call-done = (f32[768,3584]{0,1:T(8,128)}, f32[768,1792]{0,1:T(8,128)}) async-done(((f32[768,3584]{0,1:T(8,128)}, f32[768,1792]{0,1:T(8,128)}), (f32[768,3584]{0,1:T(8,128)}, f32[768,1792]{0,1:T(8,128)})) %all-reduce.3.cloned.1.call-update) | async-done | bytes 16515088 | tf_op jit(solution)/shard_map/psum | solution.py:38
  544.1 8.4 multiply_convert_fusion.2
  552.5 1.6 copy-done
  554.1 29.8 %fusion.2 = f32[768,4096]{1,0:T(8,128)} fusion(bf16[4096,1792]{0,1:T(8,128)(2,1)} %get-tuple-element.17, bf16[4096,1792]{0,1:T(8,128)(2,1)} %get-tuple-element.18, bf16[768,1792]{0,1:T(8,128)(2,1)} %get-tuple-element.15, bf16[768,1792]{0,1:T(8,128)(2,1)S(1)} %get-tuple-element.14), kind=kOutput, calls=%fused_computation.9 | convolution fusion | flops 22618308608 | bytes 47448064 | tf_op jit(solution)/shard_map/dot_general | solution.py:54
  584.0 20.5 %fusion.7 = f32[768,4096]{1,0:T(8,128)} fusion(bf16[768,1792]{0,1:T(8,128)(2,1)S(1)} %get-tuple-element.16, bf16[1792,4096]{1,0:T(8,128)(2,1)} %param.11, bf16[224,8,32,128]{3,2,1,0:T(8,128)(2,1)} %bitcast.40), kind=kOutput, calls=%fused_computation.20 | convolution fusion | flops 11281629184 | bytes 44695552 | tf_op jit(solution)/shard_map/dot_general | solution.py:43
  604.5 33.8 %convolution_bitcast_fusion = f32[4096,3584]{0,1:T(8,128)} fusion(bf16[768,4096]{1,0:T(8,128)(2,1)} %all-gather.3.cloned.1.call-done, bf16[768,1792]{0,1:T(8,128)(2,1)} %get-tuple-element.15, bf16[768,1792]{0,1:T(8,128)(2,1)} %copy-done), kind=kOutput, calls=%fused_computation | convolution fusion | flops 22559588352 | bytes 70516736 | tf_op jit(solution)/shard_map/dot_general | solution.py:59
  638.4 30.8 %fusion = (bf16[4096,1792]{0,1:T(8,128)(2,1)}, bf16[4096,1792]{0,1:T(8,128)(2,1)}) fusion(f32[4096,3584]{0,1:T(8,128)} %convolution_bitcast_fusion, bf16[4096,14]{0,1:T(8,128)(2,1)S(1)} %bitcast.44, bf16[4096,14]{0,1:T(8,128)(2,1)S(1)} %bitcast.46), kind=kLoop, calls=%fused_computation.2 | loop fusion | flops 44040192 | bytes 88309760 | tf_op jit(solution)/shard_map/convert_element_type | solution.py:63
  669.2 18.8 %copy.16 = bf16[4096,1792]{1,0:T(8,128)(2,1)} copy(bf16[4096,1792]{0,1:T(8,128)(2,1)} %get-tuple-element.12) | data formatting | bytes 29360128
  688.0 18.7 %copy.15 = bf16[4096,1792]{1,0:T(8,128)(2,1)} copy(bf16[4096,1792]{0,1:T(8,128)(2,1)} %get-tuple-element.13) | data formatting | bytes 29360128
  706.7 19.7 %multiply_convert_fusion = bf16[1792,4096]{1,0:T(8,128)(2,1)} fusion(bf16[768,1792]{0,1:T(8,128)(2,1)S(1)} %get-tuple-element.16, bf16[768,4096]{1,0:T(8,128)(2,1)} %all-gather.5.cloned.1.call-done, bf16[224,8,32,128]{3,2,1,0:T(8,128)(2,1)} %bitcast.41), kind=kOutput, calls=%fused_computation.6 | convolution fusion | flops 11296309248 | bytes 38404096 | tf_op jit(solution)/shard_map/dot_general | solution.py:64
  726.4 1.9 convert_element_type.79
  728.4 129.3 %reduce-scatter.3.cloned.1.call-done = f32[48,4096]{1,0:T(8,128)} async-done(((f32[768,4096]{1,0:T(8,128)}), f32[48,4096]{1,0:T(8,128)}) %reduce-scatter.3.cloned.1.call-update) | async-done | bytes 786448 | tf_op jit(solution)/shard_map/reduce_scatter | solution.py:42
  857.7 1.9 convert_element_type.76
  (19 shorter events, 0.3 us)
Async XLA Ops:
  7.2 67.7 %all-gather.5.cloned.1.call-start = ((), (), s32[]{:S(2)}) async-start(), calls=%async_computation.4 | async-start | bytes 6684672 | tf_op jit(solution)/shard_map/all_gather | solution.py:48
  7.9 129.7 %all-gather.3.cloned.1.call-start = ((), (), s32[]{:S(2)}) async-start(), calls=%async_computation.2 | async-start | bytes 6684672 | tf_op jit(solution)/shard_map/all_gather | solution.py:36
  8.6 535.5 %all-reduce.3.cloned.1.call-start = ((), (), s32[]{:S(2)}) async-start(), calls=%async_computation.6 | async-start | bytes 33030144 | tf_op jit(solution)/shard_map/psum | solution.py:38
  11.0 40.0 %copy-start.1 = (bf16[2,8,32,128]{3,1,2,0:T(8,128)(2,1)}, bf16[2,8,32,128]{3,1,2,0:T(8,128)(2,1)S(1)}, u32[]{:S(2)}) copy-start(bf16[2,8,32,128]{3,1,2,0:T(8,128)(2,1)S(1)} %copy.18) | copy-start | bytes 393220
  11.2 39.8 %copy-start.3 = (bf16[2,8,32,128]{3,1,2,0:T(8,128)(2,1)}, bf16[2,8,32,128]{3,1,2,0:T(8,128)(2,1)S(1)}, u32[]{:S(2)}) copy-start(bf16[2,8,32,128]{3,1,2,0:T(8,128)(2,1)S(1)} %copy.17) | copy-start | bytes 393220
  172.1 554.3 %reduce-scatter.5.cloned.1.call-start = ((), (), s32[]{:S(2)}) async-start(), calls=%async_computation.5 | async-start | bytes 13369344 | tf_op jit(solution)/shard_map/reduce_scatter | solution.py:53
  552.5 1.6 copy-start
  584.0 273.7 %reduce-scatter.3.cloned.1.call-start = ((), (), s32[]{:S(2)}) async-start(), calls=%async_computation.3 | async-start | bytes 13369344 | tf_op jit(solution)/shard_map/reduce_scatter | solution.py:42
  604.5 33.9 %copy-start.2 = (bf16[2,8,32,128]{3,1,2,0:T(8,128)(2,1)S(1)}, bf16[2,8,32,128]{3,1,2,0:T(8,128)(2,1)}, u32[]{:S(2)}) copy-start(bf16[2,8,32,128]{3,1,2,0:T(8,128)(2,1)} %copy-done.1) | copy-start | bytes 393220
  604.5 33.9 %copy-start.4 = (bf16[2,8,32,128]{3,1,2,0:T(8,128)(2,1)S(1)}, bf16[2,8,32,128]{3,1,2,0:T(8,128)(2,1)}, u32[]{:S(2)}) copy-start(bf16[2,8,32,128]{3,1,2,0:T(8,128)(2,1)} %copy-done.3) | copy-start | bytes 393220
Sparse Core Ops, SparseCore 0:
  10.3 64.5 all-gather.4
  77.1 60.4 all-gather.2
  172.2 371.8 all-reduce.2
  584.1 135.2 reduce-scatter.4
  723.9 133.7 reduce-scatter.2
where the time goes:
time: 875 us; the launch traced here: 867 us
  waiting for transfers between devices  534 us (61%)
  matrix products  162 us (19%)
  local copies, waits for them, and re-layouts  89.2 us (10%)
  other arithmetic  66.6 us (8%)
  between operations  14.3 us (2%)
    psum x1, waiting for transfers between devices, per_device(): summed = lax.psum(partial_value, 'seq')  372 us
    reduce_scatter x1, waiting for transfers between devices, per_device(): lax.psum_scatter(jnp.dot(rows_here, down_w, preferred_element_type=jnp.fl...  129 us
    unnamed x20, local copies, waits for them, and re-layouts  79.3 us
    dot_general x1, matrix products, per_device(): jnp.dot(gathered, joined, preferred_element_type=jnp.float32)  34.5 us
    dot_general x1, matrix products, per_device(): lax.dot_general(gathered, grads, contract_first, preferred_element_type=j...  33.8 us
    convert_element_type x1, other arithmetic, per_device(): grad_up = (weight_grad[:, width:] * up_mask).astype(jnp.bfloat16)  30.8 us
    dot_general x1, matrix products, per_device(): lax.dot_general(rows_here, joined, contract_last, preferred_element_type=...  29.8 us
    all_gather x1, waiting for transfers between devices, per_device(): gathered = lax.all_gather(tokens, 'tensor', axis=0, tiled=True)  28.7 us
  transfers between devices with their start and end apart: 5, of which 4 were waited for; matrix products, arithmetic and copies ran while one was open for 28% of the time, Pallas kernels for 0%

commit v1 on v0

v1 whole, which is shorter than its diff:
```python
import jax
import jax.numpy as jnp
from jax import lax
from jax.experimental import pallas as pl
from jax.experimental.pallas import tpu as pltpu
from jax.sharding import PartitionSpec as P

BF = jnp.bfloat16
F32 = jnp.float32
BLK = 128
VMEM_LIMIT = 60 * 1024 * 1024


def cost(flops, read, written):
    return pl.CostEstimate(flops=flops // 1, bytes_accessed=(read + written) // 1, transcendentals=0)


def params():
    return pltpu.CompilerParams(
        dimension_semantics=("arbitrary",), vmem_limit_bytes=VMEM_LIMIT
    )


def pick(size, largest):
    best = BLK
    for blocks in range(1, largest // BLK + 1):
        if size % (blocks * BLK) == 0:
            best = blocks * BLK
    return best


def masked_tile(w_ref, mask_ref, row, rows, col, cols, mask_row, mask_col):
    strips = []
    for i in range(rows // BLK):
        parts = []
        for j in range(cols // BLK):
            keep = mask_ref[mask_row + i, mask_col + j].astype(F32)
            part = w_ref[row + i * BLK : row + (i + 1) * BLK, col + j * BLK : col + (j + 1) * BLK]
            parts.append(part * jnp.full((BLK, BLK), keep, F32).astype(BF))
        strips.append(parts[0] if len(parts) == 1 else jnp.concatenate(parts, axis=1))
    return strips[0] if len(strips) == 1 else jnp.concatenate(strips, axis=0)


def store(core_ref, rows, outs, total):
    if outs[0].shape[0] == total.shape[0]:
        for out in outs:
            out[...] = total.astype(out.dtype)
        return
    each = [total[at : at + rows] for at in range(0, total.shape[0], rows)]
    even, odd = jnp.concatenate(each[0::2], axis=0), jnp.concatenate(each[1::2], axis=0)
    first = core_ref[0] == 0
    outs[0][...] = jnp.where(first, even, odd).astype(outs[0].dtype)
    outs[1][...] = jnp.where(first, odd, even).astype(outs[1].dtype)


def whole_block(x):
    return pl.BlockSpec(x.shape, lambda j: (0, 0))


SMEM = pl.BlockSpec(memory_space=pltpu.SMEM)
UNREAD = pl.BlockSpec(memory_space=pl.ANY)


def take_kernel(x_ref, *refs):
    refs[-1][...] = x_ref[...]


def take(x, c, rows, after):
    return pl.pallas_call(
        take_kernel,
        grid=(1,),
        in_specs=[pl.BlockSpec((rows, x.shape[1]), lambda j: (c, 0))] + [UNREAD] * len(after),
        out_specs=pl.BlockSpec((rows, x.shape[1]), lambda j: (0, 0)),
        out_shape=jax.ShapeDtypeStruct((rows, x.shape[1]), x.dtype),
        compiler_params=params(),
        name="take_rows",
    )(x, *after)


def nn_kernel(rows, mask_ref, core_ref, x_ref, w_ref, *refs):
    outs = refs[-2:]
    depth, width = w_ref.shape
    step = pick(depth, 512)
    first = pl.program_id(0) * (width // BLK)
    total = None
    for k in range(0, depth, step):
        w = masked_tile(w_ref, mask_ref, k, step, 0, width, k // BLK, first)
        part = jnp.dot(x_ref[:, k : k + step], w, preferred_element_type=F32)
        total = part if total is None else total + part
    store(core_ref, rows, outs, total)


def nn(core, each, x, w, mask, takes, tile, after):
    rows, (depth, width) = x.shape[0], w.shape
    tile = pick(width, tile)
    return pl.pallas_call(
        lambda *refs: nn_kernel(each, *refs),
        grid=(width // tile,),
        in_specs=[SMEM, SMEM, whole_block(x), pl.BlockSpec((depth, tile), lambda j: (0, j))]
        + [UNREAD] * len(after),
        out_specs=[pl.BlockSpec((r, tile), lambda j: (0, j)) for r, _ in takes],
        out_shape=[jax.ShapeDtypeStruct((r, width), t) for r, t in takes],
        compiler_params=params(),
        cost_estimate=cost(2 * rows * depth * width, 2 * (depth * width + rows * depth), 4 * rows * width),
        name="times_masked",
    )(mask, core, x, w, *after)


def nt_kernel(rows, terms, core_ref, *refs):
    total = None
    for n in range(terms):
        mask_ref, x_ref, w_ref = refs[3 * n : 3 * n + 3]
        height, depth = w_ref.shape
        first = pl.program_id(0) * (height // BLK)
        step = pick(depth, 512)
        for k in range(0, depth, step):
            w = masked_tile(w_ref, mask_ref, 0, height, k, step, first, k // BLK)
            part = lax.dot_general(
                x_ref[:, k : k + step], w, (((1,), (1,)), ((), ())), preferred_element_type=F32
            )
            total = part if total is None else total + part
    store(core_ref, rows, refs[-2:], total)


def nt(core, each, terms, takes, tile, after):
    rows = terms[0][0].shape[0]
    height, depth = terms[0][1].shape
    tile = pick(height, tile)
    specs, args = [SMEM], [core]
    for x, w, mask in terms:
        specs += [SMEM, whole_block(x), pl.BlockSpec((tile, depth), lambda j: (j, 0))]
        args += [mask, x, w]
    n = len(terms)
    return pl.pallas_call(
        lambda *refs: nt_kernel(each, n, *refs),
        grid=(height // tile,),
        in_specs=specs + [UNREAD] * len(after),
        out_specs=[pl.BlockSpec((r, tile), lambda j: (0, j)) for r, _ in takes],
        out_shape=[jax.ShapeDtypeStruct((r, height), t) for r, t in takes],
        compiler_params=params(),
        cost_estimate=cost(
            2 * n * rows * depth * height, 2 * n * (depth * height + rows * depth), 4 * rows * height
        ),
        name="times_masked_transposed",
    )(*args, *after)


def tn_kernel(chunks, mask_ref, *refs):
    xs, ds = refs[:chunks], refs[chunks : 2 * chunks]
    out, turned = refs[-chunks - 1], refs[-chunks:]
    height, width = out.shape
    first = pl.program_id(0) * (height // BLK)
    for x, t in zip(xs, turned):
        t[...] = x[...].T
    step = pick(width, 256)
    for n in range(0, width, step):
        total = None
        for t, d in zip(turned, ds):
            part = jnp.dot(t[...], d[:, n : n + step], preferred_element_type=F32)
            total = part if total is None else total + part
        for i in range(height // BLK):
            for j in range(step // BLK):
                keep = mask_ref[first + i, n // BLK + j].astype(F32)
                out[i * BLK : (i + 1) * BLK, n + j * BLK : n + (j + 1) * BLK] = (
                    total[i * BLK : (i + 1) * BLK, j * BLK : (j + 1) * BLK] * keep
                ).astype(BF)


def tn(xs, ds, mask, tile, after):
    chunks = len(xs)
    (rows, height), width = xs[0].shape, ds[0].shape[1]
    tile = pick(height, tile)
    return pl.pallas_call(
        lambda *refs: tn_kernel(chunks, *refs),
        grid=(height // tile,),
        in_specs=[SMEM]
        + [pl.BlockSpec((rows, tile), lambda i: (0, i)) for _ in xs]
        + [whole_block(d) for d in ds]
        + [UNREAD] * len(after),
        out_specs=pl.BlockSpec((tile, width), lambda i: (i, 0)),
        out_shape=jax.ShapeDtypeStruct((height, width), BF),
        scratch_shapes=[pltpu.VMEM((tile, rows), BF) for _ in xs],
        compiler_params=params(),
        cost_estimate=cost(
            2 * chunks * rows * height * width, 2 * chunks * rows * (height + width), 2 * height * width
        ),
        name="weight_grad",
    )(mask, *xs, *ds, *after)


def added(refs):
    total = refs[0][...]
    for ref in refs[1:]:
        total = total + ref[...].astype(F32)
    return total


def hidden_kernel(n, *refs):
    gate, up = added(refs[:n]), added(refs[n : 2 * n])
    refs[-1][...] = (gate * jax.nn.sigmoid(gate) * up).astype(BF)


def grads_kernel(n, *refs):
    gate, up, dh = added(refs[:n]), added(refs[n : 2 * n]), added(refs[2 * n : 3 * n])
    sig = jax.nn.sigmoid(gate)
    refs[-2][...] = (dh * up * sig * (1.0 + gate * (1.0 - sig))).astype(BF)
    refs[-1][...] = (dh * (gate * sig)).astype(BF)


def gating(kernel, sums, outs, after):
    rows, width = sums[0][0].shape
    tile = pick(width, 256)
    spec = pl.BlockSpec((rows, tile), lambda j: (0, j))
    flat = [part for parts in sums for part in parts]
    return pl.pallas_call(
        lambda *refs: kernel(len(sums[0]), *refs),
        grid=(width // tile,),
        in_specs=[spec] * len(flat) + [UNREAD] * len(after),
        out_specs=[spec] * outs,
        out_shape=[jax.ShapeDtypeStruct((rows, width), BF)] * outs,
        compiler_params=params(),
        cost_estimate=cost(20 * rows * width, 6 * len(sums) * rows * width, 2 * outs * rows * width),
        name="gating",
    )(*flat, *after)


def solution(mesh):
    size = mesh.shape["seq"]
    spread = mesh.shape["tensor"]
    chunks = 3

    def per_device(tokens, w_gate, w_up, w_down, mask_gate, mask_up, mask_down, cotangent):
        rows = tokens.shape[0] // chunks
        total = rows * spread
        cores = [(i, i ^ 1) for i in range(spread)]
        same_core = [list(range(core, spread, 2)) for core in range(2)]
        whole = ((total, F32), (total, BF))
        split = ((total // 2, F32), (total // 2, BF))
        core = jnp.reshape(lax.axis_index("tensor") % 2, (1,)).astype(jnp.int32)
        last = [mask_gate]

        def run(kernel, *args, late=()):
            out = kernel(*args, [last[0], *late])
            last[0] = out[0] if isinstance(out, (tuple, list)) else out
            return out

        def gather(x, c):
            return lax.all_gather(run(take, x, c, rows), "tensor", axis=0, tiled=True)

        def scatter(mine, others):
            both = mine + lax.ppermute(others, "tensor", cores).astype(F32)
            return lax.psum_scatter(
                both, "tensor", scatter_dimension=0, tiled=True, axis_index_groups=same_core
            ).astype(BF)

        arrived = []

        def exchange(own, sent):
            shifts = [[(i, (i + k) % size) for i in range(size)] for k in range(1, size)]
            parts = [lax.ppermute(sent, "seq", shift) for shift in shifts]
            arrived.append(parts)
            return [own] + parts

        def late():
            return arrived[-2] if len(arrived) > 1 else []

        toks, cots, gates, ups, dhs, hiddens, dgates, dups, outs, gtoks = ([] for _ in range(10))

        def gate_sums(c):
            gates.append(
                exchange(*run(nn, core, rows, toks[c], w_gate, mask_gate, whole, 256, late=late()))
            )

        def up_sums(c):
            ups.append(exchange(*run(nn, core, rows, toks[c], w_up, mask_up, whole, 256, late=late())))

        def dh_sums(c):
            terms = [(cots[c], w_down, mask_down)]
            dhs.append(exchange(*run(nt, core, rows, terms, whole, 256, late=late())))

        def back_out(c):
            (hidden,) = run(gating, hidden_kernel, [gates[c], ups[c]], 1)
            hiddens.append(hidden)
            outs.append(scatter(*run(nn, core, rows, hidden, w_down, mask_down, split, 512)))

        def back_tokens(c):
            dgate, dup = run(gating, grads_kernel, [gates[c], ups[c], dhs[c]], 2)
            dgates.append(dgate)
            dups.append(dup)
            terms = [(dgate, w_gate, mask_gate), (dup, w_up, mask_up)]
            gtoks.append(scatter(*run(nt, core, rows, terms, split, 512)))

        toks.append(gather(tokens, 0))
        cots.append(gather(cotangent, 0))
        gate_sums(0)
        toks.append(gather(tokens, 1))
        up_sums(0)
        cots.append(gather(cotangent, 1))
        dh_sums(0)
        toks.append(gather(tokens, 2))
        gate_sums(1)
        cots.append(gather(cotangent, 2))
        back_out(0)
        up_sums(1)
        back_tokens(0)
        dh_sums(1)
        gate_sums(2)
        back_out(1)
        up_sums(2)
        back_tokens(1)
        dh_sums(2)
        back_out(2)
        grad_down = run(tn, hiddens, cots, mask_down, 256)
        back_tokens(2)
        grad_gate = run(tn, toks, dgates, mask_gate, 512)
        grad_up = run(tn, toks, dups, mask_up, 512)
        output = jnp.concatenate(outs, axis=0)
        grad_tokens = jnp.concatenate(gtoks, axis=0)
        return (output, grad_tokens, grad_gate, grad_up, grad_down)

    return jax.shard_map(
        per_device,
        mesh=mesh,
        in_specs=(
            P("tensor", "seq"),
            P("seq", "tensor"),
            P("seq", "tensor"),
            P("tensor", "seq"),
            P("seq", "tensor"),
            P("seq", "tensor"),
            P("tensor", "seq"),
            P("tensor", "seq"),
        ),
        out_specs=(
            P("tensor", "seq"),
            P("tensor", "seq"),
            P("seq", "tensor"),
            P("seq", "tensor"),
            P("tensor", "seq"),
        ),
        check_vma=False,
    )
```

time: 875 us -> 702 us (0.80)
  Pallas kernels: 0 us -> 287 us
  waiting for transfers between devices: 534 us -> 343 us
  matrix products: 162 us -> 0 us
  local copies, waits for them, and re-layouts: 89.2 us -> 15.4 us
  other arithmetic: 66.6 us -> 26.7 us
  starting transfers between devices: 0.2 us -> 12.1 us
    psum x1 -> x0, waiting for transfers between devices: 372 us -> none  [per_device(): summed = lax.psum(partial_value, 'seq')]
    pallas_call x0 -> x30, Pallas kernels: none -> 287 us  [the longest x9 103 us: nn(): pl.pallas_call(lambda *refs: nn_kernel(each, *refs), grid=(width // tile,...]
    dot_general x6 -> x0, matrix products: 162 us -> none  [the longest x1 34.5 us: per_device(): jnp.dot(gathered, joined, preferred_element_type=jnp.float32)]
    ppermute x0 -> x15, waiting for transfers between devices: none -> 144 us  [the longest x9 127 us: exchange(): parts = [lax.ppermute(sent, 'seq', shift) for shift in shifts]]
    unnamed x20 -> x36, local copies, waits for them, and re-layouts: 79.3 us -> 15.4 us
    convert_element_type x7 -> x6, other arithmetic: 45.2 us -> 5.79 us  [scatter(): return lax.psum_scatter(both, 'tensor', scatter_dimension=0, tiled=True,...]
    all_gather x2 -> x6, waiting for transfers between devices: 31.2 us -> 58.2 us  [gather(): return lax.all_gather(run(take, x, c, rows), 'tensor', axis=0, tiled=True)]
    mul x1 -> x0, other arithmetic: 21.4 us -> none  [per_device(): joined = jnp.concatenate([w_gate * gate_mask, w_up * up_mask], axis=1)]
  transfers between devices with their start and end apart: 5 -> 27, of which waited for: 4 -> 21; matrix products, arithmetic and copies ran while one was open for 28% -> 4% of each run, Pallas kernels for 0% -> 41%
where the time goes in v1:
time: 702 us; the launch traced here: 698 us
  waiting for transfers between devices  343 us (49%)
  Pallas kernels  287 us (41%)
  other arithmetic  26.7 us (4%)
  local copies, waits for them, and re-layouts  15.4 us (2%)
  between operations  14.3 us (2%)
  starting transfers between devices  12.1 us (2%)
    reduce_scatter x6, waiting for transfers between devices, scatter(): lax.psum_scatter(both, 'tensor', scatter_dimension=0, tiled=True, axis_in...  140 us
    ppermute x9, waiting for transfers between devices, exchange(): parts = [lax.ppermute(sent, 'seq', shift) for shift in shifts]  127 us
    pallas_call x9, Pallas kernels, nn(): pl.pallas_call(lambda *refs: nn_kernel(each, *refs), grid=(width // tile,...  103 us
    pallas_call x6, Pallas kernels, nt(): pl.pallas_call(lambda *refs: nt_kernel(each, n, *refs), grid=(height // t...  84.5 us
    all_gather x6, waiting for transfers between devices, gather(): return lax.all_gather(run(take, x, c, rows), 'tensor', axis=0, tiled=True)  58.2 us
    pallas_call x3, Pallas kernels, tn(): pl.pallas_call(lambda *refs: tn_kernel(chunks, *refs), grid=(height // ti...  51.4 us
    pallas_call x6, Pallas kernels, gating(): pl.pallas_call(lambda *refs: kernel(len(sums[0]), *refs), grid=(width //...  38.6 us
    add x6, other arithmetic, scatter(): both = mine + lax.ppermute(others, 'tensor', cores).astype(F32)  19.4 us
  transfers between devices with their start and end apart: 27, of which 21 were waited for; matrix products, arithmetic and copies ran while one was open for 4% of the time, Pallas kernels for 41%

profile of v1, /device:TPU:0, one launch (start us, length us, event | category | flops | bytes accessed | tf_op | source)
XLA Modules:
  0.0 698.3 jit_solution(18282964258225495770)
XLA Ops:
  11.9 43.0 %all-gather.7.cloned.1.call-done.refs_2_.refs_1_ = bf16[256,4096]{1,0:T(8,128)(2,1)} async-done(((bf16[16,4096]{1,0:T(8,128)(2,1)}), bf16[256,4096]{1,0:T(8,128)(2,1)}) %all-gather.7.cloned.1.call-update) | async-done | bytes 2097168 | tf_op jit(solution)/shard_map/all_gather | solution.py:248
  54.9 11.4 %times_masked.9 = (f32[256,1792]{1,0:T(8,128)}, bf16[256,1792]{1,0:T(8,128)(2,1)}) custom-call(s32[32,14]{1,0:T(8,128)} %copy.14.refs_0_.refs_1_, s32[1]{0:T(128)} %bitcast.refs_1_.refs_0_, bf16[256,4096]{1,0:T(8,128)(2,1)} %all-gather.7.cloned.1.call-done.refs_2_.refs_1_, bf16[4096,1792]{1,0:T(8,128)(2,1)} %refs_3_.29, bf16[16,4096]{1,0:T(8,128)(2,1)} %take_rows.7.refs_4_), custom_call_target="tpu_custom_call" | custom-call | flops 3758096384 | bytes 18612224 | tf_op jit(solution)/shard_map/times_masked/pallas_call | solution.py:96
  68.6 11.4 %times_masked.10 = (f32[256,1792]{1,0:T(8,128)}, bf16[256,1792]{1,0:T(8,128)(2,1)}) custom-call(s32[32,14]{1,0:T(8,128)} %copy.15.refs_0_.refs_4_, s32[1]{0:T(128)} %bitcast.refs_1_.refs_0_, bf16[256,4096]{1,0:T(8,128)(2,1)} %all-gather.7.cloned.1.call-done.refs_2_.refs_1_, bf16[4096,1792]{1,0:T(8,128)(2,1)} %refs_6_.5, bf16[16,4096]{1,0:T(8,128)(2,1)} %take_rows.8.refs_4_), custom_call_target="tpu_custom_call" | custom-call | flops 3758096384 | bytes 18612224 | tf_op jit(solution)/shard_map/times_masked/pallas_call | solution.py:96
  83.2 14.6 %all-gather.11.cloned.1.call-done.refs_2_.refs_4_ = bf16[256,4096]{1,0:T(8,128)(2,1)} async-done(((bf16[16,4096]{1,0:T(8,128)(2,1)}), bf16[256,4096]{1,0:T(8,128)(2,1)}) %all-gather.11.cloned.1.call-update) | async-done | bytes 2097168 | tf_op jit(solution)/shard_map/all_gather | solution.py:248
  97.8 6.4 collective-permute-done.refs_5_.refs_1_
  105.2 11.5 %times_masked_transposed.6 = (f32[256,1792]{1,0:T(8,128)}, bf16[256,1792]{1,0:T(8,128)(2,1)}) custom-call(s32[1]{0:T(128)} %bitcast.refs_1_.refs_0_, s32[14,32]{1,0:T(8,128)} %refs_0_.16, bf16[256,4096]{1,0:T(8,128)(2,1)} %all-gather.11.cloned.1.call-done.refs_2_.refs_4_, bf16[1792,4096]{1,0:T(8,128)(2,1)} %refs_3_.28, bf16[16,4096]{1,0:T(8,128)(2,1)} %take_rows.9.refs_4_, ...), custom_call_target="tpu_custom_call" | custom-call | flops 3758096384 | bytes 18612224 | tf_op jit(solution)/shard_map/times_masked_transposed/pallas_call | solution.py:134
  120.0 20.2 %collective-permute-done.1.refs_5_.refs_3_ = bf16[256,1792]{1,0:T(8,128)(2,1)S(1)} collective-permute-done((bf16[256,1792]{1,0:T(8,128)(2,1)S(1)}, bf16[256,1792]{1,0:T(8,128)(2,1)S(1)}, u32[]{:S(2)}, u32[]{:S(2)}) %collective-permute-start.1) | collective-permute-done | bytes 917536 | tf_op jit(solution)/shard_map/ppermute | solution.py:260
  141.1 11.5 %times_masked.11 = (f32[256,1792]{1,0:T(8,128)}, bf16[256,1792]{1,0:T(8,128)(2,1)}) custom-call(s32[32,14]{1,0:T(8,128)} %copy.14.refs_0_.refs_1_, s32[1]{0:T(128)} %bitcast.refs_1_.refs_0_, bf16[256,4096]{1,0:T(8,128)(2,1)} %all-gather.9.cloned.1.call-done.refs_2_, bf16[4096,1792]{1,0:T(8,128)(2,1)} %refs_3_.29, bf16[16,4096]{1,0:T(8,128)(2,1)} %take_rows.10.refs_4_, ...), custom_call_target="tpu_custom_call" | custom-call | flops 3758096384 | bytes 18612224 | tf_op jit(solution)/shard_map/times_masked/pallas_call | solution.py:96
  160.1 11.4 %times_masked.12 = (f32[128,4096]{1,0:T(8,128)}, bf16[128,4096]{1,0:T(8,128)(2,1)}) custom-call(s32[14,32]{1,0:T(8,128)} %refs_0_.16, s32[1]{0:T(128)} %bitcast.refs_1_.refs_0_, bf16[256,1792]{1,0:T(8,128)(2,1)} %gating.6.refs_2_.refs_4_.refs_1_, bf16[1792,4096]{1,0:T(8,128)(2,1)} %refs_3_.28, bf16[256,1792]{1,0:T(8,128)(2,1)} %gating.6.refs_2_.refs_4_.refs_1_), custom_call_target="tpu_custom_call" | custom-call | flops 3758096384 | bytes 19791872 | tf_op jit(solution)/shard_map/times_masked/pallas_call | solution.py:96
  180.4 20.8 %collective-permute-done.4.refs_5_ = bf16[256,1792]{1,0:T(8,128)(2,1)S(1)} collective-permute-done((bf16[256,1792]{1,0:T(8,128)(2,1)S(1)}, bf16[256,1792]{1,0:T(8,128)(2,1)S(1)}, u32[]{:S(2)}, u32[]{:S(2)}) %collective-permute-start.4) | collective-permute-done | bytes 917536 | tf_op jit(solution)/shard_map/ppermute | solution.py:260
  202.2 11.7 %times_masked.13 = (f32[256,1792]{1,0:T(8,128)}, bf16[256,1792]{1,0:T(8,128)(2,1)}) custom-call(s32[32,14]{1,0:T(8,128)} %copy.15.refs_0_.refs_4_, s32[1]{0:T(128)} %bitcast.refs_1_.refs_0_, bf16[256,4096]{1,0:T(8,128)(2,1)} %all-gather.9.cloned.1.call-done.refs_2_, bf16[4096,1792]{1,0:T(8,128)(2,1)} %refs_6_.5, f32[128,4096]{1,0:T(8,128)} %get-tuple-element.47.refs_4_, ...), custom_call_target="tpu_custom_call" | custom-call | flops 3758096384 | bytes 18612224 | tf_op jit(solution)/shard_map/times_masked/pallas_call | solution.py:96
  213.9 6.9 gating.7
  220.9 16.6 %times_masked_transposed.7 = (f32[128,4096]{1,0:T(8,128)}, bf16[128,4096]{1,0:T(8,128)(2,1)}) custom-call(s32[1]{0:T(128)} %bitcast.refs_1_.refs_0_, s32[32,14]{1,0:T(8,128)} %copy.14.refs_0_.refs_1_, bf16[256,1792]{1,0:T(8,128)(2,1)} %get-tuple-element.53.refs_2_.refs_7_.refs_4_, bf16[4096,1792]{1,0:T(8,128)(2,1)} %refs_3_.29, ...), custom_call_target="tpu_custom_call" | custom-call | flops 7516192768 | bytes 35389440 | tf_op jit(solution)/shard_map/times_masked_transposed/pallas_call | solution.py:134
  246.8 21.2 %collective-permute-done.3.refs_5_.refs_1_ = bf16[256,1792]{1,0:T(8,128)(2,1)S(1)} collective-permute-done((bf16[256,1792]{1,0:T(8,128)(2,1)S(1)}, bf16[256,1792]{1,0:T(8,128)(2,1)S(1)}, u32[]{:S(2)}, u32[]{:S(2)}) %collective-permute-start.3) | collective-permute-done | bytes 917536 | tf_op jit(solution)/shard_map/ppermute | solution.py:260
  269.0 11.6 %times_masked_transposed.8 = (f32[256,1792]{1,0:T(8,128)}, bf16[256,1792]{1,0:T(8,128)(2,1)}) custom-call(s32[1]{0:T(128)} %bitcast.refs_1_.refs_0_, s32[14,32]{1,0:T(8,128)} %refs_0_.16, bf16[256,4096]{1,0:T(8,128)(2,1)} %all-gather.15.cloned.1.call-done.refs_2_.refs_5_, bf16[1792,4096]{1,0:T(8,128)(2,1)} %refs_3_.28, ...), custom_call_target="tpu_custom_call" | custom-call | flops 3758096384 | bytes 18612224 | tf_op jit(solution)/shard_map/times_masked_transposed/pallas_call | solution.py:134
  287.8 11.5 %times_masked.14 = (f32[256,1792]{1,0:T(8,128)}, bf16[256,1792]{1,0:T(8,128)(2,1)}) custom-call(s32[32,14]{1,0:T(8,128)} %copy.14.refs_0_.refs_1_, s32[1]{0:T(128)} %bitcast.refs_1_.refs_0_, bf16[256,4096]{1,0:T(8,128)(2,1)} %all-gather.13.cloned.1.call-done.refs_2_.refs_3_, bf16[4096,1792]{1,0:T(8,128)(2,1)} %refs_3_.29, ...), custom_call_target="tpu_custom_call" | custom-call | flops 3758096384 | bytes 18612224 | tf_op jit(solution)/shard_map/times_masked/pallas_call | solution.py:96
  305.2 11.3 %times_masked.15 = (f32[128,4096]{1,0:T(8,128)}, bf16[128,4096]{1,0:T(8,128)(2,1)}) custom-call(s32[14,32]{1,0:T(8,128)} %refs_0_.16, s32[1]{0:T(128)} %bitcast.refs_1_.refs_0_, bf16[256,1792]{1,0:T(8,128)(2,1)} %gating.8.refs_2_.refs_4_, bf16[1792,4096]{1,0:T(8,128)(2,1)} %refs_3_.28, bf16[256,1792]{1,0:T(8,128)(2,1)} %gating.8.refs_2_.refs_4_), custom_call_target="tpu_custom_call" | custom-call | flops 3758096384 | bytes 19791872 | tf_op jit(solution)/shard_map/times_masked/pallas_call | solution.py:96
  325.0 21.1 %collective-permute-done.8.refs_5_ = bf16[256,1792]{1,0:T(8,128)(2,1)S(1)} collective-permute-done((bf16[256,1792]{1,0:T(8,128)(2,1)S(1)}, bf16[256,1792]{1,0:T(8,128)(2,1)S(1)}, u32[]{:S(2)}, u32[]{:S(2)}) %collective-permute-start.8) | collective-permute-done | bytes 917536 | tf_op jit(solution)/shard_map/ppermute | solution.py:260
  347.0 11.6 %times_masked.16 = (f32[256,1792]{1,0:T(8,128)}, bf16[256,1792]{1,0:T(8,128)(2,1)}) custom-call(s32[32,14]{1,0:T(8,128)} %copy.15.refs_0_.refs_4_, s32[1]{0:T(128)} %bitcast.refs_1_.refs_0_, bf16[256,4096]{1,0:T(8,128)(2,1)} %all-gather.13.cloned.1.call-done.refs_2_.refs_3_, bf16[4096,1792]{1,0:T(8,128)(2,1)} %refs_6_.5, ...), custom_call_target="tpu_custom_call" | custom-call | flops 3758096384 | bytes 18612224 | tf_op jit(solution)/shard_map/times_masked/pallas_call | solution.py:96
  358.6 7.0 %gating.9 = (bf16[256,1792]{1,0:T(8,128)(2,1)}, bf16[256,1792]{1,0:T(8,128)(2,1)}) custom-call(f32[256,1792]{1,0:T(8,128)} %get-tuple-element.46.refs_0_, bf16[256,1792]{1,0:T(8,128)(2,1)} %copy-done.3, f32[256,1792]{1,0:T(8,128)} %get-tuple-element.51.refs_6_.refs_2_, bf16[256,1792]{1,0:T(8,128)(2,1)} %copy-done.2, f32[256,1792]{1,0:T(8,128)} %get-tuple-element.56.refs_4_, ...), custom_call_target="tpu_custom_call" | custom-call | flops 9175040 | bytes 10092544 | tf_op jit(solution)/shard_map/gating/pallas_call | solution.py:215
  365.6 16.6 %times_masked_transposed.9 = (f32[128,4096]{1,0:T(8,128)}, bf16[128,4096]{1,0:T(8,128)(2,1)}) custom-call(s32[1]{0:T(128)} %bitcast.refs_1_.refs_0_, s32[32,14]{1,0:T(8,128)} %copy.14.refs_0_.refs_1_, bf16[256,1792]{1,0:T(8,128)(2,1)} %get-tuple-element.64.refs_2_.refs_7_.refs_5_, bf16[4096,1792]{1,0:T(8,128)(2,1)} %refs_3_.29, ...), custom_call_target="tpu_custom_call" | custom-call | flops 7516192768 | bytes 35389440 | tf_op jit(solution)/shard_map/times_masked_transposed/pallas_call | solution.py:134
  391.5 21.2 %collective-permute-done.7.refs_5_.refs_1_ = bf16[256,1792]{1,0:T(8,128)(2,1)S(1)} collective-permute-done((bf16[256,1792]{1,0:T(8,128)(2,1)S(1)}, bf16[256,1792]{1,0:T(8,128)(2,1)S(1)}, u32[]{:S(2)}, u32[]{:S(2)}) %collective-permute-start.7) | collective-permute-done | bytes 917536 | tf_op jit(solution)/shard_map/ppermute | solution.py:260
  413.7 11.4 %times_masked_transposed.10 = (f32[256,1792]{1,0:T(8,128)}, bf16[256,1792]{1,0:T(8,128)(2,1)}) custom-call(s32[1]{0:T(128)} %bitcast.refs_1_.refs_0_, s32[14,32]{1,0:T(8,128)} %refs_0_.16, bf16[256,4096]{1,0:T(8,128)(2,1)} %all-gather.17.cloned.1.call-done.refs_2_.refs_6_, bf16[1792,4096]{1,0:T(8,128)(2,1)} %refs_3_.28, ...), custom_call_target="tpu_custom_call" | custom-call | flops 3758096384 | bytes 18612224 | tf_op jit(solution)/shard_map/times_masked_transposed/pallas_call | solution.py:134
  425.1 6.4 collective-permute-done.9.refs_3_
  438.3 11.3 %times_masked.17 = (f32[128,4096]{1,0:T(8,128)}, bf16[128,4096]{1,0:T(8,128)(2,1)}) custom-call(s32[14,32]{1,0:T(8,128)} %refs_0_.16, s32[1]{0:T(128)} %bitcast.refs_1_.refs_0_, bf16[256,1792]{1,0:T(8,128)(2,1)} %gating.10.refs_2_.refs_4_.refs_3_, bf16[1792,4096]{1,0:T(8,128)(2,1)} %refs_3_.28, bf16[256,1792]{1,0:T(8,128)(2,1)} %gating.10.refs_2_.refs_4_.refs_3_), custom_call_target="tpu_custom_call" | custom-call | flops 3758096384 | bytes 19791872 | tf_op jit(solution)/shard_map/times_masked/pallas_call | solution.py:96
  458.3 17.6 %weight_grad.3.refs_6_ = bf16[1792,4096]{1,0:T(8,128)(2,1)} custom-call(s32[14,32]{1,0:T(8,128)} %refs_0_.16, bf16[256,1792]{1,0:T(8,128)(2,1)} %gating.6.refs_2_.refs_4_.refs_1_, bf16[256,1792]{1,0:T(8,128)(2,1)} %gating.8.refs_2_.refs_4_, bf16[256,1792]{1,0:T(8,128)(2,1)} %gating.10.refs_2_.refs_4_.refs_3_, ...), custom_call_target="tpu_custom_call" | custom-call | flops 11274289152 | bytes 23724032 | tf_op jit(solution)/shard_map/weight_grad/pallas_call | solution.py:173
  480.3 6.9 gating.11
  487.2 16.8 %times_masked_transposed.11 = (f32[128,4096]{1,0:T(8,128)}, bf16[128,4096]{1,0:T(8,128)(2,1)}) custom-call(s32[1]{0:T(128)} %bitcast.refs_1_.refs_0_, s32[32,14]{1,0:T(8,128)} %copy.14.refs_0_.refs_1_, bf16[256,1792]{1,0:T(8,128)(2,1)} %get-tuple-element.73.refs_2_.refs_7_.refs_6_, bf16[4096,1792]{1,0:T(8,128)(2,1)} %refs_3_.29, ...), custom_call_target="tpu_custom_call" | custom-call | flops 7516192768 | bytes 35389440 | tf_op jit(solution)/shard_map/times_masked_transposed/pallas_call | solution.py:134
  510.1 17.0 %weight_grad.4.refs_7_ = bf16[4096,1792]{1,0:T(8,128)(2,1)} custom-call(s32[32,14]{1,0:T(8,128)} %copy.14.refs_0_.refs_1_, bf16[256,4096]{1,0:T(8,128)(2,1)} %all-gather.7.cloned.1.call-done.refs_2_.refs_1_, bf16[256,4096]{1,0:T(8,128)(2,1)} %all-gather.9.cloned.1.call-done.refs_2_, bf16[256,4096]{1,0:T(8,128)(2,1)} %all-gather.13.cloned.1.call-done.refs_2_.refs_3_, ...), custom_call_target="tpu_custom_call" | custom-call | flops 11274289152 | bytes 23724032 | tf_op jit(solution)/shard_map/weight_grad/pallas_call | solution.py:173
  527.0 16.9 %weight_grad.5 = bf16[4096,1792]{1,0:T(8,128)(2,1)} custom-call(s32[32,14]{1,0:T(8,128)} %copy.15.refs_0_.refs_4_, bf16[256,4096]{1,0:T(8,128)(2,1)} %all-gather.7.cloned.1.call-done.refs_2_.refs_1_, bf16[256,4096]{1,0:T(8,128)(2,1)} %all-gather.9.cloned.1.call-done.refs_2_, bf16[256,4096]{1,0:T(8,128)(2,1)} %all-gather.13.cloned.1.call-done.refs_2_.refs_3_, ...), custom_call_target="tpu_custom_call" | custom-call | flops 11274289152 | bytes 23724032 | tf_op jit(solution)/shard_map/weight_grad/pallas_call | solution.py:173
  549.9 69.6 %reduce-scatter.11.cloned.1.call-done = f32[16,4096]{1,0:T(8,128)} async-done(((f32[128,4096]{1,0:T(8,128)}), f32[16,4096]{1,0:T(8,128)}) %reduce-scatter.11.cloned.1.call-update) | async-done | bytes 262160 | tf_op jit(solution)/shard_map/reduce_scatter | solution.py:252
  621.2 68.5 %reduce-scatter.17.cloned.1.call-done = f32[16,4096]{1,0:T(8,128)} async-done(((f32[128,4096]{1,0:T(8,128)}), f32[16,4096]{1,0:T(8,128)}) %reduce-scatter.17.cloned.1.call-update) | async-done | bytes 262160 | tf_op jit(solution)/shard_map/reduce_scatter | solution.py:252
  (114 shorter events, 111.1 us)
Async XLA Ops:
  7.2 47.7 %all-gather.7.cloned.1.call-start = ((), (), s32[]{:S(2)}) async-start(), calls=%async_computation.6 | async-start | bytes 2228224 | tf_op jit(solution)/shard_map/all_gather | solution.py:248
  10.2 87.6 %all-gather.11.cloned.1.call-start = ((), (), s32[]{:S(2)}) async-start(), calls=%async_computation.8 | async-start | bytes 2228224 | tf_op jit(solution)/shard_map/all_gather | solution.py:248
  11.8 128.9 %all-gather.9.cloned.1.call-start = ((), (), s32[]{:S(2)}) async-start(), calls=%async_computation.7 | async-start | bytes 2228224 | tf_op jit(solution)/shard_map/all_gather | solution.py:248
  66.2 1.7 copy-start.9
  67.8 179.0 %all-gather.15.cloned.1.call-start = ((), (), s32[]{:S(2)}) async-start(), calls=%async_computation.11 | async-start | bytes 2228224 | tf_op jit(solution)/shard_map/all_gather | solution.py:248
  79.9 1.7 copy-start.16
  81.6 199.0 %all-gather.13.cloned.1.call-start = ((), (), s32[]{:S(2)}) async-start(), calls=%async_computation.10 | async-start | bytes 2228224 | tf_op jit(solution)/shard_map/all_gather | solution.py:248
  81.7 22.6 %collective-permute-start = (bf16[256,1792]{1,0:T(8,128)(2,1)S(1)}, bf16[256,1792]{1,0:T(8,128)(2,1)S(1)}, u32[]{:S(2)}, u32[]{:S(2)}) collective-permute-start(bf16[256,1792]{1,0:T(8,128)(2,1)S(1)} %copy-done.16), channel_id=1, source_target_pairs={{0,16},{16,0},{1,17},{17,1},{2,18},{18,2},{3,19},{19,3},{4,20},{20... | collective-permute-start | bytes 2752520 | tf_op jit(solution)/shard_map/ppermute | solution.py:260
  116.7 1.7 copy-start.13
  118.4 294.3 %all-gather.17.cloned.1.call-start = ((), (), s32[]{:S(2)}) async-start(), calls=%async_computation.13 | async-start | bytes 2228224 | tf_op jit(solution)/shard_map/all_gather | solution.py:248
  118.5 21.7 %collective-permute-start.1 = (bf16[256,1792]{1,0:T(8,128)(2,1)S(1)}, bf16[256,1792]{1,0:T(8,128)(2,1)S(1)}, u32[]{:S(2)}, u32[]{:S(2)}) collective-permute-start(bf16[256,1792]{1,0:T(8,128)(2,1)S(1)} %copy-done.13), channel_id=1, source_target_pairs={{0,16},{16,0},{1,17},{17,1},{2,18},{18,2},{3,19},{19,3},{4,20},{20... | collective-permute-start | bytes 2752520 | tf_op jit(solution)/shard_map/ppermute | solution.py:260
  154.1 389.8 %reduce-scatter.7.cloned.1.call-start = ((), (), s32[]{:S(2)}) async-start(), calls=%async_computation.9 | async-start | bytes 2359296 | tf_op jit(solution)/shard_map/reduce_scatter | solution.py:252
  171.5 2.9 collective-permute-start.2
  177.7 367.2 %reduce-scatter.13.cloned.1.call-start = ((), (), s32[]{:S(2)}) async-start(), calls=%async_computation.15 | async-start | bytes 2359296 | tf_op jit(solution)/shard_map/reduce_scatter | solution.py:252
  178.8 22.4 %collective-permute-start.4 = (bf16[256,1792]{1,0:T(8,128)(2,1)S(1)}, bf16[256,1792]{1,0:T(8,128)(2,1)S(1)}, u32[]{:S(2)}, u32[]{:S(2)}) collective-permute-start(bf16[256,1792]{1,0:T(8,128)(2,1)S(1)} %copy-done.12), channel_id=1, source_target_pairs={{0,16},{16,0},{1,17},{17,1},{2,18},{18,2},{3,19},{19,3},{4,20},{20... | collective-permute-start | bytes 2752520 | tf_op jit(solution)/shard_map/ppermute | solution.py:260
  237.5 2.9 collective-permute-start.11
  243.6 1.2 copy-start.10
  243.6 302.3 %reduce-scatter.9.cloned.1.call-start = ((), (), s32[]{:S(2)}) async-start(), calls=%async_computation.12 | async-start | bytes 2359296 | tf_op jit(solution)/shard_map/reduce_scatter | solution.py:252
  244.8 23.2 %collective-permute-start.3 = (bf16[256,1792]{1,0:T(8,128)(2,1)S(1)}, bf16[256,1792]{1,0:T(8,128)(2,1)S(1)}, u32[]{:S(2)}, u32[]{:S(2)}) collective-permute-start(bf16[256,1792]{1,0:T(8,128)(2,1)S(1)} %copy-done.10), channel_id=1, source_target_pairs={{0,16},{16,0},{1,17},{17,1},{2,18},{18,2},{3,19},{19,3},{4,20},{20... | collective-permute-start | bytes 2752520 | tf_op jit(solution)/shard_map/ppermute | solution.py:260
  246.1 40.8 %collective-permute-start.5 = (bf16[256,1792]{1,0:T(8,128)(2,1)}, bf16[256,1792]{1,0:T(8,128)(2,1)S(1)}, u32[]{:S(2)}, u32[]{:S(2)}) collective-permute-start(bf16[256,1792]{1,0:T(8,128)(2,1)} %get-tuple-element.52), channel_id=1, source_target_pairs={{0,16},{16,0},{1,17},{17,1},{2,18},{18,2},{3,19},{19,3},{4,20},{20... | collective-permute-start | bytes 2752520 | tf_op jit(solution)/shard_map/ppermute | solution.py:260
  316.5 2.9 collective-permute-start.6
  322.5 226.3 %reduce-scatter.15.cloned.1.call-start = ((), (), s32[]{:S(2)}) async-start(), calls=%async_computation.16 | async-start | bytes 2359296 | tf_op jit(solution)/shard_map/reduce_scatter | solution.py:252
  323.7 22.4 %collective-permute-start.8 = (bf16[256,1792]{1,0:T(8,128)(2,1)S(1)}, bf16[256,1792]{1,0:T(8,128)(2,1)S(1)}, u32[]{:S(2)}, u32[]{:S(2)}) collective-permute-start(bf16[256,1792]{1,0:T(8,128)(2,1)S(1)} %copy-done.15), channel_id=1, source_target_pairs={{0,16},{16,0},{1,17},{17,1},{2,18},{18,2},{3,19},{19,3},{4,20},{20... | collective-permute-start | bytes 2752520 | tf_op jit(solution)/shard_map/ppermute | solution.py:260
  382.2 2.9 collective-permute-start.12
  388.4 231.1 %reduce-scatter.11.cloned.1.call-start = ((), (), s32[]{:S(2)}) async-start(), calls=%async_computation.14 | async-start | bytes 2359296 | tf_op jit(solution)/shard_map/reduce_scatter | solution.py:252
  389.5 23.2 %collective-permute-start.7 = (bf16[256,1792]{1,0:T(8,128)(2,1)S(1)}, bf16[256,1792]{1,0:T(8,128)(2,1)S(1)}, u32[]{:S(2)}, u32[]{:S(2)}) collective-permute-start(bf16[256,1792]{1,0:T(8,128)(2,1)S(1)} %copy-done.11), channel_id=1, source_target_pairs={{0,16},{16,0},{1,17},{17,1},{2,18},{18,2},{3,19},{19,3},{4,20},{20... | collective-permute-start | bytes 2752520 | tf_op jit(solution)/shard_map/ppermute | solution.py:260
  390.8 40.7 %collective-permute-start.9 = (bf16[256,1792]{1,0:T(8,128)(2,1)}, bf16[256,1792]{1,0:T(8,128)(2,1)S(1)}, u32[]{:S(2)}, u32[]{:S(2)}) collective-permute-start(bf16[256,1792]{1,0:T(8,128)(2,1)} %get-tuple-element.63), channel_id=1, source_target_pairs={{0,16},{16,0},{1,17},{17,1},{2,18},{18,2},{3,19},{19,3},{4,20},{20... | collective-permute-start | bytes 2752520 | tf_op jit(solution)/shard_map/ppermute | solution.py:260
  449.7 2.9 collective-permute-start.10
  455.8 1.2 copy-start.14
  455.8 233.8 %reduce-scatter.17.cloned.1.call-start = ((), (), s32[]{:S(2)}) async-start(), calls=%async_computation.17 | async-start | bytes 2359296 | tf_op jit(solution)/shard_map/reduce_scatter | solution.py:252
  457.0 22.4 %collective-permute-start.13 = (bf16[256,1792]{1,0:T(8,128)(2,1)S(1)}, bf16[256,1792]{1,0:T(8,128)(2,1)S(1)}, u32[]{:S(2)}, u32[]{:S(2)}) collective-permute-start(bf16[256,1792]{1,0:T(8,128)(2,1)S(1)} %copy-done.14), channel_id=1, source_target_pairs={{0,16},{16,0},{1,17},{17,1},{2,18},{18,2},{3,19},{19,3},{4,20},{20... | collective-permute-start | bytes 2752520 | tf_op jit(solution)/shard_map/ppermute | solution.py:260
  504.0 2.9 collective-permute-start.14
  (12 other events, 12.1 us)
Sparse Core Ops, SparseCore 0:
  10.7 44.0 all-gather.6
  57.6 40.1 all-gather.10
  100.5 40.1 all-gather.8
  142.8 40.1 all-gather.14
  185.5 40.1 all-gather.12
  228.3 40.1 all-gather.16
  272.1 66.3 reduce-scatter.6
  342.1 66.6 reduce-scatter.12
  412.2 66.4 reduce-scatter.8
  482.2 66.6 reduce-scatter.14
  552.4 66.9 reduce-scatter.10
  622.9 66.7 reduce-scatter.16

commit v2 on v1

v2 whole, which is shorter than its diff:
```python
import jax
import jax.numpy as jnp
from jax import lax
from jax.experimental import pallas as pl
from jax.experimental.pallas import tpu as pltpu
from jax.sharding import PartitionSpec as P

BF = jnp.bfloat16
F32 = jnp.float32
BLK = 128
SHARE = 2
VMEM_LIMIT = 60 * 1024 * 1024


def cost(flops, read, written):
    return pl.CostEstimate(flops=flops // SHARE, bytes_accessed=(read + written) // SHARE, transcendentals=0)


def params():
    return pltpu.CompilerParams(
        dimension_semantics=("arbitrary",), vmem_limit_bytes=VMEM_LIMIT
    )


def pick(size, largest):
    best = BLK
    for blocks in range(1, largest // BLK + 1):
        if size % (blocks * BLK) == 0:
            best = blocks * BLK
    return best


def mask_kernel(mask_ref, w_ref, *refs):
    for j in range(w_ref.shape[1] // BLK):
        keep = mask_ref[pl.program_id(0), j].astype(F32)
        block = slice(j * BLK, (j + 1) * BLK)
        refs[-1][:, block] = (w_ref[:, block].astype(F32) * keep).astype(BF)


def masked(w, mask, after):
    block = pl.BlockSpec((BLK, w.shape[1]), lambda i: (i, 0))
    return pl.pallas_call(
        mask_kernel,
        grid=(w.shape[0] // BLK,),
        in_specs=[SMEM, block] + [UNREAD] * len(after),
        out_specs=block,
        out_shape=jax.ShapeDtypeStruct(w.shape, BF),
        compiler_params=params(),
        cost_estimate=cost(w.size, 2 * w.size, 2 * w.size),
        name="masked_weights",
    )(mask, w, *after)


def reversed_bits(value, count):
    result = 0
    for _ in range(count):
        result = result * 2 + value % 2
        value = value // 2
    return result


def store(place_ref, outs, ordered, total):
    if not ordered:
        for out in outs:
            out[...] = total.astype(out.dtype)
        return
    turned = ordered[0]
    devices, rows = turned.shape[:2]
    bits = devices.bit_length() - 1
    for r in range(devices):
        turned[lax.bitwise_xor(place_ref[0], reversed_bits(r, bits))] = total[r * rows : (r + 1) * rows]
    outs[0][...] = turned[: devices // 2]
    outs[1][...] = turned[devices // 2 :].astype(BF)


def whole_block(x):
    return pl.BlockSpec(x.shape, lambda j: (0, 0))


SMEM = pl.BlockSpec(memory_space=pltpu.SMEM)
UNREAD = pl.BlockSpec(memory_space=pl.ANY)


def product_kernel(terms, contract, by_device, place_ref, *refs):
    total = None
    for n in range(terms):
        part = lax.dot_general(
            refs[2 * n][...], refs[2 * n + 1][...], (((1,), (contract,)), ((), ())), preferred_element_type=F32
        )
        total = part if total is None else total + part
    at = len(refs) - by_device
    store(place_ref, refs[at - 2 : at], refs[at:], total)


def product(contract, place, devices, terms, tile, after):
    rows = terms[0][0].shape[0]
    width = terms[0][1].shape[1 - contract]
    depth = terms[0][1].shape[contract]
    tile = pick(width, tile)
    specs, args = [SMEM], [place]
    for x, w in terms:
        if contract:
            specs += [whole_block(x), pl.BlockSpec((tile, depth), lambda j: (j, 0))]
        else:
            specs += [whole_block(x), pl.BlockSpec((depth, tile), lambda j: (0, j))]
        args += [x, w]
    scratch = []
    if devices:
        each = rows // devices
        shape = (devices // 2, each, width)
        out_spec = pl.BlockSpec((devices // 2, each, tile), lambda j: (0, 0, j))
        scratch = [pltpu.VMEM((devices, each, tile), F32)]
    else:
        shape, out_spec = (rows, width), pl.BlockSpec((rows, tile), lambda j: (0, j))
    n = len(terms)
    return pl.pallas_call(
        lambda *refs: product_kernel(n, contract, len(scratch), *refs),
        grid=(width // tile,),
        in_specs=specs + [UNREAD] * len(after),
        out_specs=[out_spec, out_spec],
        out_shape=[jax.ShapeDtypeStruct(shape, F32), jax.ShapeDtypeStruct(shape, BF)],
        scratch_shapes=scratch,
        compiler_params=params(),
        cost_estimate=cost(
            2 * n * rows * depth * width, 2 * n * (depth * width + rows * depth), 4 * rows * width
        ),
        name="product",
    )(*args, *after)


def tn_kernel(chunks, mask_ref, *refs):
    xs, ds = refs[:chunks], refs[chunks : 2 * chunks]
    out, turned = refs[-chunks - 1], refs[-chunks:]
    height, width = out.shape
    first = pl.program_id(0) * (height // BLK)
    for x, t in zip(xs, turned):
        t[...] = x[...].T
    step = pick(width, 256)
    for n in range(0, width, step):
        total = None
        for t, d in zip(turned, ds):
            part = jnp.dot(t[...], d[:, n : n + step], preferred_element_type=F32)
            total = part if total is None else total + part
        for i in range(height // BLK):
            for j in range(step // BLK):
                keep = mask_ref[first + i, n // BLK + j].astype(F32)
                out[i * BLK : (i + 1) * BLK, n + j * BLK : n + (j + 1) * BLK] = (
                    total[i * BLK : (i + 1) * BLK, j * BLK : (j + 1) * BLK] * keep
                ).astype(BF)


def tn(xs, ds, mask, tile, after):
    chunks = len(xs)
    height, width = xs[0].shape[1], ds[0].shape[1]
    rows = sum(x.shape[0] for x in xs)
    tile = pick(height, tile)
    return pl.pallas_call(
        lambda *refs: tn_kernel(chunks, *refs),
        grid=(height // tile,),
        in_specs=[SMEM]
        + [pl.BlockSpec((x.shape[0], tile), lambda i: (0, i)) for x in xs]
        + [whole_block(d) for d in ds]
        + [UNREAD] * len(after),
        out_specs=pl.BlockSpec((tile, width), lambda i: (i, 0)),
        out_shape=jax.ShapeDtypeStruct((height, width), BF),
        scratch_shapes=[pltpu.VMEM((tile, x.shape[0]), BF) for x in xs],
        compiler_params=params(),
        cost_estimate=cost(
            2 * rows * height * width, 2 * rows * (height + width), 2 * height * width
        ),
        name="weight_grad",
    )(mask, *xs, *ds, *after)


def added(refs):
    total = refs[0][...]
    for ref in refs[1:]:
        total = total + ref[...].astype(F32)
    return total


def hidden_kernel(n, *refs):
    gate, up = added(refs[:n]), added(refs[n : 2 * n])
    refs[-1][...] = (gate * jax.nn.sigmoid(gate) * up).astype(BF)


def grads_kernel(n, *refs):
    gate, up, dh = added(refs[:n]), added(refs[n : 2 * n]), added(refs[2 * n : 3 * n])
    sig = jax.nn.sigmoid(gate)
    refs[-2][...] = (dh * up * sig * (1.0 + gate * (1.0 - sig))).astype(BF)
    refs[-1][...] = (dh * (gate * sig)).astype(BF)


def gating(kernel, sums, outs, after):
    rows, width = sums[0][0].shape
    tile = pick(width, 256)
    spec = pl.BlockSpec((rows, tile), lambda j: (0, j))
    flat = [part for parts in sums for part in parts]
    return pl.pallas_call(
        lambda *refs: kernel(len(sums[0]), *refs),
        grid=(width // tile,),
        in_specs=[spec] * len(flat) + [UNREAD] * len(after),
        out_specs=[spec] * outs,
        out_shape=[jax.ShapeDtypeStruct((rows, width), BF)] * outs,
        compiler_params=params(),
        cost_estimate=cost(20 * rows * width, 6 * len(sums) * rows * width, 2 * outs * rows * width),
        name="gating",
    )(*flat, *after)


def stage_kernel(mine_ref, got_ref, *refs):
    both = mine_ref[...] + got_ref[...].astype(F32)
    half = both.shape[0] // 2
    if half:
        refs[-2][...] = both[:half]
        refs[-1][...] = both[half:].astype(BF)
    else:
        refs[-1][...] = both.astype(BF)


def stage(mine, got, after):
    count, rows, width = mine.shape
    tile = pick(width, 1024)
    made = [(count // 2, F32), (count // 2, BF)] if count > 1 else [(count, BF)]
    block = lambda n: pl.BlockSpec((n, rows, tile), lambda j: (0, 0, j))
    return pl.pallas_call(
        stage_kernel,
        grid=(width // tile,),
        in_specs=[block(count), block(count)] + [UNREAD] * len(after),
        out_specs=[block(n) for n, _ in made],
        out_shape=[jax.ShapeDtypeStruct((n, rows, width), t) for n, t in made],
        compiler_params=params(),
        cost_estimate=cost(mine.size, 6 * mine.size, 3 * mine.size),
        name="stage",
    )(mine, got, *after)


def solution(mesh):
    size = mesh.shape["seq"]
    spread = mesh.shape["tensor"]
    bits = spread.bit_length() - 1
    FIRST, SECOND = 0, 1

    def per_device(tokens, w_gate, w_up, w_down, mask_gate, mask_up, mask_down, cotangent):
        third = tokens.shape[0] // 3
        parts = [(0, 2 * third), (2 * third, 3 * third)]
        index = lax.axis_index("tensor")
        place = jnp.reshape(reversed_bits(index, bits), (1,)).astype(jnp.int32)
        last = [mask_gate]

        def run(kernel, *args, late=()):
            out = kernel(*args, [last[0], *late])
            last[0] = out[0] if isinstance(out, (tuple, list)) else out
            return out

        def gather(x, c):
            return lax.all_gather(x[parts[c][0] : parts[c][1]], "tensor", axis=0, tiled=True)

        moving, done = [], {}

        def halving(name, mine, others):
            for bit in range(bits):
                pairs = [(i, i ^ (1 << bit)) for i in range(spread)]
                got = lax.ppermute(others, "tensor", pairs)
                yield
                sums = run(stage, mine, got)
                if len(sums) == 2:
                    mine, others = sums
            done[name] = sums[0][0]

        def start(name, sums):
            moving.append(halving(name, *sums))
            next(moving[-1])

        def advance():
            for sums in list(moving):
                next(sums, None)

        arrived = []

        def exchange(own, sent):
            shifts = [[(i, (i + k) % size) for i in range(size)] for k in range(1, size)]
            got = [lax.ppermute(sent, "seq", shift) for shift in shifts]
            arrived.append(got)
            return [own] + got

        def late():
            return arrived[-2] if len(arrived) > 1 else []

        toks = [gather(tokens, c) for c in range(2)]
        cots = [gather(cotangent, c) for c in range(2)]
        gate_w = run(masked, w_gate, mask_gate)
        up_w = run(masked, w_up, mask_up)
        down_w = run(masked, w_down, mask_down)
        hiddens, dgates, dups = [], [], []

        def ahead(x, w, contract):
            return exchange(*run(product, contract, place, 0, [(x, w)], 256, late=late()))

        def back_out(name, gate, up, wait):
            (hidden,) = run(gating, hidden_kernel, [gate, up], 1)
            hiddens.append(hidden)
            terms = [(hidden, down_w)]
            sums = run(product, 0, place, spread, terms, 512, late=wait)
            advance()
            start(name, sums)

        def back_tokens(name, gate, up, dh):
            dgate, dup = run(gating, grads_kernel, [gate, up, dh], 2)
            dgates.append(dgate)
            dups.append(dup)
            terms = [(dgate, gate_w), (dup, up_w)]
            sums = run(product, 1, place, spread, terms, 512)
            advance()
            start(name, sums)

        gates, ups, dhs = [], [], []
        for c in (FIRST, SECOND):
            gates.append(ahead(toks[c], gate_w, 0))
            ups.append(ahead(toks[c], up_w, 0))
        dhs.append(ahead(cots[FIRST], down_w, 1))
        back_out("out", gates[FIRST], ups[FIRST], [cots[SECOND], *arrived[3]])
        dhs.append(ahead(cots[SECOND], down_w, 1))
        advance()
        back_out("out last", gates[SECOND], ups[SECOND], arrived[4])
        back_tokens("tokens", gates[FIRST], ups[FIRST], dhs[FIRST])
        back_tokens("tokens last", gates[SECOND], ups[SECOND], dhs[SECOND])
        grad_down = run(tn, hiddens, cots, mask_down, 256)
        advance()
        grad_gate = run(tn, toks, dgates, mask_gate, 512)
        advance()
        grad_up = run(tn, toks, dups, mask_up, 512)
        while len(done) < 4:
            advance()
        output = jnp.concatenate([done["out"], done["out last"]], axis=0)
        grad_tokens = jnp.concatenate([done["tokens"], done["tokens last"]], axis=0)
        return (output, grad_tokens, grad_gate, grad_up, grad_down)

    return jax.shard_map(
        per_device,
        mesh=mesh,
        in_specs=(
            P("tensor", "seq"),
            P("seq", "tensor"),
            P("seq", "tensor"),
            P("tensor", "seq"),
            P("seq", "tensor"),
            P("seq", "tensor"),
            P("tensor", "seq"),
            P("tensor", "seq"),
        ),
        out_specs=(
            P("tensor", "seq"),
            P("tensor", "seq"),
            P("seq", "tensor"),
            P("seq", "tensor"),
            P("tensor", "seq"),
        ),
        check_vma=False,
    )
```

time: 702 us -> 511 us (0.73)
  waiting for transfers between devices: 343 us -> 92.5 us
  Pallas kernels: 287 us -> 343 us
  other arithmetic: 26.7 us -> 2.45 us
  starting transfers between devices: 12.1 us -> 27.7 us
  local copies, waits for them, and re-layouts: 15.4 us -> 26.2 us
    reduce_scatter x6 -> x0, waiting for transfers between devices: 140 us -> none  [scatter(): lax.psum_scatter(both, 'tensor', scatter_dimension=0, tiled=True, axis_in...]
    pallas_call x21 -> x29, Pallas kernels: 197 us -> 262 us  [the longest x10 142 us: product(): pl.pallas_call(lambda *refs: product_kernel(n, contract, len(scratch), *r...]
    all_gather x6 -> x4, waiting for transfers between devices: 58.2 us -> 0.01 us  [gather(): lax.all_gather(x[parts[c][0]:parts[c][1]], 'tensor', axis=0, tiled=True)]
    ppermute x15 -> x22, waiting for transfers between devices: 144 us -> 92.4 us  [the longest x6 73.1 us: exchange(): got = [lax.ppermute(sent, 'seq', shift) for shift in shifts]]
    add x6 -> x0, other arithmetic: 19.4 us -> none  [scatter(): both = mine + lax.ppermute(others, 'tensor', cores).astype(F32)]
    ppermute x15 -> x22, starting transfers between devices: 11.4 us -> 27.5 us  [the longest x16 16.7 us: halving(): got = lax.ppermute(others, 'tensor', pairs)]
    pallas_call x6 -> x4, Pallas kernels: 38.6 us -> 30.1 us  [gating(): pl.pallas_call(lambda *refs: kernel(len(sums[0]), *refs), grid=(width //...]
    unnamed x36 -> x60, local copies, waits for them, and re-layouts: 15.4 us -> 19.8 us
  transfers between devices with their start and end apart: 27 -> 26, of which waited for: 21 -> 6; matrix products, arithmetic and copies ran while one was open for 4% -> 1% of each run, Pallas kernels for 41% -> 55%
where the time goes in v2:
time: 511 us; the launch traced here: 506 us
  Pallas kernels  343 us (67%)
  waiting for transfers between devices  92.5 us (18%)
  starting transfers between devices  27.7 us (5%)
  local copies, waits for them, and re-layouts  26.2 us (5%)
  between operations  14 us (3%)
    pallas_call x10, Pallas kernels, product(): pl.pallas_call(lambda *refs: product_kernel(n, contract, len(scratch), *r...  142 us
    ppermute x6, waiting for transfers between devices, exchange(): got = [lax.ppermute(sent, 'seq', shift) for shift in shifts]  73.1 us
    pallas_call x3, Pallas kernels, masked(): pl.pallas_call(mask_kernel, grid=(w.shape[0] // BLK,), in_specs=[SMEM, bl...  61.9 us
    pallas_call x16, Pallas kernels, stage(): pl.pallas_call(stage_kernel, grid=(width // tile,), in_specs=[block(count...  57.5 us
    pallas_call x3, Pallas kernels, tn(): pl.pallas_call(lambda *refs: tn_kernel(chunks, *refs), grid=(height // ti...  51 us
    pallas_call x4, Pallas kernels, gating(): pl.pallas_call(lambda *refs: kernel(len(sums[0]), *refs), grid=(width //...  30.1 us
    unnamed x60, local copies, waits for them, and re-layouts  19.8 us
    ppermute x16, waiting for transfers between devices, halving(): got = lax.ppermute(others, 'tensor', pairs)  19.3 us
  transfers between devices with their start and end apart: 26, of which 6 were waited for; matrix products, arithmetic and copies ran while one was open for 1% of the time, Pallas kernels for 55%

profile of v2, /device:TPU:0, one launch (start us, length us, event | category | flops | bytes accessed | tf_op | source)
XLA Modules:
  0.0 505.5 jit_solution(11310577727662788901)
XLA Ops:
  15.4 22.6 %masked_weights.3.refs_0_.refs_2_ = bf16[4096,1792]{1,0:T(8,128)(2,1)} custom-call(s32[32,14]{1,0:T(8,128)} %copy.13.mask_ref.refs_0_, bf16[4096,1792]{1,0:T(8,128)(2,1)} %w_ref.3, s32[32,14]{1,0:T(8,128)} %copy.13.mask_ref.refs_0_), custom_call_target="tpu_custom_call" | custom-call | flops 3670016 | bytes 14680064 | tf_op jit(solution)/shard_map/masked_weights/pallas_call | solution.py:42
  38.1 22.7 %masked_weights.4.refs_0_.refs_2_.refs_4_ = bf16[4096,1792]{1,0:T(8,128)(2,1)} custom-call(s32[32,14]{1,0:T(8,128)} %copy.15.mask_ref.refs_0_, bf16[4096,1792]{1,0:T(8,128)(2,1)} %w_ref.4, bf16[4096,1792]{1,0:T(8,128)(2,1)} %masked_weights.3.refs_0_.refs_2_), custom_call_target="tpu_custom_call" | custom-call | flops 3670016 | bytes 14680064 | tf_op jit(solution)/shard_map/masked_weights/pallas_call | solution.py:42
  60.7 16.7 %masked_weights.5.refs_3_.refs_2_ = bf16[1792,4096]{1,0:T(8,128)(2,1)} custom-call(s32[14,32]{1,0:T(8,128)} %refs_0_.4, bf16[1792,4096]{1,0:T(8,128)(2,1)} %w_ref.5, bf16[4096,1792]{1,0:T(8,128)(2,1)} %masked_weights.4.refs_0_.refs_2_.refs_4_), custom_call_target="tpu_custom_call" | custom-call | flops 3670016 | bytes 14680064 | tf_op jit(solution)/shard_map/masked_weights/pallas_call | solution.py:42
  77.4 14.6 %product.10 = (f32[512,1792]{1,0:T(8,128)}, bf16[512,1792]{1,0:T(8,128)(2,1)}) custom-call(s32[1]{0:T(128)} %bitcast.refs_0_, bf16[512,4096]{1,0:T(8,128)(2,1)} %all-gather.5.cloned.1.call-done.refs_1_, bf16[4096,1792]{1,0:T(8,128)(2,1)} %masked_weights.3.refs_0_.refs_2_, bf16[1792,4096]{1,0:T(8,128)(2,1)} %masked_weights.5.refs_3_.refs_2_), custom_call_target="tpu_custom_call" | custom-call | flops 3758096384 | bytes 11272192 | tf_op jit(solution)/shard_map/product/pallas_call | solution.py:116
  94.9 14.6 %product.11 = (f32[512,1792]{1,0:T(8,128)}, bf16[512,1792]{1,0:T(8,128)(2,1)}) custom-call(s32[1]{0:T(128)} %bitcast.refs_0_, bf16[512,4096]{1,0:T(8,128)(2,1)} %all-gather.5.cloned.1.call-done.refs_1_, bf16[4096,1792]{1,0:T(8,128)(2,1)} %masked_weights.4.refs_0_.refs_2_.refs_4_, f32[512,1792]{1,0:T(8,128)} %get-tuple-element.53.refs_3_.refs_0_), custom_call_target="tpu_custom_call" | custom-call | flops 3758096384 | bytes 11272192 | tf_op jit(solution)/shard_map/product/pallas_call | solution.py:116
  109.5 26.4 %collective-permute-done.refs_4_.refs_1_ = bf16[512,1792]{1,0:T(8,128)(2,1)S(1)} collective-permute-done((bf16[512,1792]{1,0:T(8,128)(2,1)}, bf16[512,1792]{1,0:T(8,128)(2,1)S(1)}, u32[]{:S(2)}, u32[]{:S(2)}) %collective-permute-start) | collective-permute-done | bytes 1835040 | tf_op jit(solution)/shard_map/ppermute | solution.py:283
  137.2 11.5 %product.12 = (f32[256,1792]{1,0:T(8,128)}, bf16[256,1792]{1,0:T(8,128)(2,1)}) custom-call(s32[1]{0:T(128)} %bitcast.refs_0_, bf16[256,4096]{1,0:T(8,128)(2,1)} %all-gather.9.cloned.1.call-done.refs_1_.refs_2_, bf16[4096,1792]{1,0:T(8,128)(2,1)} %masked_weights.3.refs_0_.refs_2_, f32[512,1792]{1,0:T(8,128)} %get-tuple-element.55.refs_3_.refs_2_, ...), custom_call_target="tpu_custom_call" | custom-call | flops 1879048192 | bytes 9306112 | tf_op jit(solution)/shard_map/product/pallas_call | solution.py:116
  150.7 24.7 %collective-permute-done.1.refs_4_.refs_3_ = bf16[512,1792]{1,0:T(8,128)(2,1)} collective-permute-done((bf16[512,1792]{1,0:T(8,128)(2,1)}, bf16[512,1792]{1,0:T(8,128)(2,1)}, u32[]{:S(2)}, u32[]{:S(2)}) %collective-permute-start.1) | collective-permute-done | bytes 1835040 | tf_op jit(solution)/shard_map/ppermute | solution.py:283
  175.3 11.4 %product.13 = (f32[256,1792]{1,0:T(8,128)}, bf16[256,1792]{1,0:T(8,128)(2,1)}) custom-call(s32[1]{0:T(128)} %bitcast.refs_0_, bf16[256,4096]{1,0:T(8,128)(2,1)} %all-gather.9.cloned.1.call-done.refs_1_.refs_2_, bf16[4096,1792]{1,0:T(8,128)(2,1)} %masked_weights.4.refs_0_.refs_2_.refs_4_, f32[256,1792]{1,0:T(8,128)} %get-tuple-element.57.refs_3_.refs_0_, ...), custom_call_target="tpu_custom_call" | custom-call | flops 1879048192 | bytes 9306112 | tf_op jit(solution)/shard_map/product/pallas_call | solution.py:116
  188.8 6.1 %collective-permute-done.2.refs_4_.refs_1_ = bf16[256,1792]{1,0:T(8,128)(2,1)S(1)} collective-permute-done((bf16[256,1792]{1,0:T(8,128)(2,1)}, bf16[256,1792]{1,0:T(8,128)(2,1)S(1)}, u32[]{:S(2)}, u32[]{:S(2)}) %collective-permute-start.2) | collective-permute-done | bytes 917536 | tf_op jit(solution)/shard_map/ppermute | solution.py:283
  195.9 14.7 %product.14 = (f32[512,1792]{1,0:T(8,128)}, bf16[512,1792]{1,0:T(8,128)(2,1)}) custom-call(s32[1]{0:T(128)} %bitcast.refs_0_, bf16[512,4096]{1,0:T(8,128)(2,1)} %all-gather.7.cloned.1.call-done.refs_1_.refs_3_, bf16[1792,4096]{1,0:T(8,128)(2,1)} %masked_weights.5.refs_3_.refs_2_, f32[256,1792]{1,0:T(8,128)} %get-tuple-element.58.refs_3_.refs_2_, ...), custom_call_target="tpu_custom_call" | custom-call | flops 3758096384 | bytes 11272192 | tf_op jit(solution)/shard_map/product/pallas_call | solution.py:116
  210.6 7.6 %gating.4.refs_1_.refs_3_ = bf16[512,1792]{1,0:T(8,128)(2,1)} custom-call(f32[512,1792]{1,0:T(8,128)} %get-tuple-element.53.refs_3_.refs_0_, bf16[512,1792]{1,0:T(8,128)(2,1)} %copy-done, f32[512,1792]{1,0:T(8,128)} %get-tuple-element.55.refs_3_.refs_2_, bf16[512,1792]{1,0:T(8,128)(2,1)} %collective-permute-done.1.refs_4_.refs_3_, ...), custom_call_target="tpu_custom_call" | custom-call | flops 9175040 | bytes 6422528 | tf_op jit(solution)/shard_map/gating/pallas_call | solution.py:199
  219.2 14.6 %product.15 = (f32[8,32,4096]{2,1,0:T(8,128)}, bf16[8,32,4096]{2,1,0:T(8,128)(2,1)}) custom-call(s32[1]{0:T(128)} %bitcast.refs_0_, bf16[512,1792]{1,0:T(8,128)(2,1)} %gating.4.refs_1_.refs_3_, bf16[1792,4096]{1,0:T(8,128)(2,1)} %masked_weights.5.refs_3_.refs_2_, bf16[512,1792]{1,0:T(8,128)(2,1)} %gating.4.refs_1_.refs_3_, ...), custom_call_target="tpu_custom_call" | custom-call | flops 3758096384 | bytes 12451840 | tf_op jit(solution)/shard_map/product/pallas_call | solution.py:116
  235.8 11.4 %product.16 = (f32[256,1792]{1,0:T(8,128)}, bf16[256,1792]{1,0:T(8,128)(2,1)}) custom-call(s32[1]{0:T(128)} %bitcast.refs_0_, bf16[256,4096]{1,0:T(8,128)(2,1)} %all-gather.11.cloned.1.call-done.refs_4_.refs_1_, bf16[1792,4096]{1,0:T(8,128)(2,1)} %masked_weights.5.refs_3_.refs_2_, f32[8,32,4096]{2,1,0:T(8,128)} %get-tuple-element.62.refs_3_.mine_ref, ...), custom_call_target="tpu_custom_call" | custom-call | flops 1879048192 | bytes 9306112 | tf_op jit(solution)/shard_map/product/pallas_call | solution.py:116
  248.4 4.9 stage.16
  254.9 5.8 %gating.5.refs_1_.refs_3_.refs_2_ = bf16[256,1792]{1,0:T(8,128)(2,1)} custom-call(f32[256,1792]{1,0:T(8,128)} %get-tuple-element.57.refs_3_.refs_0_, bf16[256,1792]{1,0:T(8,128)(2,1)} %copy-done.2, f32[256,1792]{1,0:T(8,128)} %get-tuple-element.58.refs_3_.refs_2_, bf16[256,1792]{1,0:T(8,128)(2,1)} %copy-done.1, f32[4,32,4096]{2,1,0:T(8,128)} %get-tuple-element.65.refs_4_.mine_ref), custom_call_target="tpu_custom_call" | custom-call | flops 4587520 | bytes 3211264 | tf_op jit(solution)/shard_map/gating/pallas_call | solution.py:199
  260.8 15.9 %collective-permute-done.6.refs_4_.refs_5_ = bf16[512,1792]{1,0:T(8,128)(2,1)S(1)} collective-permute-done((bf16[512,1792]{1,0:T(8,128)(2,1)}, bf16[512,1792]{1,0:T(8,128)(2,1)S(1)}, u32[]{:S(2)}, u32[]{:S(2)}) %collective-permute-start.6) | collective-permute-done | bytes 1835040 | tf_op jit(solution)/shard_map/ppermute | solution.py:283
  277.9 11.3 %product.17 = (f32[8,16,4096]{2,1,0:T(8,128)}, bf16[8,16,4096]{2,1,0:T(8,128)(2,1)}) custom-call(s32[1]{0:T(128)} %bitcast.refs_0_, bf16[256,1792]{1,0:T(8,128)(2,1)} %gating.5.refs_1_.refs_3_.refs_2_, bf16[1792,4096]{1,0:T(8,128)(2,1)} %masked_weights.5.refs_3_.refs_2_, bf16[256,1792]{1,0:T(8,128)(2,1)} %gating.5.refs_1_.refs_3_.refs_2_, ...), custom_call_target="tpu_custom_call" | custom-call | flops 1879048192 | bytes 9895936 | tf_op jit(solution)/shard_map/product/pallas_call | solution.py:116
  290.2 3.9 stage.17
  294.1 9.7 %gating.6 = (bf16[512,1792]{1,0:T(8,128)(2,1)}, bf16[512,1792]{1,0:T(8,128)(2,1)}) custom-call(f32[512,1792]{1,0:T(8,128)} %get-tuple-element.53.refs_3_.refs_0_, bf16[512,1792]{1,0:T(8,128)(2,1)} %copy-done, f32[512,1792]{1,0:T(8,128)} %get-tuple-element.55.refs_3_.refs_2_, bf16[512,1792]{1,0:T(8,128)(2,1)} %collective-permute-done.1.refs_4_.refs_3_, ...), custom_call_target="tpu_custom_call" | custom-call | flops 9175040 | bytes 10092544 | tf_op jit(solution)/shard_map/gating/pallas_call | solution.py:199
  303.8 21.9 %product.18 = (f32[8,32,4096]{2,1,0:T(8,128)}, bf16[8,32,4096]{2,1,0:T(8,128)(2,1)}) custom-call(s32[1]{0:T(128)} %bitcast.refs_0_, bf16[512,1792]{1,0:T(8,128)(2,1)} %get-tuple-element.71.refs_1_.refs_5_.refs_3_, bf16[4096,1792]{1,0:T(8,128)(2,1)} %masked_weights.3.refs_0_.refs_2_, bf16[512,1792]{1,0:T(8,128)(2,1)} %get-tuple-element.72.refs_3_, ...), custom_call_target="tpu_custom_call" | custom-call | flops 7516192768 | bytes 20709376 | tf_op jit(solution)/shard_map/product/pallas_call | solution.py:116
  329.5 12.4 %collective-permute-done.7.got_ref = bf16[2,32,4096]{2,1,0:T(8,128)(2,1)} collective-permute-done((bf16[2,32,4096]{2,1,0:T(8,128)(2,1)}, bf16[2,32,4096]{2,1,0:T(8,128)(2,1)}, u32[]{:S(2)}, u32[]{:S(2)}) %collective-permute-start.7) | collective-permute-done | bytes 524320 | tf_op jit(solution)/shard_map/ppermute | solution.py:264
  346.2 3.9 stage.19
  355.3 6.9 %gating.7 = (bf16[256,1792]{1,0:T(8,128)(2,1)}, bf16[256,1792]{1,0:T(8,128)(2,1)}) custom-call(f32[256,1792]{1,0:T(8,128)} %get-tuple-element.57.refs_3_.refs_0_, bf16[256,1792]{1,0:T(8,128)(2,1)} %copy-done.2, f32[256,1792]{1,0:T(8,128)} %get-tuple-element.58.refs_3_.refs_2_, bf16[256,1792]{1,0:T(8,128)(2,1)} %copy-done.1, ...), custom_call_target="tpu_custom_call" | custom-call | flops 4587520 | bytes 5046272 | tf_op jit(solution)/shard_map/gating/pallas_call | solution.py:199
  362.2 16.4 %product.19 = (f32[8,16,4096]{2,1,0:T(8,128)}, bf16[8,16,4096]{2,1,0:T(8,128)(2,1)}) custom-call(s32[1]{0:T(128)} %bitcast.refs_0_, bf16[256,1792]{1,0:T(8,128)(2,1)} %get-tuple-element.79.refs_1_.refs_5_.refs_4_, bf16[4096,1792]{1,0:T(8,128)(2,1)} %masked_weights.3.refs_0_.refs_2_, bf16[256,1792]{1,0:T(8,128)(2,1)} %get-tuple-element.80.refs_3_.refs_4_, ...), custom_call_target="tpu_custom_call" | custom-call | flops 3758096384 | bytes 17694720 | tf_op jit(solution)/shard_map/product/pallas_call | solution.py:116
  387.9 5.0 stage.22
  394.9 17.5 %weight_grad.3.refs_0_ = bf16[1792,4096]{1,0:T(8,128)(2,1)} custom-call(s32[14,32]{1,0:T(8,128)} %refs_0_.4, bf16[512,1792]{1,0:T(8,128)(2,1)} %gating.4.refs_1_.refs_3_, bf16[256,1792]{1,0:T(8,128)(2,1)} %gating.5.refs_1_.refs_3_.refs_2_, bf16[512,4096]{1,0:T(8,128)(2,1)} %all-gather.7.cloned.1.call-done.refs_1_.refs_3_, ...), custom_call_target="tpu_custom_call" | custom-call | flops 5637144576 | bytes 11862016 | tf_op jit(solution)/shard_map/weight_grad/pallas_call | solution.py:157
  417.6 3.9 stage.24
  422.4 4.0 stage.25
  428.5 16.7 %weight_grad.4.refs_0_ = bf16[4096,1792]{1,0:T(8,128)(2,1)} custom-call(s32[32,14]{1,0:T(8,128)} %copy.13.mask_ref.refs_0_, bf16[512,4096]{1,0:T(8,128)(2,1)} %all-gather.5.cloned.1.call-done.refs_1_, bf16[256,4096]{1,0:T(8,128)(2,1)} %all-gather.9.cloned.1.call-done.refs_1_.refs_2_, bf16[512,1792]{1,0:T(8,128)(2,1)} %get-tuple-element.71.refs_1_.refs_5_.refs_3_, ...), custom_call_target="tpu_custom_call" | custom-call | flops 5637144576 | bytes 11862016 | tf_op jit(solution)/shard_map/weight_grad/pallas_call | solution.py:157
  461.2 16.7 %weight_grad.5.refs_0_ = bf16[4096,1792]{1,0:T(8,128)(2,1)} custom-call(s32[32,14]{1,0:T(8,128)} %copy.15.mask_ref.refs_0_, bf16[512,4096]{1,0:T(8,128)(2,1)} %all-gather.5.cloned.1.call-done.refs_1_, bf16[256,4096]{1,0:T(8,128)(2,1)} %all-gather.9.cloned.1.call-done.refs_1_.refs_2_, bf16[512,1792]{1,0:T(8,128)(2,1)} %get-tuple-element.72.refs_3_, ...), custom_call_target="tpu_custom_call" | custom-call | flops 5637144576 | bytes 11862016 | tf_op jit(solution)/shard_map/weight_grad/pallas_call | solution.py:157
  486.9 6.8 %collective-permute-done.21.got_ref = bf16[1,16,4096]{2,1,0:T(8,128)(2,1)S(1)} collective-permute-done((bf16[1,16,4096]{2,1,0:T(8,128)(2,1)}, bf16[1,16,4096]{2,1,0:T(8,128)(2,1)S(1)}, u32[]{:S(2)}, u32[]{:S(2)}) %collective-permute-start.21) | collective-permute-done | bytes 131104 | tf_op jit(solution)/shard_map/ppermute | solution.py:264
  (126 shorter events, 88.4 us)
Async XLA Ops:
  7.2 6.9 %copy-start.23 = (s32[32,14]{0,1:T(8,128)S(1)}, s32[32,14]{0,1:T(8,128)}, u32[]{:S(2)}) copy-start(s32[32,14]{0,1:T(8,128)} %param.12) | copy-start | bytes 5380
  7.2 7.6 %copy-start.24 = (s32[32,14]{0,1:T(8,128)S(1)}, s32[32,14]{0,1:T(8,128)}, u32[]{:S(2)}) copy-start(s32[32,14]{0,1:T(8,128)} %param.13) | copy-start | bytes 5380
  7.2 70.2 %all-gather.5.cloned.1.call-start = ((), (), s32[]{:S(2)}) async-start(), calls=%async_computation | async-start | bytes 4456448 | tf_op jit(solution)/shard_map/all_gather | solution.py:257
  8.9 100.6 %all-gather.9.cloned.1.call-start = ((), (), s32[]{:S(2)}) async-start(), calls=%async_computation.2 | async-start | bytes 2228224 | tf_op jit(solution)/shard_map/all_gather | solution.py:257
  10.6 178.2 %all-gather.7.cloned.1.call-start = ((), (), s32[]{:S(2)}) async-start(), calls=%async_computation.1 | async-start | bytes 4456448 | tf_op jit(solution)/shard_map/all_gather | solution.py:257
  12.3 205.9 %all-gather.11.cloned.1.call-start = ((), (), s32[]{:S(2)}) async-start(), calls=%async_computation.3 | async-start | bytes 2228224 | tf_op jit(solution)/shard_map/all_gather | solution.py:257
  91.9 44.0 %collective-permute-start = (bf16[512,1792]{1,0:T(8,128)(2,1)}, bf16[512,1792]{1,0:T(8,128)(2,1)S(1)}, u32[]{:S(2)}, u32[]{:S(2)}) collective-permute-start(bf16[512,1792]{1,0:T(8,128)(2,1)} %get-tuple-element.54), channel_id=1, source_target_pairs={{0,16},{16,0},{1,17},{17,1},{2,18},{18,2},{3,19},{19,3},{4,20},{20... | collective-permute-start | bytes 5505032 | tf_op jit(solution)/shard_map/ppermute | solution.py:283
  109.5 65.8 %collective-permute-start.1 = (bf16[512,1792]{1,0:T(8,128)(2,1)}, bf16[512,1792]{1,0:T(8,128)(2,1)}, u32[]{:S(2)}, u32[]{:S(2)}) collective-permute-start(bf16[512,1792]{1,0:T(8,128)(2,1)} %get-tuple-element.56), channel_id=1, source_target_pairs={{0,16},{16,0},{1,17},{17,1},{2,18},{18,2},{3,19},{19,3},{4,20},{20... | collective-permute-start | bytes 5505032 | tf_op jit(solution)/shard_map/ppermute | solution.py:283
  148.7 46.2 %collective-permute-start.2 = (bf16[256,1792]{1,0:T(8,128)(2,1)}, bf16[256,1792]{1,0:T(8,128)(2,1)S(1)}, u32[]{:S(2)}, u32[]{:S(2)}) collective-permute-start(bf16[256,1792]{1,0:T(8,128)(2,1)} %get-tuple-element.59), channel_id=1, source_target_pairs={{0,16},{16,0},{1,17},{17,1},{2,18},{18,2},{3,19},{19,3},{4,20},{20... | collective-permute-start | bytes 2752520 | tf_op jit(solution)/shard_map/ppermute | solution.py:283
  186.7 31.5 %collective-permute-start.3 = (bf16[256,1792]{1,0:T(8,128)(2,1)}, bf16[256,1792]{1,0:T(8,128)(2,1)S(1)}, u32[]{:S(2)}, u32[]{:S(2)}) collective-permute-start(bf16[256,1792]{1,0:T(8,128)(2,1)} %get-tuple-element.61), channel_id=1, source_target_pairs={{0,16},{16,0},{1,17},{17,1},{2,18},{18,2},{3,19},{19,3},{4,20},{20... | collective-permute-start | bytes 2752520 | tf_op jit(solution)/shard_map/ppermute | solution.py:283
  233.7 13.4 %collective-permute-start.4 = (bf16[8,32,4096]{2,1,0:T(8,128)(2,1)}, bf16[8,32,4096]{2,1,0:T(8,128)(2,1)S(1)}, u32[]{:S(2)}, u32[]{:S(2)}) collective-permute-start(bf16[8,32,4096]{2,1,0:T(8,128)(2,1)} %get-tuple-element.63), channel_id=1, source_target_pairs={{0,1},{1,0},{2,3},{3,2},{4,5},{5,4},{6,7},{7,6},{8,9},{9,8},{10,11... | collective-permute-start | bytes 6291464 | tf_op jit(solution)/shard_map/ppermute | solution.py:264
  233.7 42.9 %collective-permute-start.6 = (bf16[512,1792]{1,0:T(8,128)(2,1)}, bf16[512,1792]{1,0:T(8,128)(2,1)S(1)}, u32[]{:S(2)}, u32[]{:S(2)}) collective-permute-start(bf16[512,1792]{1,0:T(8,128)(2,1)} %get-tuple-element.67), channel_id=1, source_target_pairs={{0,16},{16,0},{1,17},{17,1},{2,18},{18,2},{3,19},{19,3},{4,20},{20... | collective-permute-start | bytes 5505032 | tf_op jit(solution)/shard_map/ppermute | solution.py:283
  253.4 35.8 %collective-permute-start.5 = (bf16[4,32,4096]{2,1,0:T(8,128)(2,1)}, bf16[4,32,4096]{2,1,0:T(8,128)(2,1)S(1)}, u32[]{:S(2)}, u32[]{:S(2)}) collective-permute-start(bf16[4,32,4096]{2,1,0:T(8,128)(2,1)} %get-tuple-element.66), channel_id=1, source_target_pairs={{0,2},{1,3},{2,0},{3,1},{4,6},{5,7},{6,4},{7,5},{8,10},{9,11},{10,... | collective-permute-start | bytes 3145736 | tf_op jit(solution)/shard_map/ppermute | solution.py:264
  325.7 60.9 %collective-permute-start.13 = (bf16[8,32,4096]{2,1,0:T(8,128)(2,1)}, bf16[8,32,4096]{2,1,0:T(8,128)(2,1)S(1)}, u32[]{:S(2)}, u32[]{:S(2)}) collective-permute-start(bf16[8,32,4096]{2,1,0:T(8,128)(2,1)} %get-tuple-element.85), channel_id=1, source_target_pairs={{0,1},{1,0},{2,3},{3,2},{4,5},{5,4},{6,7},{7,6},{8,9},{9,8},{10,11... | collective-permute-start | bytes 6291464 | tf_op jit(solution)/shard_map/ppermute | solution.py:264
  325.7 19.6 %collective-permute-start.10 = (bf16[8,16,4096]{2,1,0:T(8,128)(2,1)}, bf16[8,16,4096]{2,1,0:T(8,128)(2,1)S(1)}, u32[]{:S(2)}, u32[]{:S(2)}) collective-permute-start(bf16[8,16,4096]{2,1,0:T(8,128)(2,1)} %get-tuple-element.77), channel_id=1, source_target_pairs={{0,1},{1,0},{2,3},{3,2},{4,5},{5,4},{6,7},{7,6},{8,9},{9,8},{10,11... | collective-permute-start | bytes 3145736 | tf_op jit(solution)/shard_map/ppermute | solution.py:264
  326.2 28.1 %collective-permute-start.9 = (bf16[256,1792]{1,0:T(8,128)(2,1)}, bf16[256,1792]{1,0:T(8,128)(2,1)S(1)}, u32[]{:S(2)}, u32[]{:S(2)}) collective-permute-start(bf16[256,1792]{1,0:T(8,128)(2,1)} %get-tuple-element.76), channel_id=1, source_target_pairs={{0,16},{16,0},{1,17},{17,1},{2,18},{18,2},{3,19},{19,3},{4,20},{20... | collective-permute-start | bytes 2752520 | tf_op jit(solution)/shard_map/ppermute | solution.py:283
  327.9 13.9 %collective-permute-start.7 = (bf16[2,32,4096]{2,1,0:T(8,128)(2,1)}, bf16[2,32,4096]{2,1,0:T(8,128)(2,1)}, u32[]{:S(2)}, u32[]{:S(2)}) collective-permute-start(bf16[2,32,4096]{2,1,0:T(8,128)(2,1)} %get-tuple-element.70), channel_id=1, source_target_pairs={{0,4},{1,5},{2,6},{3,7},{4,0},{5,1},{6,2},{7,3},{8,12},{9,13},{10,... | collective-permute-start | bytes 1572872 | tf_op jit(solution)/shard_map/ppermute | solution.py:264
  350.1 32.3 %collective-permute-start.11 = (bf16[4,16,4096]{2,1,0:T(8,128)(2,1)}, bf16[4,16,4096]{2,1,0:T(8,128)(2,1)S(1)}, u32[]{:S(2)}, u32[]{:S(2)}) collective-permute-start(bf16[4,16,4096]{2,1,0:T(8,128)(2,1)} %get-tuple-element.82), channel_id=1, source_target_pairs={{0,2},{1,3},{2,0},{3,1},{4,6},{5,7},{6,4},{7,5},{8,10},{9,11},{10,... | collective-permute-start | bytes 1572872 | tf_op jit(solution)/shard_map/ppermute | solution.py:264
  351.7 26.9 %collective-permute-start.8 = (bf16[1,32,4096]{2,1,0:T(8,128)(2,1)}, bf16[1,32,4096]{2,1,0:T(8,128)(2,1)S(1)}, u32[]{:S(2)}, u32[]{:S(2)}) collective-permute-start(bf16[1,32,4096]{2,1,0:T(8,128)(2,1)} %get-tuple-element.75), channel_id=1, source_target_pairs={{0,8},{1,9},{2,10},{3,11},{4,12},{5,13},{6,14},{7,15},{8,0},{9,1},... | collective-permute-start | bytes 786440 | tf_op jit(solution)/shard_map/ppermute | solution.py:264
  392.9 23.7 %collective-permute-start.16 = (bf16[4,32,4096]{2,1,0:T(8,128)(2,1)}, bf16[4,32,4096]{2,1,0:T(8,128)(2,1)S(1)}, u32[]{:S(2)}, u32[]{:S(2)}) collective-permute-start(bf16[4,32,4096]{2,1,0:T(8,128)(2,1)} %get-tuple-element.90), channel_id=1, source_target_pairs={{0,2},{1,3},{2,0},{3,1},{4,6},{5,7},{6,4},{7,5},{8,10},{9,11},{10,... | collective-permute-start | bytes 3145736 | tf_op jit(solution)/shard_map/ppermute | solution.py:264
  393.3 28.2 %collective-permute-start.15 = (bf16[8,16,4096]{2,1,0:T(8,128)(2,1)S(1)}, bf16[8,16,4096]{2,1,0:T(8,128)(2,1)S(1)}, u32[]{:S(2)}, u32[]{:S(2)}) collective-permute-start(bf16[8,16,4096]{2,1,0:T(8,128)(2,1)S(1)} %copy-done.25), channel_id=1, source_target_pairs={{0,1},{1,0},{2,3},{3,2},{4,5},{5,4},{6,7},{7,6},{8,9},{9,8},{10,11... | collective-permute-start | bytes 3145736 | tf_op jit(solution)/shard_map/ppermute | solution.py:264
  393.3 19.1 %collective-permute-start.12 = (bf16[2,16,4096]{2,1,0:T(8,128)(2,1)S(1)}, bf16[2,16,4096]{2,1,0:T(8,128)(2,1)S(1)}, u32[]{:S(2)}, u32[]{:S(2)}) collective-permute-start(bf16[2,16,4096]{2,1,0:T(8,128)(2,1)S(1)} %copy-done.27), channel_id=1, source_target_pairs={{0,4},{1,5},{2,6},{3,7},{4,0},{5,1},{6,2},{7,3},{8,12},{9,13},{10,... | collective-permute-start | bytes 786440 | tf_op jit(solution)/shard_map/ppermute | solution.py:264
  416.3 29.0 %collective-permute-start.14 = (bf16[1,16,4096]{2,1,0:T(8,128)(2,1)}, bf16[1,16,4096]{2,1,0:T(8,128)(2,1)S(1)}, u32[]{:S(2)}, u32[]{:S(2)}) collective-permute-start(bf16[1,16,4096]{2,1,0:T(8,128)(2,1)} %get-tuple-element.88), channel_id=1, source_target_pairs={{0,8},{1,9},{2,10},{3,11},{4,12},{5,13},{6,14},{7,15},{8,0},{9,1},... | collective-permute-start | bytes 393224 | tf_op jit(solution)/shard_map/ppermute | solution.py:264
  426.4 26.6 %collective-permute-start.19 = (bf16[4,16,4096]{2,1,0:T(8,128)(2,1)}, bf16[4,16,4096]{2,1,0:T(8,128)(2,1)S(1)}, u32[]{:S(2)}, u32[]{:S(2)}) collective-permute-start(bf16[4,16,4096]{2,1,0:T(8,128)(2,1)} %get-tuple-element.96), channel_id=1, source_target_pairs={{0,2},{1,3},{2,0},{3,1},{4,6},{5,7},{6,4},{7,5},{8,10},{9,11},{10,... | collective-permute-start | bytes 1572872 | tf_op jit(solution)/shard_map/ppermute | solution.py:264
  428.0 20.8 %collective-permute-start.17 = (bf16[2,32,4096]{2,1,0:T(8,128)(2,1)S(1)}, bf16[2,32,4096]{2,1,0:T(8,128)(2,1)S(1)}, u32[]{:S(2)}, u32[]{:S(2)}) collective-permute-start(bf16[2,32,4096]{2,1,0:T(8,128)(2,1)S(1)} %copy-done.26), channel_id=1, source_target_pairs={{0,4},{1,5},{2,6},{3,7},{4,0},{5,1},{6,2},{7,3},{8,12},{9,13},{10,... | collective-permute-start | bytes 1572872 | tf_op jit(solution)/shard_map/ppermute | solution.py:264
  453.0 5.8 %copy-start.28 = (bf16[1,32,4096]{2,1,0:T(8,128)(2,1)S(1)}, bf16[1,32,4096]{2,1,0:T(8,128)(2,1)}, u32[]{:S(2)}) copy-start(bf16[1,32,4096]{2,1,0:T(8,128)(2,1)} %get-tuple-element.95) | copy-start | bytes 786436
  457.2 24.6 %collective-permute-start.20 = (bf16[2,16,4096]{2,1,0:T(8,128)(2,1)}, bf16[2,16,4096]{2,1,0:T(8,128)(2,1)S(1)}, u32[]{:S(2)}, u32[]{:S(2)}) collective-permute-start(bf16[2,16,4096]{2,1,0:T(8,128)(2,1)} %get-tuple-element.98), channel_id=1, source_target_pairs={{0,4},{1,5},{2,6},{3,7},{4,0},{5,1},{6,2},{7,3},{8,12},{9,13},{10,... | collective-permute-start | bytes 786440 | tf_op jit(solution)/shard_map/ppermute | solution.py:264
  458.8 19.2 %collective-permute-start.18 = (bf16[1,32,4096]{2,1,0:T(8,128)(2,1)S(1)}, bf16[1,32,4096]{2,1,0:T(8,128)(2,1)S(1)}, u32[]{:S(2)}, u32[]{:S(2)}) collective-permute-start(bf16[1,32,4096]{2,1,0:T(8,128)(2,1)S(1)} %copy-done.28), channel_id=1, source_target_pairs={{0,8},{1,9},{2,10},{3,11},{4,12},{5,13},{6,14},{7,15},{8,0},{9,1},... | collective-permute-start | bytes 786440 | tf_op jit(solution)/shard_map/ppermute | solution.py:264
  478.0 8.1 %copy-start.5 = (bf16[1,32,4096]{2,1,0:T(8,128)(2,1)S(1)}, bf16[1,32,4096]{2,1,0:T(8,128)(2,1)}, u32[]{:S(2)}) copy-start(bf16[1,32,4096]{2,1,0:T(8,128)(2,1)} %stage.20.refs_0_) | copy-start | bytes 786436
  478.0 8.1 %copy-start.8 = (bf16[1,16,4096]{2,1,0:T(8,128)(2,1)S(1)}, bf16[1,16,4096]{2,1,0:T(8,128)(2,1)}, u32[]{:S(2)}) copy-start(bf16[1,16,4096]{2,1,0:T(8,128)(2,1)} %stage.26.refs_0_) | copy-start | bytes 393220
  481.8 15.5 %copy-start.4 = (bf16[1,32,4096]{2,1,0:T(8,128)(2,1)S(1)}, bf16[1,32,4096]{2,1,0:T(8,128)(2,1)}, u32[]{:S(2)}) copy-start(bf16[1,32,4096]{2,1,0:T(8,128)(2,1)} %stage.29.refs_0_) | copy-start | bytes 786436
  485.7 8.1 %collective-permute-start.21 = (bf16[1,16,4096]{2,1,0:T(8,128)(2,1)}, bf16[1,16,4096]{2,1,0:T(8,128)(2,1)S(1)}, u32[]{:S(2)}, u32[]{:S(2)}) collective-permute-start(bf16[1,16,4096]{2,1,0:T(8,128)(2,1)} %get-tuple-element.100), channel_id=1, source_target_pairs={{0,8},{1,9},{2,10},{3,11},{4,12},{5,13},{6,14},{7,15},{8,0},{9,1},... | collective-permute-start | bytes 393224 | tf_op jit(solution)/shard_map/ppermute | solution.py:264
  (23 other events, 34.7 us)
Sparse Core Ops, SparseCore 0:
  10.8 53.2 all-gather.4
  66.2 39.8 all-gather.8
  108.9 49.3 all-gather.6
  160.2 39.7 all-gather.10

commit v3 on v2

--- a/solution.py
+++ b/solution.py
@@ -31,17 +31,20 @@
 
 
 def mask_kernel(mask_ref, w_ref, *refs):
-    for j in range(w_ref.shape[1] // BLK):
-        keep = mask_ref[pl.program_id(0), j].astype(F32)
-        block = slice(j * BLK, (j + 1) * BLK)
-        refs[-1][:, block] = (w_ref[:, block].astype(F32) * keep).astype(BF)
+    blocks = w_ref.shape[0] // BLK
+    for i in range(blocks):
+        for j in range(w_ref.shape[1] // BLK):
+            keep = mask_ref[pl.program_id(0) * blocks + i, j].astype(F32)
+            block = (slice(i * BLK, (i + 1) * BLK), slice(j * BLK, (j + 1) * BLK))
+            refs[-1][block] = (w_ref[block].astype(F32) * keep).astype(BF)
 
 
 def masked(w, mask, after):
-    block = pl.BlockSpec((BLK, w.shape[1]), lambda i: (i, 0))
+    tall = pick(w.shape[0], 2 * 1024 * 1024 // w.shape[1])
+    block = pl.BlockSpec((tall, w.shape[1]), lambda i: (i, 0))
     return pl.pallas_call(
         mask_kernel,
-        grid=(w.shape[0] // BLK,),
+        grid=(w.shape[0] // tall,),
         in_specs=[SMEM, block] + [UNREAD] * len(after),
         out_specs=block,
         out_shape=jax.ShapeDtypeStruct(w.shape, BF),
@@ -220,7 +223,7 @@
 
 def stage(mine, got, after):
     count, rows, width = mine.shape
-    tile = pick(width, 1024)
+    tile = pick(width, 256 * 1024 // (count * rows))
     made = [(count // 2, F32), (count // 2, BF)] if count > 1 else [(count, BF)]
     block = lambda n: pl.BlockSpec((n, rows, tile), lambda j: (0, 0, j))
     return pl.pallas_call(
@@ -287,26 +290,23 @@
         def late():
             return arrived[-2] if len(arrived) > 1 else []
 
-        toks = [gather(tokens, c) for c in range(2)]
-        cots = [gather(cotangent, c) for c in range(2)]
+        toks, cots = [], []
+        for c in range(2):
+            toks.append(gather(tokens, c))
+            cots.append(gather(cotangent, c))
         gate_w = run(masked, w_gate, mask_gate)
         up_w = run(masked, w_up, mask_up)
-        down_w = run(masked, w_down, mask_down)
         hiddens, dgates, dups = [], [], []
 
         def ahead(x, w, contract):
             return exchange(*run(product, contract, place, 0, [(x, w)], 256, late=late()))
 
-        def back_out(name, gate, up, wait):
-            (hidden,) = run(gating, hidden_kernel, [gate, up], 1)
-            hiddens.append(hidden)
-            terms = [(hidden, down_w)]
-            sums = run(product, 0, place, spread, terms, 512, late=wait)
+        def back_out(name, wait):
+            sums = run(product, 0, place, spread, [(hiddens[-1], down_w)], 512, late=wait)
             advance()
             start(name, sums)
 
-        def back_tokens(name, gate, up, dh):
-            dgate, dup = run(gating, grads_kernel, [gate, up, dh], 2)
+        def back_tokens(name, dgate, dup):
             dgates.append(dgate)
             dups.append(dup)
             terms = [(dgate, gate_w), (dup, up_w)]
@@ -314,17 +314,35 @@
             advance()
             start(name, sums)
 
+        def make_hidden(c, wait):
+            hiddens.extend(run(gating, hidden_kernel, [gates[c], ups[c]], 1, late=wait))
+
+        def exchange_halves(own, sent):
+            half = sent.shape[0] // 2
+            first, last = exchange(own, sent[:half])[1:], exchange(own, sent[half:])[1:]
+            return [own] + [jnp.concatenate(both, axis=0) for both in zip(first, last)], first
+
         gates, ups, dhs = [], [], []
-        for c in (FIRST, SECOND):
-            gates.append(ahead(toks[c], gate_w, 0))
-            ups.append(ahead(toks[c], up_w, 0))
-        dhs.append(ahead(cots[FIRST], down_w, 1))
-        back_out("out", gates[FIRST], ups[FIRST], [cots[SECOND], *arrived[3]])
-        dhs.append(ahead(cots[SECOND], down_w, 1))
+        gates.append(ahead(toks[FIRST], gate_w, 0))
+        ups.append(ahead(toks[FIRST], up_w, 0))
+        down_w = run(masked, w_down, mask_down)
+        sums = run(product, 1, place, 0, [(cots[FIRST], down_w)], 256, late=late())
+        dh, first_half = exchange_halves(*sums)
+        dhs.append(dh)
+        gates.append(exchange(*run(product, 0, place, 0, [(toks[SECOND], gate_w)], 256, late=arrived[1])))
+        make_hidden(FIRST, [])
+        back_out("out", [cots[SECOND], *first_half])
+        ups.append(exchange(*run(product, 0, place, 0, [(toks[SECOND], up_w)], 256)))
         advance()
-        back_out("out last", gates[SECOND], ups[SECOND], arrived[4])
-        back_tokens("tokens", gates[FIRST], ups[FIRST], dhs[FIRST])
-        back_tokens("tokens last", gates[SECOND], ups[SECOND], dhs[SECOND])
+        dgrads = run(gating, grads_kernel, [gates[FIRST], ups[FIRST], dhs[FIRST]], 2)
+        sums = run(product, 1, place, 0, [(cots[SECOND], down_w)], 256, late=gates[SECOND][1:])
+        dhs.append(exchange(*sums))
+        advance()
+        back_tokens("tokens", *dgrads)
+        make_hidden(SECOND, [])
+        back_out("out last", [])
+        dgrads = run(gating, grads_kernel, [gates[SECOND], ups[SECOND], dhs[SECOND]], 2)
+        back_tokens("tokens last", *dgrads)
         grad_down = run(tn, hiddens, cots, mask_down, 256)
         advance()
         grad_gate = run(tn, toks, dgates, mask_gate, 512)

time: 511 us -> 482 us (0.943)
  Pallas kernels: 343 us -> 302 us
  waiting for transfers between devices: 92.5 us -> 108 us
  starting transfers between devices: 27.7 us -> 20.4 us
    all_gather x4, waiting for transfers between devices: 0.01 us -> 68 us  [gather(): lax.all_gather(x[parts[c][0]:parts[c][1]], 'tensor', axis=0, tiled=True)]
    ppermute x6 -> x7, waiting for transfers between devices: 73.1 us -> 23.2 us  [exchange(): got = [lax.ppermute(sent, 'seq', shift) for shift in shifts]]
    pallas_call x3, Pallas kernels: 61.9 us -> 37.4 us  [masked(): pl.pallas_call(mask_kernel, grid=(w.shape[0] // tall,), in_specs=[SMEM, b...]
    pallas_call x16, Pallas kernels: 57.5 us -> 41.1 us  [stage(): pl.pallas_call(stage_kernel, grid=(width // tile,), in_specs=[block(count...]
    ppermute x6 -> x7, starting transfers between devices: 10.8 us -> 7.25 us  [exchange(): got = [lax.ppermute(sent, 'seq', shift) for shift in shifts]]
    unnamed x60 -> x54, local copies, waits for them, and re-layouts: 19.8 us -> 18.7 us
  transfers between devices with their start and end apart: 26 -> 27, of which waited for: 6 -> 11; matrix products, arithmetic and copies ran while one was open for 1% -> 3% of each run, Pallas kernels for 55% -> 54%
where the time goes in v3:
time: 482 us; the launch traced here: 479 us
  Pallas kernels  302 us (63%)
  waiting for transfers between devices  108 us (22%)
  local copies, waits for them, and re-layouts  28 us (6%)
  starting transfers between devices  20.4 us (4%)
  between operations  14 us (3%)
  other arithmetic  5.87 us (1%)
    pallas_call x10, Pallas kernels, product(): pl.pallas_call(lambda *refs: product_kernel(n, contract, len(scratch), *r...  143 us
    all_gather x4, waiting for transfers between devices, gather(): lax.all_gather(x[parts[c][0]:parts[c][1]], 'tensor', axis=0, tiled=True)  68 us
    pallas_call x3, Pallas kernels, tn(): pl.pallas_call(lambda *refs: tn_kernel(chunks, *refs), grid=(height // ti...  50.9 us
    pallas_call x16, Pallas kernels, stage(): pl.pallas_call(stage_kernel, grid=(width // tile,), in_specs=[block(count...  41.1 us
    pallas_call x3, Pallas kernels, masked(): pl.pallas_call(mask_kernel, grid=(w.shape[0] // tall,), in_specs=[SMEM, b...  37.4 us
    pallas_call x4, Pallas kernels, gating(): pl.pallas_call(lambda *refs: kernel(len(sums[0]), *refs), grid=(width //...  30.2 us
    ppermute x7, waiting for transfers between devices, exchange(): got = [lax.ppermute(sent, 'seq', shift) for shift in shifts]  23.2 us
    unnamed x54, local copies, waits for them, and re-layouts  18.7 us
  transfers between devices with their start and end apart: 27, of which 11 were waited for; matrix products, arithmetic and copies ran while one was open for 3% of the time, Pallas kernels for 54%

profile of v3, /device:TPU:0, one launch (start us, length us, event | category | flops | bytes accessed | tf_op | source)
XLA Modules:
  0.0 478.6 jit_solution(3220114527384753413)
XLA Ops:
  15.4 11.4 %masked_weights.3.refs_0_.refs_2_ = bf16[4096,1792]{1,0:T(8,128)(2,1)} custom-call(s32[32,14]{1,0:T(8,128)} %copy.13.mask_ref.refs_0_, bf16[4096,1792]{1,0:T(8,128)(2,1)} %w_ref.3, s32[32,14]{1,0:T(8,128)} %copy.13.mask_ref.refs_0_), custom_call_target="tpu_custom_call" | custom-call | flops 3670016 | bytes 14680064 | tf_op jit(solution)/shard_map/masked_weights/pallas_call | solution.py:45
  26.8 11.4 %masked_weights.4.refs_3_.refs_2_.refs_4_ = bf16[4096,1792]{1,0:T(8,128)(2,1)} custom-call(s32[32,14]{1,0:T(8,128)} %copy.15.mask_ref.refs_0_, bf16[4096,1792]{1,0:T(8,128)(2,1)} %w_ref.4, bf16[4096,1792]{1,0:T(8,128)(2,1)} %masked_weights.3.refs_0_.refs_2_), custom_call_target="tpu_custom_call" | custom-call | flops 3670016 | bytes 14680064 | tf_op jit(solution)/shard_map/masked_weights/pallas_call | solution.py:45
  38.2 25.9 %all-gather.5.cloned.1.call-done.refs_1_ = bf16[512,4096]{1,0:T(8,128)(2,1)} async-done(((bf16[32,4096]{1,0:T(8,128)(2,1)}), bf16[512,4096]{1,0:T(8,128)(2,1)}) %all-gather.5.cloned.1.call-update) | async-done | bytes 4194320 | tf_op jit(solution)/shard_map/all_gather | solution.py:260
  64.0 14.6 %product.10 = (f32[512,1792]{1,0:T(8,128)}, bf16[512,1792]{1,0:T(8,128)(2,1)}) custom-call(s32[1]{0:T(128)} %bitcast.refs_0_, bf16[512,4096]{1,0:T(8,128)(2,1)} %all-gather.5.cloned.1.call-done.refs_1_, bf16[4096,1792]{1,0:T(8,128)(2,1)} %masked_weights.3.refs_0_.refs_2_, bf16[4096,1792]{1,0:T(8,128)(2,1)} %masked_weights.4.refs_3_.refs_2_.refs_4_), custom_call_target="tpu_custom_call" | custom-call | flops 3758096384 | bytes 11272192 | tf_op jit(solution)/shard_map/product/pallas_call | solution.py:119
  80.1 14.9 %product.11 = (f32[512,1792]{1,0:T(8,128)}, bf16[512,1792]{1,0:T(8,128)(2,1)}) custom-call(s32[1]{0:T(128)} %bitcast.refs_0_, bf16[512,4096]{1,0:T(8,128)(2,1)} %all-gather.5.cloned.1.call-done.refs_1_, bf16[4096,1792]{1,0:T(8,128)(2,1)} %masked_weights.4.refs_3_.refs_2_.refs_4_, f32[512,1792]{1,0:T(8,128)} %get-tuple-element.53.refs_3_.refs_0_), custom_call_target="tpu_custom_call" | custom-call | flops 3758096384 | bytes 11272192 | tf_op jit(solution)/shard_map/product/pallas_call | solution.py:119
  95.3 14.6 %masked_weights.5.refs_2_.refs_3_ = bf16[1792,4096]{1,0:T(8,128)(2,1)} custom-call(s32[14,32]{1,0:T(8,128)} %refs_0_.4, bf16[1792,4096]{1,0:T(8,128)(2,1)} %w_ref.5, f32[512,1792]{1,0:T(8,128)} %get-tuple-element.55.refs_0_.refs_2_), custom_call_target="tpu_custom_call" | custom-call | flops 3670016 | bytes 14680064 | tf_op jit(solution)/shard_map/masked_weights/pallas_call | solution.py:45
  109.9 6.0 %all-gather.9.cloned.1.call-done.refs_1_.refs_3_ = bf16[512,4096]{1,0:T(8,128)(2,1)} async-done(((bf16[32,4096]{1,0:T(8,128)(2,1)}), bf16[512,4096]{1,0:T(8,128)(2,1)}) %all-gather.9.cloned.1.call-update) | async-done | bytes 4194320 | tf_op jit(solution)/shard_map/all_gather | solution.py:260
  115.9 5.9 %collective-permute-done.refs_4_.refs_1_ = bf16[512,1792]{1,0:T(8,128)(2,1)} collective-permute-done((bf16[512,1792]{1,0:T(8,128)(2,1)}, bf16[512,1792]{1,0:T(8,128)(2,1)}, u32[]{:S(2)}, u32[]{:S(2)}) %collective-permute-start) | collective-permute-done | bytes 1835040 | tf_op jit(solution)/shard_map/ppermute | solution.py:286
  121.8 14.7 %product.12 = (f32[512,1792]{1,0:T(8,128)}, bf16[512,1792]{1,0:T(8,128)(2,1)}) custom-call(s32[1]{0:T(128)} %bitcast.refs_0_, bf16[512,4096]{1,0:T(8,128)(2,1)} %all-gather.9.cloned.1.call-done.refs_1_.refs_3_, bf16[1792,4096]{1,0:T(8,128)(2,1)} %masked_weights.5.refs_2_.refs_3_, bf16[1792,4096]{1,0:T(8,128)(2,1)} %masked_weights.5.refs_2_.refs_3_, ...), custom_call_target="tpu_custom_call" | custom-call | flops 3758096384 | bytes 11272192 | tf_op jit(solution)/shard_map/product/pallas_call | solution.py:119
  140.8 17.2 %all-gather.7.cloned.1.call-done.refs_1_.refs_2_ = bf16[256,4096]{1,0:T(8,128)(2,1)} async-done(((bf16[16,4096]{1,0:T(8,128)(2,1)}), bf16[256,4096]{1,0:T(8,128)(2,1)}) %all-gather.7.cloned.1.call-update) | async-done | bytes 2097168 | tf_op jit(solution)/shard_map/all_gather | solution.py:260
  162.3 11.4 %product.13 = (f32[256,1792]{1,0:T(8,128)}, bf16[256,1792]{1,0:T(8,128)(2,1)}) custom-call(s32[1]{0:T(128)} %bitcast.refs_0_, bf16[256,4096]{1,0:T(8,128)(2,1)} %all-gather.7.cloned.1.call-done.refs_1_.refs_2_, bf16[4096,1792]{1,0:T(8,128)(2,1)} %masked_weights.3.refs_0_.refs_2_, f32[512,1792]{1,0:T(8,128)} %get-tuple-element.57.refs_3_.refs_4_, ...), custom_call_target="tpu_custom_call" | custom-call | flops 1879048192 | bytes 9306112 | tf_op jit(solution)/shard_map/product/pallas_call | solution.py:119
  173.7 7.6 %gating.4.refs_1_.refs_3_ = bf16[512,1792]{1,0:T(8,128)(2,1)} custom-call(f32[512,1792]{1,0:T(8,128)} %get-tuple-element.53.refs_3_.refs_0_, bf16[512,1792]{1,0:T(8,128)(2,1)} %collective-permute-done.refs_4_.refs_1_, f32[512,1792]{1,0:T(8,128)} %get-tuple-element.55.refs_0_.refs_2_, bf16[512,1792]{1,0:T(8,128)(2,1)} %copy-done, ...), custom_call_target="tpu_custom_call" | custom-call | flops 9175040 | bytes 6422528 | tf_op jit(solution)/shard_map/gating/pallas_call | solution.py:202
  181.3 18.9 %all-gather.11.cloned.1.call-done.refs_4_.refs_1_ = bf16[256,4096]{1,0:T(8,128)(2,1)} async-done(((bf16[16,4096]{1,0:T(8,128)(2,1)}), bf16[256,4096]{1,0:T(8,128)(2,1)}) %all-gather.11.cloned.1.call-update) | async-done | bytes 2097168 | tf_op jit(solution)/shard_map/all_gather | solution.py:260
  201.1 14.5 %product.14 = (f32[8,32,4096]{2,1,0:T(8,128)}, bf16[8,32,4096]{2,1,0:T(8,128)(2,1)}) custom-call(s32[1]{0:T(128)} %bitcast.refs_0_, bf16[512,1792]{1,0:T(8,128)(2,1)} %gating.4.refs_1_.refs_3_, bf16[1792,4096]{1,0:T(8,128)(2,1)} %masked_weights.5.refs_2_.refs_3_, bf16[512,1792]{1,0:T(8,128)(2,1)} %gating.4.refs_1_.refs_3_, ...), custom_call_target="tpu_custom_call" | custom-call | flops 3758096384 | bytes 12451840 | tf_op jit(solution)/shard_map/product/pallas_call | solution.py:119
  218.0 11.4 %product.15 = (f32[256,1792]{1,0:T(8,128)}, bf16[256,1792]{1,0:T(8,128)(2,1)}) custom-call(s32[1]{0:T(128)} %bitcast.refs_0_, bf16[256,4096]{1,0:T(8,128)(2,1)} %all-gather.7.cloned.1.call-done.refs_1_.refs_2_, bf16[4096,1792]{1,0:T(8,128)(2,1)} %masked_weights.4.refs_3_.refs_2_.refs_4_, f32[8,32,4096]{2,1,0:T(8,128)} %get-tuple-element.60.refs_3_.mine_ref), custom_call_target="tpu_custom_call" | custom-call | flops 1879048192 | bytes 9306112 | tf_op jit(solution)/shard_map/product/pallas_call | solution.py:119
  230.6 5.0 %stage.16 = (f32[4,32,4096]{2,1,0:T(8,128)}, bf16[4,32,4096]{2,1,0:T(8,128)(2,1)}) custom-call(f32[8,32,4096]{2,1,0:T(8,128)} %get-tuple-element.60.refs_3_.mine_ref, bf16[8,32,4096]{2,1,0:T(8,128)(2,1)} %copy-done.8, f32[256,1792]{1,0:T(8,128)} %get-tuple-element.62.refs_0_.refs_2_), custom_call_target="tpu_custom_call" | custom-call | flops 524288 | bytes 4718592 | tf_op jit(solution)/shard_map/stage/pallas_call | solution.py:229
  236.1 3.3 collective-permute-done.5
  241.9 9.8 %gating.5 = (bf16[512,1792]{1,0:T(8,128)(2,1)}, bf16[512,1792]{1,0:T(8,128)(2,1)}) custom-call(f32[512,1792]{1,0:T(8,128)} %get-tuple-element.53.refs_3_.refs_0_, bf16[512,1792]{1,0:T(8,128)(2,1)} %collective-permute-done.refs_4_.refs_1_, f32[512,1792]{1,0:T(8,128)} %get-tuple-element.55.refs_0_.refs_2_, bf16[512,1792]{1,0:T(8,128)(2,1)} %copy-done, ...), custom_call_target="tpu_custom_call" | custom-call | flops 9175040 | bytes 10092544 | tf_op jit(solution)/shard_map/gating/pallas_call | solution.py:202
  251.7 6.6 %collective-permute-done.6.refs_4_.refs_1_ = bf16[256,1792]{1,0:T(8,128)(2,1)S(1)} collective-permute-done((bf16[256,1792]{1,0:T(8,128)(2,1)}, bf16[256,1792]{1,0:T(8,128)(2,1)S(1)}, u32[]{:S(2)}, u32[]{:S(2)}) %collective-permute-start.6) | collective-permute-done | bytes 917536 | tf_op jit(solution)/shard_map/ppermute | solution.py:286
  259.2 11.3 %product.16 = (f32[256,1792]{1,0:T(8,128)}, bf16[256,1792]{1,0:T(8,128)(2,1)}) custom-call(s32[1]{0:T(128)} %bitcast.refs_0_, bf16[256,4096]{1,0:T(8,128)(2,1)} %all-gather.11.cloned.1.call-done.refs_4_.refs_1_, bf16[1792,4096]{1,0:T(8,128)(2,1)} %masked_weights.5.refs_2_.refs_3_, bf16[512,1792]{1,0:T(8,128)(2,1)} %get-tuple-element.65.refs_3_.refs_1_, ...), custom_call_target="tpu_custom_call" | custom-call | flops 1879048192 | bytes 9306112 | tf_op jit(solution)/shard_map/product/pallas_call | solution.py:119
  274.4 21.9 %product.17 = (f32[8,32,4096]{2,1,0:T(8,128)}, bf16[8,32,4096]{2,1,0:T(8,128)(2,1)}) custom-call(s32[1]{0:T(128)} %bitcast.refs_0_, bf16[512,1792]{1,0:T(8,128)(2,1)} %get-tuple-element.65.refs_3_.refs_1_, bf16[4096,1792]{1,0:T(8,128)(2,1)} %masked_weights.3.refs_0_.refs_2_, bf16[512,1792]{1,0:T(8,128)(2,1)} %get-tuple-element.70.refs_3_, ...), custom_call_target="tpu_custom_call" | custom-call | flops 7516192768 | bytes 20709376 | tf_op jit(solution)/shard_map/product/pallas_call | solution.py:119
  298.9 13.2 %collective-permute-done.7.got_ref = bf16[2,32,4096]{2,1,0:T(8,128)(2,1)} collective-permute-done((bf16[2,32,4096]{2,1,0:T(8,128)(2,1)}, bf16[2,32,4096]{2,1,0:T(8,128)(2,1)}, u32[]{:S(2)}, u32[]{:S(2)}) %collective-permute-start.7) | collective-permute-done | bytes 524320 | tf_op jit(solution)/shard_map/ppermute | solution.py:267
  315.4 4.4 collective-permute-done.9.refs_3_
  320.7 5.8 %gating.6.refs_1_.refs_3_.refs_2_ = bf16[256,1792]{1,0:T(8,128)(2,1)} custom-call(f32[256,1792]{1,0:T(8,128)} %get-tuple-element.58.refs_4_.refs_0_, bf16[256,1792]{1,0:T(8,128)(2,1)} %copy-done.1, f32[256,1792]{1,0:T(8,128)} %get-tuple-element.62.refs_0_.refs_2_, bf16[256,1792]{1,0:T(8,128)(2,1)} %copy-done.2, f32[1,32,4096]{2,1,0:T(8,128)} %get-tuple-element.72.refs_4_.mine_ref), custom_call_target="tpu_custom_call" | custom-call | flops 4587520 | bytes 3211264 | tf_op jit(solution)/shard_map/gating/pallas_call | solution.py:202
  326.5 11.2 %product.18 = (f32[8,16,4096]{2,1,0:T(8,128)}, bf16[8,16,4096]{2,1,0:T(8,128)(2,1)}) custom-call(s32[1]{0:T(128)} %bitcast.refs_0_, bf16[256,1792]{1,0:T(8,128)(2,1)} %gating.6.refs_1_.refs_3_.refs_2_, bf16[1792,4096]{1,0:T(8,128)(2,1)} %masked_weights.5.refs_2_.refs_3_, bf16[256,1792]{1,0:T(8,128)(2,1)} %gating.6.refs_1_.refs_3_.refs_2_), custom_call_target="tpu_custom_call" | custom-call | flops 1879048192 | bytes 9895936 | tf_op jit(solution)/shard_map/product/pallas_call | solution.py:119
  341.0 4.9 %stage.20 = (f32[4,32,4096]{2,1,0:T(8,128)}, bf16[4,32,4096]{2,1,0:T(8,128)(2,1)}) custom-call(f32[8,32,4096]{2,1,0:T(8,128)} %get-tuple-element.71.refs_0_.mine_ref, bf16[8,32,4096]{2,1,0:T(8,128)(2,1)} %copy-done.7, bf16[1,32,4096]{2,1,0:T(8,128)(2,1)} %stage.19.refs_0_), custom_call_target="tpu_custom_call" | custom-call | flops 524288 | bytes 4718592 | tf_op jit(solution)/shard_map/stage/pallas_call | solution.py:229
  347.4 6.9 %gating.7 = (bf16[256,1792]{1,0:T(8,128)(2,1)}, bf16[256,1792]{1,0:T(8,128)(2,1)}) custom-call(f32[256,1792]{1,0:T(8,128)} %get-tuple-element.58.refs_4_.refs_0_, bf16[256,1792]{1,0:T(8,128)(2,1)} %copy-done.1, f32[256,1792]{1,0:T(8,128)} %get-tuple-element.62.refs_0_.refs_2_, bf16[256,1792]{1,0:T(8,128)(2,1)} %copy-done.2, ...), custom_call_target="tpu_custom_call" | custom-call | flops 4587520 | bytes 5046272 | tf_op jit(solution)/shard_map/gating/pallas_call | solution.py:202
  354.3 16.6 %product.19 = (f32[8,16,4096]{2,1,0:T(8,128)}, bf16[8,16,4096]{2,1,0:T(8,128)(2,1)}) custom-call(s32[1]{0:T(128)} %bitcast.refs_0_, bf16[256,1792]{1,0:T(8,128)(2,1)} %get-tuple-element.81.refs_1_.refs_5_.refs_4_, bf16[4096,1792]{1,0:T(8,128)(2,1)} %masked_weights.3.refs_0_.refs_2_, bf16[256,1792]{1,0:T(8,128)(2,1)} %get-tuple-element.82.refs_3_.refs_4_, ...), custom_call_target="tpu_custom_call" | custom-call | flops 3758096384 | bytes 17694720 | tf_op jit(solution)/shard_map/product/pallas_call | solution.py:119
  381.0 17.5 %weight_grad.3.refs_0_ = bf16[1792,4096]{1,0:T(8,128)(2,1)} custom-call(s32[14,32]{1,0:T(8,128)} %refs_0_.4, bf16[512,1792]{1,0:T(8,128)(2,1)} %gating.4.refs_1_.refs_3_, bf16[256,1792]{1,0:T(8,128)(2,1)} %gating.6.refs_1_.refs_3_.refs_2_, bf16[512,4096]{1,0:T(8,128)(2,1)} %all-gather.9.cloned.1.call-done.refs_1_.refs_3_, ...), custom_call_target="tpu_custom_call" | custom-call | flops 5637144576 | bytes 11862016 | tf_op jit(solution)/shard_map/weight_grad/pallas_call | solution.py:160
  411.2 16.7 %weight_grad.4.refs_0_ = bf16[4096,1792]{1,0:T(8,128)(2,1)} custom-call(s32[32,14]{1,0:T(8,128)} %copy.13.mask_ref.refs_0_, bf16[512,4096]{1,0:T(8,128)(2,1)} %all-gather.5.cloned.1.call-done.refs_1_, bf16[256,4096]{1,0:T(8,128)(2,1)} %all-gather.7.cloned.1.call-done.refs_1_.refs_2_, bf16[512,1792]{1,0:T(8,128)(2,1)} %get-tuple-element.65.refs_3_.refs_1_, ...), custom_call_target="tpu_custom_call" | custom-call | flops 5637144576 | bytes 11862016 | tf_op jit(solution)/shard_map/weight_grad/pallas_call | solution.py:160
  438.9 16.7 %weight_grad.5.refs_0_ = bf16[4096,1792]{1,0:T(8,128)(2,1)} custom-call(s32[32,14]{1,0:T(8,128)} %copy.15.mask_ref.refs_0_, bf16[512,4096]{1,0:T(8,128)(2,1)} %all-gather.5.cloned.1.call-done.refs_1_, bf16[256,4096]{1,0:T(8,128)(2,1)} %all-gather.7.cloned.1.call-done.refs_1_.refs_2_, bf16[512,1792]{1,0:T(8,128)(2,1)} %get-tuple-element.70.refs_3_, ...), custom_call_target="tpu_custom_call" | custom-call | flops 5637144576 | bytes 11862016 | tf_op jit(solution)/shard_map/weight_grad/pallas_call | solution.py:160
  464.4 3.7 collective-permute-done.22.got_ref
  (124 shorter events, 88.6 us)
Async XLA Ops:
  7.2 6.9 %copy-start.22 = (s32[32,14]{0,1:T(8,128)S(1)}, s32[32,14]{0,1:T(8,128)}, u32[]{:S(2)}) copy-start(s32[32,14]{0,1:T(8,128)} %param.12) | copy-start | bytes 5380
  7.2 7.5 %copy-start.23 = (s32[32,14]{0,1:T(8,128)S(1)}, s32[32,14]{0,1:T(8,128)}, u32[]{:S(2)}) copy-start(s32[32,14]{0,1:T(8,128)} %param.13) | copy-start | bytes 5380
  7.2 56.9 %all-gather.5.cloned.1.call-start = ((), (), s32[]{:S(2)}) async-start(), calls=%async_computation | async-start | bytes 4456448 | tf_op jit(solution)/shard_map/all_gather | solution.py:260
  8.9 106.9 %all-gather.9.cloned.1.call-start = ((), (), s32[]{:S(2)}) async-start(), calls=%async_computation.2 | async-start | bytes 4456448 | tf_op jit(solution)/shard_map/all_gather | solution.py:260
  10.7 147.3 %all-gather.7.cloned.1.call-start = ((), (), s32[]{:S(2)}) async-start(), calls=%async_computation.1 | async-start | bytes 2228224 | tf_op jit(solution)/shard_map/all_gather | solution.py:260
  12.3 187.9 %all-gather.11.cloned.1.call-start = ((), (), s32[]{:S(2)}) async-start(), calls=%async_computation.3 | async-start | bytes 2228224 | tf_op jit(solution)/shard_map/all_gather | solution.py:260
  78.6 43.2 %collective-permute-start = (bf16[512,1792]{1,0:T(8,128)(2,1)}, bf16[512,1792]{1,0:T(8,128)(2,1)}, u32[]{:S(2)}, u32[]{:S(2)}) collective-permute-start(bf16[512,1792]{1,0:T(8,128)(2,1)} %get-tuple-element.54), channel_id=1, source_target_pairs={{0,16},{16,0},{1,17},{17,1},{2,18},{18,2},{3,19},{19,3},{4,20},{20... | collective-permute-start | bytes 5505032 | tf_op jit(solution)/shard_map/ppermute | solution.py:286
  95.0 66.0 %collective-permute-start.1 = (bf16[512,1792]{1,0:T(8,128)(2,1)}, bf16[512,1792]{1,0:T(8,128)(2,1)S(1)}, u32[]{:S(2)}, u32[]{:S(2)}) collective-permute-start(bf16[512,1792]{1,0:T(8,128)(2,1)} %get-tuple-element.56), channel_id=1, source_target_pairs={{0,16},{16,0},{1,17},{17,1},{2,18},{18,2},{3,19},{19,3},{4,20},{20... | collective-permute-start | bytes 5505032 | tf_op jit(solution)/shard_map/ppermute | solution.py:286
  139.3 60.8 %collective-permute-start.2 = (bf16[256,1792]{1,0:T(8,128)(2,1)}, bf16[256,1792]{1,0:T(8,128)(2,1)S(1)}, u32[]{:S(2)}, u32[]{:S(2)}) collective-permute-start(bf16[256,1792]{1,0:T(8,128)(2,1)} %get-tuple-element.102), channel_id=1, source_target_pairs={{0,16},{16,0},{1,17},{17,1},{2,18},{18,2},{3,19},{19,3},{4,20},{20... | collective-permute-start | bytes 2752520 | tf_op jit(solution)/shard_map/ppermute | solution.py:286
  215.7 13.6 %collective-permute-start.3 = (bf16[8,32,4096]{2,1,0:T(8,128)(2,1)}, bf16[8,32,4096]{2,1,0:T(8,128)(2,1)S(1)}, u32[]{:S(2)}, u32[]{:S(2)}) collective-permute-start(bf16[8,32,4096]{2,1,0:T(8,128)(2,1)} %get-tuple-element.61), channel_id=1, source_target_pairs={{0,1},{1,0},{2,3},{3,2},{4,5},{5,4},{6,7},{7,6},{8,9},{9,8},{10,11... | collective-permute-start | bytes 6291464 | tf_op jit(solution)/shard_map/ppermute | solution.py:267
  215.9 23.5 %collective-permute-start.5 = (bf16[256,1792]{1,0:T(8,128)(2,1)}, bf16[256,1792]{1,0:T(8,128)(2,1)}, u32[]{:S(2)}, u32[]{:S(2)}) collective-permute-start(bf16[256,1792]{1,0:T(8,128)(2,1)} %get-tuple-element.101), channel_id=1, source_target_pairs={{0,16},{16,0},{1,17},{17,1},{2,18},{18,2},{3,19},{19,3},{4,20},{20... | collective-permute-start | bytes 2752520 | tf_op jit(solution)/shard_map/ppermute | solution.py:286
  217.4 40.9 %collective-permute-start.6 = (bf16[256,1792]{1,0:T(8,128)(2,1)}, bf16[256,1792]{1,0:T(8,128)(2,1)S(1)}, u32[]{:S(2)}, u32[]{:S(2)}) collective-permute-start(bf16[256,1792]{1,0:T(8,128)(2,1)} %get-tuple-element.66), channel_id=1, source_target_pairs={{0,16},{16,0},{1,17},{17,1},{2,18},{18,2},{3,19},{19,3},{4,20},{20... | collective-permute-start | bytes 2752520 | tf_op jit(solution)/shard_map/ppermute | solution.py:286
  230.6 8.8 %copy-start.4 = (bf16[256,1792]{1,0:T(8,128)(2,1)S(1)}, bf16[256,1792]{1,0:T(8,128)(2,1)}, u32[]{:S(2)}) copy-start(bf16[256,1792]{1,0:T(8,128)(2,1)} %copy-done.3) | copy-start | bytes 2752516
  235.6 35.0 %collective-permute-start.4 = (bf16[4,32,4096]{2,1,0:T(8,128)(2,1)}, bf16[4,32,4096]{2,1,0:T(8,128)(2,1)S(1)}, u32[]{:S(2)}, u32[]{:S(2)}) collective-permute-start(bf16[4,32,4096]{2,1,0:T(8,128)(2,1)} %get-tuple-element.64), channel_id=1, source_target_pairs={{0,2},{1,3},{2,0},{3,1},{4,6},{5,7},{6,4},{7,5},{8,10},{9,11},{10,... | collective-permute-start | bytes 3145736 | tf_op jit(solution)/shard_map/ppermute | solution.py:267
  296.3 43.3 %collective-permute-start.11 = (bf16[8,32,4096]{2,1,0:T(8,128)(2,1)}, bf16[8,32,4096]{2,1,0:T(8,128)(2,1)S(1)}, u32[]{:S(2)}, u32[]{:S(2)}) collective-permute-start(bf16[8,32,4096]{2,1,0:T(8,128)(2,1)} %get-tuple-element.77), channel_id=1, source_target_pairs={{0,1},{1,0},{2,3},{3,2},{4,5},{5,4},{6,7},{7,6},{8,9},{9,8},{10,11... | collective-permute-start | bytes 6291464 | tf_op jit(solution)/shard_map/ppermute | solution.py:267
  296.3 23.4 %collective-permute-start.9 = (bf16[256,1792]{1,0:T(8,128)(2,1)}, bf16[256,1792]{1,0:T(8,128)(2,1)S(1)}, u32[]{:S(2)}, u32[]{:S(2)}) collective-permute-start(bf16[256,1792]{1,0:T(8,128)(2,1)} %get-tuple-element.74), channel_id=1, source_target_pairs={{0,16},{16,0},{1,17},{17,1},{2,18},{18,2},{3,19},{19,3},{4,20},{20... | collective-permute-start | bytes 2752520 | tf_op jit(solution)/shard_map/ppermute | solution.py:286
  297.9 14.3 %collective-permute-start.7 = (bf16[2,32,4096]{2,1,0:T(8,128)(2,1)}, bf16[2,32,4096]{2,1,0:T(8,128)(2,1)}, u32[]{:S(2)}, u32[]{:S(2)}) collective-permute-start(bf16[2,32,4096]{2,1,0:T(8,128)(2,1)} %get-tuple-element.69), channel_id=1, source_target_pairs={{0,4},{1,5},{2,6},{3,7},{4,0},{5,1},{6,2},{7,3},{8,12},{9,13},{10,... | collective-permute-start | bytes 1572872 | tf_op jit(solution)/shard_map/ppermute | solution.py:267
  298.4 48.1 %collective-permute-start.13 = (bf16[256,1792]{1,0:T(8,128)(2,1)}, bf16[256,1792]{1,0:T(8,128)(2,1)S(1)}, u32[]{:S(2)}, u32[]{:S(2)}) collective-permute-start(bf16[256,1792]{1,0:T(8,128)(2,1)} %get-tuple-element.80), channel_id=1, source_target_pairs={{0,16},{16,0},{1,17},{17,1},{2,18},{18,2},{3,19},{19,3},{4,20},{20... | collective-permute-start | bytes 2752520 | tf_op jit(solution)/shard_map/ppermute | solution.py:286
  314.4 23.3 %collective-permute-start.8 = (bf16[1,32,4096]{2,1,0:T(8,128)(2,1)}, bf16[1,32,4096]{2,1,0:T(8,128)(2,1)}, u32[]{:S(2)}, u32[]{:S(2)}) collective-permute-start(bf16[1,32,4096]{2,1,0:T(8,128)(2,1)} %get-tuple-element.73), channel_id=1, source_target_pairs={{0,8},{1,9},{2,10},{3,11},{4,12},{5,13},{6,14},{7,15},{8,0},{9,1},... | collective-permute-start | bytes 786440 | tf_op jit(solution)/shard_map/ppermute | solution.py:267
  345.9 25.5 %collective-permute-start.12 = (bf16[4,32,4096]{2,1,0:T(8,128)(2,1)}, bf16[4,32,4096]{2,1,0:T(8,128)(2,1)S(1)}, u32[]{:S(2)}, u32[]{:S(2)}) collective-permute-start(bf16[4,32,4096]{2,1,0:T(8,128)(2,1)} %get-tuple-element.79), channel_id=1, source_target_pairs={{0,2},{1,3},{2,0},{3,1},{4,6},{5,7},{6,4},{7,5},{8,10},{9,11},{10,... | collective-permute-start | bytes 3145736 | tf_op jit(solution)/shard_map/ppermute | solution.py:267
  346.5 28.7 %collective-permute-start.10 = (bf16[8,16,4096]{2,1,0:T(8,128)(2,1)}, bf16[8,16,4096]{2,1,0:T(8,128)(2,1)S(1)}, u32[]{:S(2)}, u32[]{:S(2)}) collective-permute-start(bf16[8,16,4096]{2,1,0:T(8,128)(2,1)} %get-tuple-element.76), channel_id=1, source_target_pairs={{0,1},{1,0},{2,3},{3,2},{4,5},{5,4},{6,7},{7,6},{8,9},{9,8},{10,11... | collective-permute-start | bytes 3145736 | tf_op jit(solution)/shard_map/ppermute | solution.py:267
  370.9 35.9 %collective-permute-start.18 = (bf16[8,16,4096]{2,1,0:T(8,128)(2,1)}, bf16[8,16,4096]{2,1,0:T(8,128)(2,1)S(1)}, u32[]{:S(2)}, u32[]{:S(2)}) collective-permute-start(bf16[8,16,4096]{2,1,0:T(8,128)(2,1)} %get-tuple-element.92), channel_id=1, source_target_pairs={{0,1},{1,0},{2,3},{3,2},{4,5},{5,4},{6,7},{7,6},{8,9},{9,8},{10,11... | collective-permute-start | bytes 3145736 | tf_op jit(solution)/shard_map/ppermute | solution.py:267
  379.0 22.5 %collective-permute-start.14 = (bf16[4,16,4096]{2,1,0:T(8,128)(2,1)}, bf16[4,16,4096]{2,1,0:T(8,128)(2,1)S(1)}, u32[]{:S(2)}, u32[]{:S(2)}) collective-permute-start(bf16[4,16,4096]{2,1,0:T(8,128)(2,1)} %get-tuple-element.86), channel_id=1, source_target_pairs={{0,2},{1,3},{2,0},{3,1},{4,6},{5,7},{6,4},{7,5},{8,10},{9,11},{10,... | collective-permute-start | bytes 1572872 | tf_op jit(solution)/shard_map/ppermute | solution.py:267
  380.5 18.0 %collective-permute-start.15 = (bf16[2,32,4096]{2,1,0:T(8,128)(2,1)S(1)}, bf16[2,32,4096]{2,1,0:T(8,128)(2,1)S(1)}, u32[]{:S(2)}, u32[]{:S(2)}) collective-permute-start(bf16[2,32,4096]{2,1,0:T(8,128)(2,1)S(1)} %copy-done.24), channel_id=1, source_target_pairs={{0,4},{1,5},{2,6},{3,7},{4,0},{5,1},{6,2},{7,3},{8,12},{9,13},{10,... | collective-permute-start | bytes 1572872 | tf_op jit(solution)/shard_map/ppermute | solution.py:267
  404.7 25.8 %collective-permute-start.16 = (bf16[2,16,4096]{2,1,0:T(8,128)(2,1)}, bf16[2,16,4096]{2,1,0:T(8,128)(2,1)S(1)}, u32[]{:S(2)}, u32[]{:S(2)}) collective-permute-start(bf16[2,16,4096]{2,1,0:T(8,128)(2,1)} %get-tuple-element.90), channel_id=1, source_target_pairs={{0,4},{1,5},{2,6},{3,7},{4,0},{5,1},{6,2},{7,3},{8,12},{9,13},{10,... | collective-permute-start | bytes 786440 | tf_op jit(solution)/shard_map/ppermute | solution.py:267
  406.2 21.8 %collective-permute-start.17 = (bf16[1,32,4096]{2,1,0:T(8,128)(2,1)S(1)}, bf16[1,32,4096]{2,1,0:T(8,128)(2,1)S(1)}, u32[]{:S(2)}, u32[]{:S(2)}) collective-permute-start(bf16[1,32,4096]{2,1,0:T(8,128)(2,1)S(1)} %copy-done.25), channel_id=1, source_target_pairs={{0,8},{1,9},{2,10},{3,11},{4,12},{5,13},{6,14},{7,15},{8,0},{9,1},... | collective-permute-start | bytes 786440 | tf_op jit(solution)/shard_map/ppermute | solution.py:267
  410.6 24.7 %collective-permute-start.20 = (bf16[4,16,4096]{2,1,0:T(8,128)(2,1)}, bf16[4,16,4096]{2,1,0:T(8,128)(2,1)S(1)}, u32[]{:S(2)}, u32[]{:S(2)}) collective-permute-start(bf16[4,16,4096]{2,1,0:T(8,128)(2,1)} %get-tuple-element.96), channel_id=1, source_target_pairs={{0,2},{1,3},{2,0},{3,1},{4,6},{5,7},{6,4},{7,5},{8,10},{9,11},{10,... | collective-permute-start | bytes 1572872 | tf_op jit(solution)/shard_map/ppermute | solution.py:267
  433.1 22.6 %collective-permute-start.19 = (bf16[1,16,4096]{2,1,0:T(8,128)(2,1)}, bf16[1,16,4096]{2,1,0:T(8,128)(2,1)S(1)}, u32[]{:S(2)}, u32[]{:S(2)}) collective-permute-start(bf16[1,16,4096]{2,1,0:T(8,128)(2,1)} %get-tuple-element.95), channel_id=1, source_target_pairs={{0,8},{1,9},{2,10},{3,11},{4,12},{5,13},{6,14},{7,15},{8,0},{9,1},... | collective-permute-start | bytes 393224 | tf_op jit(solution)/shard_map/ppermute | solution.py:267
  438.4 19.6 %collective-permute-start.21 = (bf16[2,16,4096]{2,1,0:T(8,128)(2,1)}, bf16[2,16,4096]{2,1,0:T(8,128)(2,1)S(1)}, u32[]{:S(2)}, u32[]{:S(2)}) collective-permute-start(bf16[2,16,4096]{2,1,0:T(8,128)(2,1)} %get-tuple-element.98), channel_id=1, source_target_pairs={{0,4},{1,5},{2,6},{3,7},{4,0},{5,1},{6,2},{7,3},{8,12},{9,13},{10,... | collective-permute-start | bytes 786440 | tf_op jit(solution)/shard_map/ppermute | solution.py:267
  455.7 7.1 %copy-start.6 = (bf16[1,32,4096]{2,1,0:T(8,128)(2,1)S(1)}, bf16[1,32,4096]{2,1,0:T(8,128)(2,1)}, u32[]{:S(2)}) copy-start(bf16[1,32,4096]{2,1,0:T(8,128)(2,1)} %stage.19.refs_0_) | copy-start | bytes 786436
  458.0 12.4 %copy-start.5 = (bf16[1,32,4096]{2,1,0:T(8,128)(2,1)S(1)}, bf16[1,32,4096]{2,1,0:T(8,128)(2,1)}, u32[]{:S(2)}) copy-start(bf16[1,32,4096]{2,1,0:T(8,128)(2,1)} %stage.26.refs_0_) | copy-start | bytes 786436
  460.6 7.5 %collective-permute-start.22 = (bf16[1,16,4096]{2,1,0:T(8,128)(2,1)}, bf16[1,16,4096]{2,1,0:T(8,128)(2,1)S(1)}, u32[]{:S(2)}, u32[]{:S(2)}) collective-permute-start(bf16[1,16,4096]{2,1,0:T(8,128)(2,1)} %get-tuple-element.100), channel_id=1, source_target_pairs={{0,8},{1,9},{2,10},{3,11},{4,12},{5,13},{6,14},{7,15},{8,0},{9,1},... | collective-permute-start | bytes 393224 | tf_op jit(solution)/shard_map/ppermute | solution.py:267
  (21 other events, 26.3 us)
Sparse Core Ops, SparseCore 0:
  10.8 53.2 all-gather.4
  66.8 49.0 all-gather.8
  118.0 39.8 all-gather.6
  160.0 40.1 all-gather.10

commit v4 on v3

--- a/solution.py
+++ b/solution.py
@@ -306,12 +306,13 @@
             advance()
             start(name, sums)
 
-        def back_tokens(name, dgate, dup):
+        def back_tokens(name, dgate, dup, onward):
             dgates.append(dgate)
             dups.append(dup)
             terms = [(dgate, gate_w), (dup, up_w)]
             sums = run(product, 1, place, spread, terms, 512)
-            advance()
+            if onward:
+                advance()
             start(name, sums)
 
         def make_hidden(c, wait):
@@ -331,18 +332,18 @@
         dhs.append(dh)
         gates.append(exchange(*run(product, 0, place, 0, [(toks[SECOND], gate_w)], 256, late=arrived[1])))
         make_hidden(FIRST, [])
-        back_out("out", [cots[SECOND], *first_half])
-        ups.append(exchange(*run(product, 0, place, 0, [(toks[SECOND], up_w)], 256)))
+        back_out("out", first_half)
+        ups.append(exchange(*run(product, 0, place, 0, [(toks[SECOND], up_w)], 256, late=[cots[SECOND]])))
         advance()
         dgrads = run(gating, grads_kernel, [gates[FIRST], ups[FIRST], dhs[FIRST]], 2)
         sums = run(product, 1, place, 0, [(cots[SECOND], down_w)], 256, late=gates[SECOND][1:])
         dhs.append(exchange(*sums))
         advance()
-        back_tokens("tokens", *dgrads)
+        back_tokens("tokens", *dgrads, False)
         make_hidden(SECOND, [])
         back_out("out last", [])
         dgrads = run(gating, grads_kernel, [gates[SECOND], ups[SECOND], dhs[SECOND]], 2)
-        back_tokens("tokens last", *dgrads)
+        back_tokens("tokens last", *dgrads, True)
         grad_down = run(tn, hiddens, cots, mask_down, 256)
         advance()
         grad_gate = run(tn, toks, dgates, mask_gate, 512)

time: 482 us -> 479 us (level)
  waiting for transfers between devices: 108 us -> 103 us
    all_gather x4, waiting for transfers between devices: 68 us -> 52.1 us  [gather(): lax.all_gather(x[parts[c][0]:parts[c][1]], 'tensor', axis=0, tiled=True)]
    ppermute x7, waiting for transfers between devices: 23.2 us -> 36 us  [exchange(): got = [lax.ppermute(sent, 'seq', shift) for shift in shifts]]
    unnamed x54 -> x58, local copies, waits for them, and re-layouts: 18.7 us -> 19.4 us
  transfers between devices with their start and end apart: 27 -> 27, of which waited for: 11 -> 11; matrix products, arithmetic and copies ran while one was open for 3% -> 3% of each run, Pallas kernels for 54% -> 58%
where the time goes in v4:
time: 479 us; the launch traced here: 476 us
  Pallas kernels  302 us (63%)
  waiting for transfers between devices  103 us (22%)
  local copies, waits for them, and re-layouts  28.7 us (6%)
  starting transfers between devices  22 us (5%)
  between operations  14 us (3%)
  other arithmetic  5.89 us (1%)
    pallas_call x10, Pallas kernels, product(): pl.pallas_call(lambda *refs: product_kernel(n, contract, len(scratch), *r...  142 us
    all_gather x4, waiting for transfers between devices, gather(): lax.all_gather(x[parts[c][0]:parts[c][1]], 'tensor', axis=0, tiled=True)  52.1 us
    pallas_call x3, Pallas kernels, tn(): pl.pallas_call(lambda *refs: tn_kernel(chunks, *refs), grid=(height // ti...  51 us
    pallas_call x16, Pallas kernels, stage(): pl.pallas_call(stage_kernel, grid=(width // tile,), in_specs=[block(count...  41 us
    pallas_call x3, Pallas kernels, masked(): pl.pallas_call(mask_kernel, grid=(w.shape[0] // tall,), in_specs=[SMEM, b...  37.3 us
    ppermute x7, waiting for transfers between devices, exchange(): got = [lax.ppermute(sent, 'seq', shift) for shift in shifts]  36 us
    pallas_call x4, Pallas kernels, gating(): pl.pallas_call(lambda *refs: kernel(len(sums[0]), *refs), grid=(width //...  30.2 us
    unnamed x58, local copies, waits for them, and re-layouts  19.4 us
  transfers between devices with their start and end apart: 27, of which 11 were waited for; matrix products, arithmetic and copies ran while one was open for 3% of the time, Pallas kernels for 58%

profile of v4, /device:TPU:0, one launch (start us, length us, event | category | flops | bytes accessed | tf_op | source)
XLA Modules:
  0.0 475.6 jit_solution(2696001896229420508)
XLA Ops:
  13.8 11.3 %masked_weights.3.refs_0_.refs_2_ = bf16[4096,1792]{1,0:T(8,128)(2,1)} custom-call(s32[32,14]{1,0:T(8,128)} %copy.13.mask_ref.refs_0_, bf16[4096,1792]{1,0:T(8,128)(2,1)} %w_ref.3, s32[32,14]{1,0:T(8,128)} %copy.13.mask_ref.refs_0_), custom_call_target="tpu_custom_call" | custom-call | flops 3670016 | bytes 14680064 | tf_op jit(solution)/shard_map/masked_weights/pallas_call | solution.py:45
  25.2 11.3 %masked_weights.4.refs_3_.refs_2_.refs_4_ = bf16[4096,1792]{1,0:T(8,128)(2,1)} custom-call(s32[32,14]{1,0:T(8,128)} %copy.15.mask_ref.refs_0_, bf16[4096,1792]{1,0:T(8,128)(2,1)} %w_ref.4, bf16[4096,1792]{1,0:T(8,128)(2,1)} %masked_weights.3.refs_0_.refs_2_), custom_call_target="tpu_custom_call" | custom-call | flops 3670016 | bytes 14680064 | tf_op jit(solution)/shard_map/masked_weights/pallas_call | solution.py:45
  36.5 27.5 %all-gather.5.cloned.1.call-done.refs_1_ = bf16[512,4096]{1,0:T(8,128)(2,1)} async-done(((bf16[32,4096]{1,0:T(8,128)(2,1)}), bf16[512,4096]{1,0:T(8,128)(2,1)}) %all-gather.5.cloned.1.call-update) | async-done | bytes 4194320 | tf_op jit(solution)/shard_map/all_gather | solution.py:260
  64.0 14.6 %product.10 = (f32[512,1792]{1,0:T(8,128)}, bf16[512,1792]{1,0:T(8,128)(2,1)}) custom-call(s32[1]{0:T(128)} %bitcast.refs_0_, bf16[512,4096]{1,0:T(8,128)(2,1)} %all-gather.5.cloned.1.call-done.refs_1_, bf16[4096,1792]{1,0:T(8,128)(2,1)} %masked_weights.3.refs_0_.refs_2_, bf16[4096,1792]{1,0:T(8,128)(2,1)} %masked_weights.4.refs_3_.refs_2_.refs_4_), custom_call_target="tpu_custom_call" | custom-call | flops 3758096384 | bytes 11272192 | tf_op jit(solution)/shard_map/product/pallas_call | solution.py:119
  80.1 14.7 %product.11 = (f32[512,1792]{1,0:T(8,128)}, bf16[512,1792]{1,0:T(8,128)(2,1)}) custom-call(s32[1]{0:T(128)} %bitcast.refs_0_, bf16[512,4096]{1,0:T(8,128)(2,1)} %all-gather.5.cloned.1.call-done.refs_1_, bf16[4096,1792]{1,0:T(8,128)(2,1)} %masked_weights.4.refs_3_.refs_2_.refs_4_, f32[512,1792]{1,0:T(8,128)} %get-tuple-element.53.refs_3_.refs_0_), custom_call_target="tpu_custom_call" | custom-call | flops 3758096384 | bytes 11272192 | tf_op jit(solution)/shard_map/product/pallas_call | solution.py:119
  96.8 14.6 %masked_weights.5.refs_2_.refs_3_ = bf16[1792,4096]{1,0:T(8,128)(2,1)} custom-call(s32[14,32]{1,0:T(8,128)} %refs_0_.4, bf16[1792,4096]{1,0:T(8,128)(2,1)} %w_ref.5, f32[512,1792]{1,0:T(8,128)} %get-tuple-element.55.refs_0_.refs_2_), custom_call_target="tpu_custom_call" | custom-call | flops 3670016 | bytes 14680064 | tf_op jit(solution)/shard_map/masked_weights/pallas_call | solution.py:45
  111.4 4.6 all-gather.9.cloned.1.call-done.refs_1_.refs_3_
  116.0 5.8 %collective-permute-done.refs_4_.refs_1_ = bf16[512,1792]{1,0:T(8,128)(2,1)} collective-permute-done((bf16[512,1792]{1,0:T(8,128)(2,1)}, bf16[512,1792]{1,0:T(8,128)(2,1)}, u32[]{:S(2)}, u32[]{:S(2)}) %collective-permute-start) | collective-permute-done | bytes 1835040 | tf_op jit(solution)/shard_map/ppermute | solution.py:286
  121.8 14.7 %product.12 = (f32[512,1792]{1,0:T(8,128)}, bf16[512,1792]{1,0:T(8,128)(2,1)}) custom-call(s32[1]{0:T(128)} %bitcast.refs_0_, bf16[512,4096]{1,0:T(8,128)(2,1)} %all-gather.9.cloned.1.call-done.refs_1_.refs_3_, bf16[1792,4096]{1,0:T(8,128)(2,1)} %masked_weights.5.refs_2_.refs_3_, bf16[1792,4096]{1,0:T(8,128)(2,1)} %masked_weights.5.refs_2_.refs_3_, ...), custom_call_target="tpu_custom_call" | custom-call | flops 3758096384 | bytes 11272192 | tf_op jit(solution)/shard_map/product/pallas_call | solution.py:119
  136.5 2.8 fusion
  140.8 17.4 %all-gather.7.cloned.1.call-done.refs_1_.refs_2_ = bf16[256,4096]{1,0:T(8,128)(2,1)} async-done(((bf16[16,4096]{1,0:T(8,128)(2,1)}), bf16[256,4096]{1,0:T(8,128)(2,1)}) %all-gather.7.cloned.1.call-update) | async-done | bytes 2097168 | tf_op jit(solution)/shard_map/all_gather | solution.py:260
  158.1 2.9 collective-permute-done.1.refs_4_.refs_3_
  162.3 11.4 %product.13 = (f32[256,1792]{1,0:T(8,128)}, bf16[256,1792]{1,0:T(8,128)(2,1)}) custom-call(s32[1]{0:T(128)} %bitcast.refs_0_, bf16[256,4096]{1,0:T(8,128)(2,1)} %all-gather.7.cloned.1.call-done.refs_1_.refs_2_, bf16[4096,1792]{1,0:T(8,128)(2,1)} %masked_weights.3.refs_0_.refs_2_, f32[512,1792]{1,0:T(8,128)} %get-tuple-element.57.refs_3_.refs_4_, ...), custom_call_target="tpu_custom_call" | custom-call | flops 1879048192 | bytes 9306112 | tf_op jit(solution)/shard_map/product/pallas_call | solution.py:119
  173.7 7.6 %gating.4.refs_1_.refs_3_ = bf16[512,1792]{1,0:T(8,128)(2,1)} custom-call(f32[512,1792]{1,0:T(8,128)} %get-tuple-element.53.refs_3_.refs_0_, bf16[512,1792]{1,0:T(8,128)(2,1)} %collective-permute-done.refs_4_.refs_1_, f32[512,1792]{1,0:T(8,128)} %get-tuple-element.55.refs_0_.refs_2_, bf16[512,1792]{1,0:T(8,128)(2,1)} %copy-done, ...), custom_call_target="tpu_custom_call" | custom-call | flops 9175040 | bytes 6422528 | tf_op jit(solution)/shard_map/gating/pallas_call | solution.py:202
  182.3 14.6 %product.14 = (f32[8,32,4096]{2,1,0:T(8,128)}, bf16[8,32,4096]{2,1,0:T(8,128)(2,1)}) custom-call(s32[1]{0:T(128)} %bitcast.refs_0_, bf16[512,1792]{1,0:T(8,128)(2,1)} %gating.4.refs_1_.refs_3_, bf16[1792,4096]{1,0:T(8,128)(2,1)} %masked_weights.5.refs_2_.refs_3_, bf16[512,1792]{1,0:T(8,128)(2,1)} %gating.4.refs_1_.refs_3_, bf16[256,1792]{1,0:T(8,128)(2,1)} %copy-done.3), custom_call_target="tpu_custom_call" | custom-call | flops 3758096384 | bytes 12451840 | tf_op jit(solution)/shard_map/product/pallas_call | solution.py:119
  201.4 11.4 %product.15 = (f32[256,1792]{1,0:T(8,128)}, bf16[256,1792]{1,0:T(8,128)(2,1)}) custom-call(s32[1]{0:T(128)} %bitcast.refs_0_, bf16[256,4096]{1,0:T(8,128)(2,1)} %all-gather.7.cloned.1.call-done.refs_1_.refs_2_, bf16[4096,1792]{1,0:T(8,128)(2,1)} %masked_weights.4.refs_3_.refs_2_.refs_4_, f32[8,32,4096]{2,1,0:T(8,128)} %get-tuple-element.60.refs_3_.mine_ref, ...), custom_call_target="tpu_custom_call" | custom-call | flops 1879048192 | bytes 9306112 | tf_op jit(solution)/shard_map/product/pallas_call | solution.py:119
  214.1 4.9 %stage.16 = (f32[4,32,4096]{2,1,0:T(8,128)}, bf16[4,32,4096]{2,1,0:T(8,128)(2,1)}) custom-call(f32[8,32,4096]{2,1,0:T(8,128)} %get-tuple-element.60.refs_3_.mine_ref, bf16[8,32,4096]{2,1,0:T(8,128)(2,1)} %copy-done.8, f32[256,1792]{1,0:T(8,128)} %get-tuple-element.62.refs_0_.refs_2_), custom_call_target="tpu_custom_call" | custom-call | flops 524288 | bytes 4718592 | tf_op jit(solution)/shard_map/stage/pallas_call | solution.py:229
  222.8 9.8 %gating.5 = (bf16[512,1792]{1,0:T(8,128)(2,1)}, bf16[512,1792]{1,0:T(8,128)(2,1)}) custom-call(f32[512,1792]{1,0:T(8,128)} %get-tuple-element.53.refs_3_.refs_0_, bf16[512,1792]{1,0:T(8,128)(2,1)} %collective-permute-done.refs_4_.refs_1_, f32[512,1792]{1,0:T(8,128)} %get-tuple-element.55.refs_0_.refs_2_, bf16[512,1792]{1,0:T(8,128)(2,1)} %copy-done, ...), custom_call_target="tpu_custom_call" | custom-call | flops 9175040 | bytes 10092544 | tf_op jit(solution)/shard_map/gating/pallas_call | solution.py:202
  232.7 6.8 %collective-permute-done.6.refs_4_.refs_1_ = bf16[256,1792]{1,0:T(8,128)(2,1)S(1)} collective-permute-done((bf16[256,1792]{1,0:T(8,128)(2,1)}, bf16[256,1792]{1,0:T(8,128)(2,1)S(1)}, u32[]{:S(2)}, u32[]{:S(2)}) %collective-permute-start.6) | collective-permute-done | bytes 917536 | tf_op jit(solution)/shard_map/ppermute | solution.py:286
  240.4 11.3 %product.16 = (f32[256,1792]{1,0:T(8,128)}, bf16[256,1792]{1,0:T(8,128)(2,1)}) custom-call(s32[1]{0:T(128)} %bitcast.refs_0_, bf16[256,4096]{1,0:T(8,128)(2,1)} %all-gather.11.cloned.1.call-done.refs_4_.refs_1_, bf16[1792,4096]{1,0:T(8,128)(2,1)} %masked_weights.5.refs_2_.refs_3_, bf16[512,1792]{1,0:T(8,128)(2,1)} %get-tuple-element.65.refs_3_.refs_1_, ...), custom_call_target="tpu_custom_call" | custom-call | flops 1879048192 | bytes 9306112 | tf_op jit(solution)/shard_map/product/pallas_call | solution.py:119
  255.5 21.9 %product.17 = (f32[8,32,4096]{2,1,0:T(8,128)}, bf16[8,32,4096]{2,1,0:T(8,128)(2,1)}) custom-call(s32[1]{0:T(128)} %bitcast.refs_0_, bf16[512,1792]{1,0:T(8,128)(2,1)} %get-tuple-element.65.refs_3_.refs_1_, bf16[4096,1792]{1,0:T(8,128)(2,1)} %masked_weights.3.refs_0_.refs_2_, bf16[512,1792]{1,0:T(8,128)(2,1)} %get-tuple-element.71.refs_3_, ...), custom_call_target="tpu_custom_call" | custom-call | flops 7516192768 | bytes 20709376 | tf_op jit(solution)/shard_map/product/pallas_call | solution.py:119
  281.0 19.9 %collective-permute-done.8.refs_3_ = bf16[256,1792]{1,0:T(8,128)(2,1)S(1)} collective-permute-done((bf16[256,1792]{1,0:T(8,128)(2,1)}, bf16[256,1792]{1,0:T(8,128)(2,1)S(1)}, u32[]{:S(2)}, u32[]{:S(2)}) %collective-permute-start.8) | collective-permute-done | bytes 917536 | tf_op jit(solution)/shard_map/ppermute | solution.py:286
  301.8 5.8 %gating.6.refs_1_.refs_3_.refs_2_ = bf16[256,1792]{1,0:T(8,128)(2,1)} custom-call(f32[256,1792]{1,0:T(8,128)} %get-tuple-element.58.refs_4_.refs_0_, bf16[256,1792]{1,0:T(8,128)(2,1)} %copy-done.1, f32[256,1792]{1,0:T(8,128)} %get-tuple-element.62.refs_0_.refs_2_, bf16[256,1792]{1,0:T(8,128)(2,1)} %copy-done.2, f32[8,32,4096]{2,1,0:T(8,128)} %get-tuple-element.72.refs_4_.mine_ref), custom_call_target="tpu_custom_call" | custom-call | flops 4587520 | bytes 3211264 | tf_op jit(solution)/shard_map/gating/pallas_call | solution.py:202
  307.6 11.3 %product.18 = (f32[8,16,4096]{2,1,0:T(8,128)}, bf16[8,16,4096]{2,1,0:T(8,128)(2,1)}) custom-call(s32[1]{0:T(128)} %bitcast.refs_0_, bf16[256,1792]{1,0:T(8,128)(2,1)} %gating.6.refs_1_.refs_3_.refs_2_, bf16[1792,4096]{1,0:T(8,128)(2,1)} %masked_weights.5.refs_2_.refs_3_, bf16[256,1792]{1,0:T(8,128)(2,1)} %gating.6.refs_1_.refs_3_.refs_2_), custom_call_target="tpu_custom_call" | custom-call | flops 1879048192 | bytes 9895936 | tf_op jit(solution)/shard_map/product/pallas_call | solution.py:119
  322.5 4.9 %stage.19 = (f32[4,32,4096]{2,1,0:T(8,128)}, bf16[4,32,4096]{2,1,0:T(8,128)(2,1)}) custom-call(f32[8,32,4096]{2,1,0:T(8,128)} %get-tuple-element.72.refs_4_.mine_ref, bf16[8,32,4096]{2,1,0:T(8,128)(2,1)} %copy-done.7, f32[1,32,4096]{2,1,0:T(8,128)} %get-tuple-element.74.refs_0_.mine_ref), custom_call_target="tpu_custom_call" | custom-call | flops 524288 | bytes 4718592 | tf_op jit(solution)/shard_map/stage/pallas_call | solution.py:229
  328.9 6.9 %gating.7 = (bf16[256,1792]{1,0:T(8,128)(2,1)}, bf16[256,1792]{1,0:T(8,128)(2,1)}) custom-call(f32[256,1792]{1,0:T(8,128)} %get-tuple-element.58.refs_4_.refs_0_, bf16[256,1792]{1,0:T(8,128)(2,1)} %copy-done.1, f32[256,1792]{1,0:T(8,128)} %get-tuple-element.62.refs_0_.refs_2_, bf16[256,1792]{1,0:T(8,128)(2,1)} %copy-done.2, ...), custom_call_target="tpu_custom_call" | custom-call | flops 4587520 | bytes 5046272 | tf_op jit(solution)/shard_map/gating/pallas_call | solution.py:202
  335.8 16.6 %product.19 = (f32[8,16,4096]{2,1,0:T(8,128)}, bf16[8,16,4096]{2,1,0:T(8,128)(2,1)}) custom-call(s32[1]{0:T(128)} %bitcast.refs_0_, bf16[256,1792]{1,0:T(8,128)(2,1)} %get-tuple-element.79.refs_1_.refs_5_.refs_4_, bf16[4096,1792]{1,0:T(8,128)(2,1)} %masked_weights.3.refs_0_.refs_2_, bf16[256,1792]{1,0:T(8,128)(2,1)} %get-tuple-element.80.refs_3_.refs_4_, ...), custom_call_target="tpu_custom_call" | custom-call | flops 3758096384 | bytes 17694720 | tf_op jit(solution)/shard_map/product/pallas_call | solution.py:119
  354.8 13.0 %collective-permute-done.9.got_ref = bf16[1,32,4096]{2,1,0:T(8,128)(2,1)S(1)} collective-permute-done((bf16[1,32,4096]{2,1,0:T(8,128)(2,1)S(1)}, bf16[1,32,4096]{2,1,0:T(8,128)(2,1)S(1)}, u32[]{:S(2)}, u32[]{:S(2)}) %collective-permute-start.9) | collective-permute-done | bytes 262176 | tf_op jit(solution)/shard_map/ppermute | solution.py:267
  375.1 2.9 stage.22
  379.3 17.5 %weight_grad.3.refs_0_ = bf16[1792,4096]{1,0:T(8,128)(2,1)} custom-call(s32[14,32]{1,0:T(8,128)} %refs_0_.4, bf16[512,1792]{1,0:T(8,128)(2,1)} %gating.4.refs_1_.refs_3_, bf16[256,1792]{1,0:T(8,128)(2,1)} %gating.6.refs_1_.refs_3_.refs_2_, bf16[512,4096]{1,0:T(8,128)(2,1)} %all-gather.9.cloned.1.call-done.refs_1_.refs_3_, ...), custom_call_target="tpu_custom_call" | custom-call | flops 5637144576 | bytes 11862016 | tf_op jit(solution)/shard_map/weight_grad/pallas_call | solution.py:160
  409.8 16.8 %weight_grad.4.refs_0_ = bf16[4096,1792]{1,0:T(8,128)(2,1)} custom-call(s32[32,14]{1,0:T(8,128)} %copy.13.mask_ref.refs_0_, bf16[512,4096]{1,0:T(8,128)(2,1)} %all-gather.5.cloned.1.call-done.refs_1_, bf16[256,4096]{1,0:T(8,128)(2,1)} %all-gather.7.cloned.1.call-done.refs_1_.refs_2_, bf16[512,1792]{1,0:T(8,128)(2,1)} %get-tuple-element.65.refs_3_.refs_1_, ...), custom_call_target="tpu_custom_call" | custom-call | flops 5637144576 | bytes 11862016 | tf_op jit(solution)/shard_map/weight_grad/pallas_call | solution.py:160
  437.4 16.7 %weight_grad.5.refs_0_ = bf16[4096,1792]{1,0:T(8,128)(2,1)} custom-call(s32[32,14]{1,0:T(8,128)} %copy.15.mask_ref.refs_0_, bf16[512,4096]{1,0:T(8,128)(2,1)} %all-gather.5.cloned.1.call-done.refs_1_, bf16[256,4096]{1,0:T(8,128)(2,1)} %all-gather.7.cloned.1.call-done.refs_1_.refs_2_, bf16[512,1792]{1,0:T(8,128)(2,1)} %get-tuple-element.71.refs_3_, ...), custom_call_target="tpu_custom_call" | custom-call | flops 5637144576 | bytes 11862016 | tf_op jit(solution)/shard_map/weight_grad/pallas_call | solution.py:160
  (128 shorter events, 87.4 us)
Async XLA Ops:
  7.2 6.0 %copy-start.24 = (s32[32,14]{0,1:T(8,128)S(1)}, s32[32,14]{0,1:T(8,128)}, u32[]{:S(2)}) copy-start(s32[32,14]{0,1:T(8,128)} %param.13) | copy-start | bytes 5380
  7.2 56.9 %all-gather.5.cloned.1.call-start = ((), (), s32[]{:S(2)}) async-start(), calls=%async_computation | async-start | bytes 4456448 | tf_op jit(solution)/shard_map/all_gather | solution.py:260
  8.9 107.1 %all-gather.9.cloned.1.call-start = ((), (), s32[]{:S(2)}) async-start(), calls=%async_computation.2 | async-start | bytes 4456448 | tf_op jit(solution)/shard_map/all_gather | solution.py:260
  10.7 147.4 %all-gather.7.cloned.1.call-start = ((), (), s32[]{:S(2)}) async-start(), calls=%async_computation.1 | async-start | bytes 2228224 | tf_op jit(solution)/shard_map/all_gather | solution.py:260
  12.3 189.1 %all-gather.11.cloned.1.call-start = ((), (), s32[]{:S(2)}) async-start(), calls=%async_computation.3 | async-start | bytes 2228224 | tf_op jit(solution)/shard_map/all_gather | solution.py:260
  78.7 43.2 %collective-permute-start = (bf16[512,1792]{1,0:T(8,128)(2,1)}, bf16[512,1792]{1,0:T(8,128)(2,1)}, u32[]{:S(2)}, u32[]{:S(2)}) collective-permute-start(bf16[512,1792]{1,0:T(8,128)(2,1)} %get-tuple-element.54), channel_id=1, source_target_pairs={{0,16},{16,0},{1,17},{17,1},{2,18},{18,2},{3,19},{19,3},{4,20},{20... | collective-permute-start | bytes 5505032 | tf_op jit(solution)/shard_map/ppermute | solution.py:286
  94.9 66.2 %collective-permute-start.1 = (bf16[512,1792]{1,0:T(8,128)(2,1)}, bf16[512,1792]{1,0:T(8,128)(2,1)S(1)}, u32[]{:S(2)}, u32[]{:S(2)}) collective-permute-start(bf16[512,1792]{1,0:T(8,128)(2,1)} %get-tuple-element.56), channel_id=1, source_target_pairs={{0,16},{16,0},{1,17},{17,1},{2,18},{18,2},{3,19},{19,3},{4,20},{20... | collective-permute-start | bytes 5505032 | tf_op jit(solution)/shard_map/ppermute | solution.py:286
  139.3 42.0 %collective-permute-start.2 = (bf16[256,1792]{1,0:T(8,128)(2,1)}, bf16[256,1792]{1,0:T(8,128)(2,1)S(1)}, u32[]{:S(2)}, u32[]{:S(2)}) collective-permute-start(bf16[256,1792]{1,0:T(8,128)(2,1)} %get-tuple-element.102), channel_id=1, source_target_pairs={{0,16},{16,0},{1,17},{17,1},{2,18},{18,2},{3,19},{19,3},{4,20},{20... | collective-permute-start | bytes 2752520 | tf_op jit(solution)/shard_map/ppermute | solution.py:286
  196.8 16.0 %collective-permute-start.3 = (bf16[8,32,4096]{2,1,0:T(8,128)(2,1)}, bf16[8,32,4096]{2,1,0:T(8,128)(2,1)S(1)}, u32[]{:S(2)}, u32[]{:S(2)}) collective-permute-start(bf16[8,32,4096]{2,1,0:T(8,128)(2,1)} %get-tuple-element.61), channel_id=1, source_target_pairs={{0,1},{1,0},{2,3},{3,2},{4,5},{5,4},{6,7},{7,6},{8,9},{9,8},{10,11... | collective-permute-start | bytes 6291464 | tf_op jit(solution)/shard_map/ppermute | solution.py:267
  196.8 23.5 %collective-permute-start.5 = (bf16[256,1792]{1,0:T(8,128)(2,1)}, bf16[256,1792]{1,0:T(8,128)(2,1)}, u32[]{:S(2)}, u32[]{:S(2)}) collective-permute-start(bf16[256,1792]{1,0:T(8,128)(2,1)} %get-tuple-element.101), channel_id=1, source_target_pairs={{0,16},{16,0},{1,17},{17,1},{2,18},{18,2},{3,19},{19,3},{4,20},{20... | collective-permute-start | bytes 2752520 | tf_op jit(solution)/shard_map/ppermute | solution.py:286
  198.2 41.2 %collective-permute-start.6 = (bf16[256,1792]{1,0:T(8,128)(2,1)}, bf16[256,1792]{1,0:T(8,128)(2,1)S(1)}, u32[]{:S(2)}, u32[]{:S(2)}) collective-permute-start(bf16[256,1792]{1,0:T(8,128)(2,1)} %get-tuple-element.66), channel_id=1, source_target_pairs={{0,16},{16,0},{1,17},{17,1},{2,18},{18,2},{3,19},{19,3},{4,20},{20... | collective-permute-start | bytes 2752520 | tf_op jit(solution)/shard_map/ppermute | solution.py:286
  214.1 6.2 %copy-start.4 = (bf16[256,1792]{1,0:T(8,128)(2,1)S(1)}, bf16[256,1792]{1,0:T(8,128)(2,1)}, u32[]{:S(2)}) copy-start(bf16[256,1792]{1,0:T(8,128)(2,1)} %copy-done.3) | copy-start | bytes 2752516
  219.0 32.7 %collective-permute-start.4 = (bf16[4,32,4096]{2,1,0:T(8,128)(2,1)}, bf16[4,32,4096]{2,1,0:T(8,128)(2,1)S(1)}, u32[]{:S(2)}, u32[]{:S(2)}) collective-permute-start(bf16[4,32,4096]{2,1,0:T(8,128)(2,1)} %get-tuple-element.64), channel_id=1, source_target_pairs={{0,2},{1,3},{2,0},{3,1},{4,6},{5,7},{6,4},{7,5},{8,10},{9,11},{10,... | collective-permute-start | bytes 3145736 | tf_op jit(solution)/shard_map/ppermute | solution.py:267
  277.4 43.7 %collective-permute-start.11 = (bf16[8,32,4096]{2,1,0:T(8,128)(2,1)}, bf16[8,32,4096]{2,1,0:T(8,128)(2,1)S(1)}, u32[]{:S(2)}, u32[]{:S(2)}) collective-permute-start(bf16[8,32,4096]{2,1,0:T(8,128)(2,1)} %get-tuple-element.77), channel_id=1, source_target_pairs={{0,1},{1,0},{2,3},{3,2},{4,5},{5,4},{6,7},{7,6},{8,9},{9,8},{10,11... | collective-permute-start | bytes 6291464 | tf_op jit(solution)/shard_map/ppermute | solution.py:267
  277.4 23.4 %collective-permute-start.8 = (bf16[256,1792]{1,0:T(8,128)(2,1)}, bf16[256,1792]{1,0:T(8,128)(2,1)S(1)}, u32[]{:S(2)}, u32[]{:S(2)}) collective-permute-start(bf16[256,1792]{1,0:T(8,128)(2,1)} %get-tuple-element.70), channel_id=1, source_target_pairs={{0,16},{16,0},{1,17},{17,1},{2,18},{18,2},{3,19},{19,3},{4,20},{20... | collective-permute-start | bytes 2752520 | tf_op jit(solution)/shard_map/ppermute | solution.py:286
  278.9 49.1 %collective-permute-start.10 = (bf16[256,1792]{1,0:T(8,128)(2,1)}, bf16[256,1792]{1,0:T(8,128)(2,1)S(1)}, u32[]{:S(2)}, u32[]{:S(2)}) collective-permute-start(bf16[256,1792]{1,0:T(8,128)(2,1)} %get-tuple-element.76), channel_id=1, source_target_pairs={{0,16},{16,0},{1,17},{17,1},{2,18},{18,2},{3,19},{19,3},{4,20},{20... | collective-permute-start | bytes 2752520 | tf_op jit(solution)/shard_map/ppermute | solution.py:286
  279.5 39.4 %collective-permute-start.7 = (bf16[2,32,4096]{2,1,0:T(8,128)(2,1)}, bf16[2,32,4096]{2,1,0:T(8,128)(2,1)}, u32[]{:S(2)}, u32[]{:S(2)}) collective-permute-start(bf16[2,32,4096]{2,1,0:T(8,128)(2,1)} %get-tuple-element.69), channel_id=1, source_target_pairs={{0,4},{1,5},{2,6},{3,7},{4,0},{5,1},{6,2},{7,3},{8,12},{9,13},{10,... | collective-permute-start | bytes 1572872 | tf_op jit(solution)/shard_map/ppermute | solution.py:267
  327.3 43.0 %collective-permute-start.13 = (bf16[4,32,4096]{2,1,0:T(8,128)(2,1)}, bf16[4,32,4096]{2,1,0:T(8,128)(2,1)S(1)}, u32[]{:S(2)}, u32[]{:S(2)}) collective-permute-start(bf16[4,32,4096]{2,1,0:T(8,128)(2,1)} %get-tuple-element.83), channel_id=1, source_target_pairs={{0,2},{1,3},{2,0},{3,1},{4,6},{5,7},{6,4},{7,5},{8,10},{9,11},{10,... | collective-permute-start | bytes 3145736 | tf_op jit(solution)/shard_map/ppermute | solution.py:267
  328.0 46.1 %collective-permute-start.12 = (bf16[8,16,4096]{2,1,0:T(8,128)(2,1)}, bf16[8,16,4096]{2,1,0:T(8,128)(2,1)S(1)}, u32[]{:S(2)}, u32[]{:S(2)}) collective-permute-start(bf16[8,16,4096]{2,1,0:T(8,128)(2,1)} %get-tuple-element.82), channel_id=1, source_target_pairs={{0,1},{1,0},{2,3},{3,2},{4,5},{5,4},{6,7},{7,6},{8,9},{9,8},{10,11... | collective-permute-start | bytes 3145736 | tf_op jit(solution)/shard_map/ppermute | solution.py:267
  335.8 17.2 %copy-start.26 = (bf16[1,32,4096]{2,1,0:T(8,128)(2,1)S(1)}, bf16[1,32,4096]{2,1,0:T(8,128)(2,1)}, u32[]{:S(2)}) copy-start(bf16[1,32,4096]{2,1,0:T(8,128)(2,1)} %get-tuple-element.75) | copy-start | bytes 786436
  352.5 53.0 %collective-permute-start.18 = (bf16[8,16,4096]{2,1,0:T(8,128)(2,1)}, bf16[8,16,4096]{2,1,0:T(8,128)(2,1)S(1)}, u32[]{:S(2)}, u32[]{:S(2)}) collective-permute-start(bf16[8,16,4096]{2,1,0:T(8,128)(2,1)} %get-tuple-element.92), channel_id=1, source_target_pairs={{0,1},{1,0},{2,3},{3,2},{4,5},{5,4},{6,7},{7,6},{8,9},{9,8},{10,11... | collective-permute-start | bytes 3145736 | tf_op jit(solution)/shard_map/ppermute | solution.py:267
  353.0 14.8 %collective-permute-start.9 = (bf16[1,32,4096]{2,1,0:T(8,128)(2,1)S(1)}, bf16[1,32,4096]{2,1,0:T(8,128)(2,1)S(1)}, u32[]{:S(2)}, u32[]{:S(2)}) collective-permute-start(bf16[1,32,4096]{2,1,0:T(8,128)(2,1)S(1)} %copy-done.26), channel_id=1, source_target_pairs={{0,8},{1,9},{2,10},{3,11},{4,12},{5,13},{6,14},{7,15},{8,0},{9,1},... | collective-permute-start | bytes 786440 | tf_op jit(solution)/shard_map/ppermute | solution.py:267
  378.0 21.9 %collective-permute-start.14 = (bf16[4,16,4096]{2,1,0:T(8,128)(2,1)}, bf16[4,16,4096]{2,1,0:T(8,128)(2,1)S(1)}, u32[]{:S(2)}, u32[]{:S(2)}) collective-permute-start(bf16[4,16,4096]{2,1,0:T(8,128)(2,1)} %get-tuple-element.86), channel_id=1, source_target_pairs={{0,2},{1,3},{2,0},{3,1},{4,6},{5,7},{6,4},{7,5},{8,10},{9,11},{10,... | collective-permute-start | bytes 1572872 | tf_op jit(solution)/shard_map/ppermute | solution.py:267
  379.3 17.5 %collective-permute-start.15 = (bf16[2,32,4096]{2,1,0:T(8,128)(2,1)S(1)}, bf16[2,32,4096]{2,1,0:T(8,128)(2,1)S(1)}, u32[]{:S(2)}, u32[]{:S(2)}) collective-permute-start(bf16[2,32,4096]{2,1,0:T(8,128)(2,1)S(1)} %copy-done.25), channel_id=1, source_target_pairs={{0,4},{1,5},{2,6},{3,7},{4,0},{5,1},{6,2},{7,3},{8,12},{9,13},{10,... | collective-permute-start | bytes 1572872 | tf_op jit(solution)/shard_map/ppermute | solution.py:267
  403.0 26.1 %collective-permute-start.16 = (bf16[2,16,4096]{2,1,0:T(8,128)(2,1)}, bf16[2,16,4096]{2,1,0:T(8,128)(2,1)S(1)}, u32[]{:S(2)}, u32[]{:S(2)}) collective-permute-start(bf16[2,16,4096]{2,1,0:T(8,128)(2,1)} %get-tuple-element.90), channel_id=1, source_target_pairs={{0,4},{1,5},{2,6},{3,7},{4,0},{5,1},{6,2},{7,3},{8,12},{9,13},{10,... | collective-permute-start | bytes 786440 | tf_op jit(solution)/shard_map/ppermute | solution.py:267
  405.0 21.6 %collective-permute-start.17 = (bf16[1,32,4096]{2,1,0:T(8,128)(2,1)S(1)}, bf16[1,32,4096]{2,1,0:T(8,128)(2,1)S(1)}, u32[]{:S(2)}, u32[]{:S(2)}) collective-permute-start(bf16[1,32,4096]{2,1,0:T(8,128)(2,1)S(1)} %copy-done.27), channel_id=1, source_target_pairs={{0,8},{1,9},{2,10},{3,11},{4,12},{5,13},{6,14},{7,15},{8,0},{9,1},... | collective-permute-start | bytes 786440 | tf_op jit(solution)/shard_map/ppermute | solution.py:267
  409.3 25.0 %collective-permute-start.20 = (bf16[4,16,4096]{2,1,0:T(8,128)(2,1)}, bf16[4,16,4096]{2,1,0:T(8,128)(2,1)S(1)}, u32[]{:S(2)}, u32[]{:S(2)}) collective-permute-start(bf16[4,16,4096]{2,1,0:T(8,128)(2,1)} %get-tuple-element.96), channel_id=1, source_target_pairs={{0,2},{1,3},{2,0},{3,1},{4,6},{5,7},{6,4},{7,5},{8,10},{9,11},{10,... | collective-permute-start | bytes 1572872 | tf_op jit(solution)/shard_map/ppermute | solution.py:267
  431.7 22.4 %collective-permute-start.19 = (bf16[1,16,4096]{2,1,0:T(8,128)(2,1)}, bf16[1,16,4096]{2,1,0:T(8,128)(2,1)S(1)}, u32[]{:S(2)}, u32[]{:S(2)}) collective-permute-start(bf16[1,16,4096]{2,1,0:T(8,128)(2,1)} %get-tuple-element.95), channel_id=1, source_target_pairs={{0,8},{1,9},{2,10},{3,11},{4,12},{5,13},{6,14},{7,15},{8,0},{9,1},... | collective-permute-start | bytes 393224 | tf_op jit(solution)/shard_map/ppermute | solution.py:267
  437.3 19.1 %collective-permute-start.21 = (bf16[2,16,4096]{2,1,0:T(8,128)(2,1)}, bf16[2,16,4096]{2,1,0:T(8,128)(2,1)S(1)}, u32[]{:S(2)}, u32[]{:S(2)}) collective-permute-start(bf16[2,16,4096]{2,1,0:T(8,128)(2,1)} %get-tuple-element.98), channel_id=1, source_target_pairs={{0,4},{1,5},{2,6},{3,7},{4,0},{5,1},{6,2},{7,3},{8,12},{9,13},{10,... | collective-permute-start | bytes 786440 | tf_op jit(solution)/shard_map/ppermute | solution.py:267
  454.1 7.2 %copy-start.6 = (bf16[1,32,4096]{2,1,0:T(8,128)(2,1)S(1)}, bf16[1,32,4096]{2,1,0:T(8,128)(2,1)}, u32[]{:S(2)}) copy-start(bf16[1,32,4096]{2,1,0:T(8,128)(2,1)} %stage.20.refs_0_) | copy-start | bytes 786436
  456.5 11.0 %copy-start.5 = (bf16[1,32,4096]{2,1,0:T(8,128)(2,1)S(1)}, bf16[1,32,4096]{2,1,0:T(8,128)(2,1)}, u32[]{:S(2)}) copy-start(bf16[1,32,4096]{2,1,0:T(8,128)(2,1)} %stage.26.refs_0_) | copy-start | bytes 786436
  459.0 6.1 %collective-permute-start.22 = (bf16[1,16,4096]{2,1,0:T(8,128)(2,1)}, bf16[1,16,4096]{2,1,0:T(8,128)(2,1)S(1)}, u32[]{:S(2)}, u32[]{:S(2)}) collective-permute-start(bf16[1,16,4096]{2,1,0:T(8,128)(2,1)} %get-tuple-element.100), channel_id=1, source_target_pairs={{0,8},{1,9},{2,10},{3,11},{4,12},{5,13},{6,14},{7,15},{8,0},{9,1},... | collective-permute-start | bytes 393224 | tf_op jit(solution)/shard_map/ppermute | solution.py:267
  (23 other events, 32.7 us)
Sparse Core Ops, SparseCore 0:
  10.8 53.2 all-gather.4
  66.8 49.2 all-gather.8
  118.2 39.8 all-gather.6
  160.7 40.6 all-gather.10
